TPU v7x, 32 devices: a whole 2x2x4 slice. The times are simulated.
32 devices in a mesh: row: 8 (over z, x), col: 4 (over y, core).
Axes of the slice: x: 2, y: 2, z: 4, core: 2. Of those that a mesh axis runs over, the one named last changes fastest.
Arguments:
- tensor: bfloat16 [2048, 512, 128], P('row', 'col'), may hold values from -96 to 96
- factor_a: float32 [2048, 128], P(('row', 'col')), may hold values from -4.5 to 4.5
- factor_b: float32 [512, 128], P(('col', 'row')), may hold values from -4.5 to 4.5
- factor_c: float32 [128, 128], replicated, may hold values from -4.5 to 4.5
Outputs:
- new_a: float32 [2048, 128], P(('row', 'col'))
- new_b: float32 [512, 128], P(('col', 'row'))
- new_c: float32 [128, 128], replicated
All inputs are finite; a program needn't handle non-finite values.
Results may differ from a plain program's by a relative error of at most 0.01.
Values may be sent and summed in bfloat16 or wider, within the bound.
No kernel may reach another device: no remote copies, remote signals or barrier semaphores. Data moves between devices by JAX's collectives and lax.ppermute only.
A program may use at most 128 MiB of HBM per device.

v0:
```python
import jax
import jax.numpy as jnp
from jax import lax
from jax.sharding import PartitionSpec as P

STEPS = 2


damping = 0.9
scaling = 0.25
epsilon = 1e-06


def column_squares(values16):
    return jnp.sum(jnp.square(values16.astype(jnp.float32)), axis=0)


def local_terms(block, tile_a, tile_b, c16):
    rows_i, rows_j, depth = block.shape
    rank = tile_a.shape[1]
    pairs = (
        tile_a.astype(jnp.float32)[:, None, :] * tile_b.astype(jnp.float32)[None, :, :]
    ).astype(jnp.bfloat16)
    pairs = pairs.reshape(rows_i * rows_j, rank)
    model = jnp.dot(pairs, c16.T, preferred_element_type=jnp.float32)
    resid = (block.reshape(rows_i * rows_j, depth).astype(jnp.float32) - model).astype(jnp.bfloat16)
    along = jnp.dot(resid, c16, preferred_element_type=jnp.float32).reshape(rows_i, rows_j, rank)
    grad_a = jnp.sum(along * tile_b.astype(jnp.float32)[None, :, :], axis=1)
    grad_b = jnp.sum(along * tile_a.astype(jnp.float32)[:, None, :], axis=0)
    grad_c = lax.dot_general(
        resid, pairs, (((0,), (0,)), ((), ())), preferred_element_type=jnp.float32
    )
    return (grad_a, grad_b, grad_c)


def local(tensor, factor_a, factor_b, factor_c):
    tile_i, tile_j, depth = tensor.shape
    n_col = lax.axis_size("col")
    k_rows = depth // n_col
    own_a, own_b, third = (factor_a, factor_b, factor_c)
    for step in range(STEPS):
        a_mine16 = own_a.astype(jnp.bfloat16)
        b_mine16 = own_b.astype(jnp.bfloat16)
        tile_a = lax.all_gather(a_mine16, "col", axis=0, tiled=True)
        tile_b = lax.all_gather(b_mine16, "row", axis=0, tiled=True)
        norm_a, norm_b = lax.psum(
            (column_squares(a_mine16), column_squares(b_mine16)), ("row", "col")
        )
        c16 = third.astype(jnp.bfloat16)
        norm_c = column_squares(c16)
        step_a = scaling / (norm_b * norm_c + epsilon)
        step_b = scaling / (norm_a * norm_c + epsilon)
        step_c = scaling / (norm_a * norm_b + epsilon)
        grad_a, grad_b, grad_c = local_terms(tensor, tile_a, tile_b, c16)
        grad_a = lax.psum_scatter(
            grad_a.astype(jnp.bfloat16), "col", scatter_dimension=0, tiled=True
        ).astype(jnp.float32)
        grad_b = lax.psum_scatter(
            grad_b.astype(jnp.bfloat16), "row", scatter_dimension=0, tiled=True
        ).astype(jnp.float32)
        own_a = damping * own_a + step_a * grad_a
        own_b = damping * own_b + step_b * grad_b
        share = lax.psum_scatter(
            grad_c.astype(jnp.bfloat16), "col", scatter_dimension=0, tiled=True
        ).astype(jnp.float32)
        share = lax.psum(share, "row")
        part_c = lax.dynamic_slice_in_dim(third, lax.axis_index("col") * k_rows, k_rows, 0)
        part_c = damping * part_c + step_c * share
        third = lax.all_gather(part_c, "col", axis=0, tiled=True)
    return (own_a, own_b, third)


def solution(mesh):
    return jax.shard_map(
        local,
        mesh=mesh,
        in_specs=(P("row", "col", None), P(("row", "col"), None), P(("col", "row"), None), P()),
        out_specs=(P(("row", "col"), None), P(("col", "row"), None), P()),
        check_vma=False,
    )
```

profile of v0, /device:TPU:0, one launch (start us, length us, event | category | flops | bytes accessed | tf_op | source)
XLA Modules:
  0.0 348.2 jit_solution(18439813869469563145)
XLA Ops:
  8.7 32.2 %all_gather.19 = bf16[128,128]{1,0:T(8,128)(2,1)S(1)} all-gather(bf16[16,128]{1,0:T(8,128)(2,1)S(1)} %get-tuple-element.12), channel_id=1, replica_groups=mesh['row'=8,'col'=4] {'row'}, dimensions={0}, use_global_device_ids=true | all-gather | bytes 36864 | tf_op jit(solution)/shard_map/all_gather | solution.py:45
  40.9 5.2 %all_gather.18 = bf16[256,128]{1,0:T(8,128)(2,1)S(1)} all-gather(bf16[64,128]{1,0:T(8,128)(2,1)S(1)} %get-tuple-element.14), channel_id=1, replica_groups=mesh['row'=8,'col'=4] {'col'}, dimensions={0}, use_global_device_ids=true | all-gather | bytes 81920 | tf_op jit(solution)/shard_map/all_gather | solution.py:44
  46.2 5.6 %multiply_convert_fusion.1 = bf16[256,128,128]{2,1,0:T(8,128)(2,1)} fusion(f32[128,128]{1,0:T(8,128)S(1)} %convert_element_type.123, f32[256,128]{1,0:T(8,128)S(1)} %convert_element_type.122), kind=kLoop, calls=%fused_computation.9 | loop fusion | flops 8388608 | bytes 8585216 | tf_op jit(solution)/shard_map/convert_element_type | solution.py:23
  51.8 8.1 %fusion.1 = bf16[32768,128]{1,0:T(8,128)(2,1)S(1)} fusion(bf16[32768,128]{1,0:T(8,128)(2,1)} %bitcast.16, bf16[32768,128]{1,0:T(8,128)(2,1)} %bitcast.22, f32[128,128]{1,0:T(8,128)S(1)} %copy-done.2), kind=kOutput, calls=%fused_computation.3 | convolution fusion | flops 1086341120 | bytes 25231360 | tf_op jit(solution)/shard_map/dot_general | solution.py:25
  59.9 3.2 copy-done
  63.1 6.4 %convolution_convert_fusion.1 = bf16[128,128]{1,0:T(8,128)(2,1)} fusion(bf16[32768,128]{1,0:T(8,128)(2,1)S(1)} %fusion.1, bf16[32768,128]{1,0:T(8,128)(2,1)} %bitcast.17), kind=kOutput, calls=%fused_computation.11 | convolution fusion | flops 1073758208 | bytes 16809984 | tf_op jit(solution)/shard_map/dot_general | solution.py:30
  69.6 12.1 %multiply_reduce_fusion.3 = (bf16[256,128]{1,0:T(8,128)(2,1)}, f32[32768,128]{1,0:T(8,128)}) fusion(f32[128,128]{1,0:T(8,128)S(1)} %convert_element_type.123, bf16[32768,128]{1,0:T(8,128)(2,1)} %copy-done, f32[128,128]{1,0:T(8,128)S(1)} %copy-done.2), kind=kOutput, calls=%fused_computation.8 | convolution fusion | flops 1082114048 | bytes 25362432 | tf_op jit(solution)/shard_map/dot_general | solution.py:27
  81.7 8.0 %multiply_reduce_fusion.2 = bf16[128,128]{1,0:T(8,128)(2,1)} fusion(f32[256,128,128]{2,1,0:T(8,128)} %bitcast.21, f32[256,128]{1,0:T(8,128)S(1)} %convert_element_type.122), kind=kLoop, calls=%fused_computation.7 | loop fusion | flops 8372224 | bytes 16941056 | tf_op jit(solution)/shard_map/reduce_sum | solution.py:29
  90.5 39.8 %all-reduce.1 = (f32[128]{0:T(128)S(1)}, f32[128]{0:T(128)S(1)}) all-reduce(f32[128]{0:T(128)S(1)} %get-tuple-element.13, f32[128]{0:T(128)S(1)} %get-tuple-element.11), channel_id=1, replica_groups=mesh['row'=8,'col'=4] {'row','col'}, use_global_device_ids=true, to_apply=%region_6.0 | all-reduce | flops 256 | bytes 2048 | tf_op jit(solution)/shard_map/psum | solution.py:46
  130.3 36.5 %psum.45 = f32[32,128]{1,0:T(8,128)S(1)} all-reduce(bf16[32,128]{1,0:T(8,128)(2,1)} %reduce-scatter.11.cloned.1.call-done), channel_id=1, replica_groups=mesh['row'=8,'col'=4] {'row'}, use_global_device_ids=true, to_apply=%region_12.0 | all-reduce | flops 4096 | bytes 24576 | tf_op jit(solution)/shard_map/psum | solution.py:66
  167.5 30.4 %all_gather.22 = bf16[128,128]{1,0:T(8,128)(2,1)S(1)} all-gather(bf16[16,128]{1,0:T(8,128)(2,1)S(1)} %get-tuple-element.10), channel_id=1, replica_groups=mesh['row'=8,'col'=4] {'row'}, dimensions={0}, use_global_device_ids=true | all-gather | bytes 36864 | tf_op jit(solution)/shard_map/all_gather | solution.py:45
  197.9 5.2 %all_gather.20 = f32[128,128]{1,0:T(8,128)S(1)} all-gather(f32[32,128]{1,0:T(8,128)S(1)} %multiply_add_fusion.3), channel_id=1, replica_groups=mesh['row'=8,'col'=4] {'col'}, dimensions={0}, use_global_device_ids=true | all-gather | bytes 81920 | tf_op jit(solution)/shard_map/all_gather | solution.py:69
  203.9 5.2 %all_gather.21 = bf16[256,128]{1,0:T(8,128)(2,1)S(1)} all-gather(bf16[64,128]{1,0:T(8,128)(2,1)S(1)} %get-tuple-element.8), channel_id=1, replica_groups=mesh['row'=8,'col'=4] {'col'}, dimensions={0}, use_global_device_ids=true | all-gather | bytes 81920 | tf_op jit(solution)/shard_map/all_gather | solution.py:44
  209.2 5.6 %multiply_convert_fusion = bf16[256,128,128]{2,1,0:T(8,128)(2,1)} fusion(f32[128,128]{1,0:T(8,128)S(1)} %convert_element_type.140, f32[256,128]{1,0:T(8,128)S(1)} %convert_element_type.139), kind=kLoop, calls=%fused_computation.6 | loop fusion | flops 8388608 | bytes 8585216 | tf_op jit(solution)/shard_map/convert_element_type | solution.py:23
  214.8 8.1 %fusion = bf16[32768,128]{1,0:T(8,128)(2,1)S(1)} fusion(bf16[32768,128]{1,0:T(8,128)(2,1)} %bitcast.18, bf16[32768,128]{1,0:T(8,128)(2,1)} %bitcast.23, f32[128,128]{1,0:T(8,128)S(1)} %all_gather.20), kind=kOutput, calls=%fused_computation.1 | convolution fusion | flops 1086341120 | bytes 25231360 | tf_op jit(solution)/shard_map/dot_general | solution.py:25
  222.9 3.2 copy-done.1
  226.1 6.4 %convolution_convert_fusion = bf16[128,128]{1,0:T(8,128)(2,1)} fusion(bf16[32768,128]{1,0:T(8,128)(2,1)S(1)} %fusion, bf16[32768,128]{1,0:T(8,128)(2,1)} %bitcast.19), kind=kOutput, calls=%fused_computation.10 | convolution fusion | flops 1073758208 | bytes 16809984 | tf_op jit(solution)/shard_map/dot_general | solution.py:30
  232.5 12.1 %multiply_reduce_fusion.1 = (bf16[256,128]{1,0:T(8,128)(2,1)}, f32[32768,128]{1,0:T(8,128)}) fusion(f32[128,128]{1,0:T(8,128)S(1)} %convert_element_type.140, bf16[32768,128]{1,0:T(8,128)(2,1)} %copy-done.1, f32[128,128]{1,0:T(8,128)S(1)} %all_gather.20), kind=kOutput, calls=%fused_computation.5 | convolution fusion | flops 1082114048 | bytes 25362432 | tf_op jit(solution)/shard_map/dot_general | solution.py:27
  244.9 8.0 %multiply_reduce_fusion = bf16[128,128]{1,0:T(8,128)(2,1)} fusion(f32[256,128,128]{2,1,0:T(8,128)} %bitcast.20, f32[256,128]{1,0:T(8,128)S(1)} %convert_element_type.139), kind=kLoop, calls=%fused_computation.4 | loop fusion | flops 8372224 | bytes 16941056 | tf_op jit(solution)/shard_map/reduce_sum | solution.py:29
  253.0 36.9 %all-reduce = (f32[128]{0:T(128)S(1)}, f32[128]{0:T(128)S(1)}) all-reduce(f32[128]{0:T(128)S(1)} %get-tuple-element.9, f32[128]{0:T(128)S(1)} %get-tuple-element.7), channel_id=1, replica_groups=mesh['row'=8,'col'=4] {'row','col'}, use_global_device_ids=true, to_apply=%region_10.0 | all-reduce | flops 256 | bytes 2048 | tf_op jit(solution)/shard_map/psum | solution.py:46
  290.0 36.8 %psum.47 = f32[32,128]{1,0:T(8,128)S(1)} all-reduce(bf16[32,128]{1,0:T(8,128)(2,1)} %reduce-scatter.17.cloned.1.call-done), channel_id=1, replica_groups=mesh['row'=8,'col'=4] {'row'}, use_global_device_ids=true, to_apply=%region_21.0 | all-reduce | flops 4096 | bytes 24576 | tf_op jit(solution)/shard_map/psum | solution.py:66
  326.9 5.2 %all_gather.23 = f32[128,128]{1,0:T(8,128)S(1)} all-gather(f32[32,128]{1,0:T(8,128)S(1)} %multiply_add_fusion.2), channel_id=1, replica_groups=mesh['row'=8,'col'=4] {'col'}, dimensions={0}, use_global_device_ids=true | all-gather | bytes 81920 | tf_op jit(solution)/shard_map/all_gather | solution.py:69
  333.4 6.0 %reduce-scatter.13.cloned.1.call-done = bf16[64,128]{1,0:T(8,128)(2,1)} async-done(((bf16[256,128]{1,0:T(8,128)(2,1)}), bf16[64,128]{1,0:T(8,128)(2,1)}) %reduce-scatter.13.cloned.1.call-update) | async-done | bytes 16400 | tf_op jit(solution)/shard_map/reduce_scatter | solution.py:55
  339.4 1.3 multiply_add_fusion
  (45 shorter events, 6.3 us)
Async XLA Ops:
  7.2 44.6 %copy-start.2 = (f32[128,128]{1,0:T(8,128)S(1)}, f32[128,128]{1,0:T(8,128)}, u32[]{:S(2)}) copy-start(f32[128,128]{1,0:T(8,128)} %param.7) | copy-start | bytes 196612
  7.2 123.1 %reduce-scatter.11.cloned.1.call-start = ((), (), s32[]{:S(2)}) async-start(), calls=%async_computation.8 | async-start | bytes 40960 | tf_op jit(solution)/shard_map/reduce_scatter | solution.py:63
  59.9 3.2 copy-start
  69.5 97.3 %reduce-scatter.9.cloned.1.call-start = ((), (), s32[]{:S(2)}) async-start(), calls=%async_computation.7 | async-start | bytes 36864 | tf_op jit(solution)/shard_map/reduce_scatter | solution.py:58
  81.7 85.2 %copy-start.4 = (f32[16,128]{1,0:T(8,128)S(1)}, f32[16,128]{1,0:T(8,128)}, u32[]{:S(2)}) copy-start(f32[16,128]{1,0:T(8,128)} %param.6) | copy-start | bytes 24580
  81.7 121.5 %copy-start.3 = (f32[64,128]{1,0:T(8,128)S(1)}, f32[64,128]{1,0:T(8,128)}, u32[]{:S(2)}) copy-start(f32[64,128]{1,0:T(8,128)} %param.5) | copy-start | bytes 98308
  89.7 113.5 %reduce-scatter.7.cloned.1.call-start = ((), (), s32[]{:S(2)}) async-start(), calls=%async_computation.6 | async-start | bytes 81920 | tf_op jit(solution)/shard_map/reduce_scatter | solution.py:55
  90.4 199.6 %reduce-scatter.17.cloned.1.call-start = ((), (), s32[]{:S(2)}) async-start(), calls=%async_computation.11 | async-start | bytes 40960 | tf_op jit(solution)/shard_map/reduce_scatter | solution.py:63
  222.9 3.2 copy-start.1
  244.6 87.5 %reduce-scatter.15.cloned.1.call-start = ((), (), s32[]{:S(2)}) async-start(), calls=%async_computation.10 | async-start | bytes 36864 | tf_op jit(solution)/shard_map/reduce_scatter | solution.py:58
  244.9 87.2 %copy-start.6 = (bf16[16,128]{1,0:T(8,128)(2,1)S(1)}, bf16[16,128]{1,0:T(8,128)(2,1)}, u32[]{:S(2)}) copy-start(bf16[16,128]{1,0:T(8,128)(2,1)} %reduce-scatter.9.cloned.1.call-done) | copy-start | bytes 12292
  244.9 94.5 %copy-start.5 = (bf16[64,128]{1,0:T(8,128)(2,1)S(1)}, bf16[64,128]{1,0:T(8,128)(2,1)}, u32[]{:S(2)}) copy-start(bf16[64,128]{1,0:T(8,128)(2,1)} %reduce-scatter.7.cloned.1.call-done) | copy-start | bytes 49156
  252.9 86.4 %reduce-scatter.13.cloned.1.call-start = ((), (), s32[]{:S(2)}) async-start(), calls=%async_computation.9 | async-start | bytes 81920 | tf_op jit(solution)/shard_map/reduce_scatter | solution.py:55
Sparse Core Ops, SparseCore 0:
  69.7 20.2 reduce-scatter.10
  93.9 53.5 reduce-scatter.8
  150.6 18.4 reduce-scatter.6
  244.7 15.6 reduce-scatter.16
  264.3 53.5 reduce-scatter.14
  320.8 18.4 reduce-scatter.12
where the time goes:
time: 349 us; the launch traced here: 348 us
  blocking collectives  234 us (67%)
  matrix products  53.1 us (15%)
  other arithmetic  32.9 us (9%)
  between operations  14.2 us (4%)
  local copies, waits for them, and re-layouts  7.07 us (2%)
  waiting for transfers between devices  6.8 us (2%)
    psum x2, blocking collectives, local(): lax.psum((column_squares(a_mine16), column_squares(b_mine16)), ('row', 'c...  76.7 us
    psum x2, blocking collectives, local(): share = lax.psum(share, 'row')  73.3 us
    all_gather x2, blocking collectives, local(): tile_b = lax.all_gather(b_mine16, 'row', axis=0, tiled=True)  62.6 us
    dot_general x2, matrix products, local_terms(): jnp.dot(resid, c16, preferred_element_type=jnp.float32)  24.1 us
    dot_general x2, matrix products, local_terms(): model = jnp.dot(pairs, c16.T, preferred_element_type=jnp.float32)  16.2 us
    reduce_sum x2, other arithmetic, local_terms(): grad_b = jnp.sum(along * tile_a.astype(jnp.float32)[:, None, :], axis=0)  16 us
    dot_general x2, matrix products, local_terms(): lax.dot_general(resid, pairs, (((0,), (0,)), ((), ())), preferred_element...  12.7 us
    convert_element_type x2, other arithmetic, local_terms(): pairs = (tile_a.astype(jnp.float32)[:, None, :] * tile_b.astype(jnp.float...  11.2 us
  transfers between devices with their start and end apart: 6, of which 1 were waited for; matrix products, arithmetic and copies ran while one was open for 9% of the time, Pallas kernels for 0%

commit v1 on v0

v1 whole, which is shorter than its diff:
```python
import functools

import jax
import jax.numpy as jnp
from jax import lax
from jax.experimental import pallas as pl
from jax.experimental.pallas import tpu as pltpu
from jax.sharding import PartitionSpec as P

STEPS = 2
F32 = jnp.float32
BF16 = jnp.bfloat16
NORM_ROWS = 16
VMEM_LIMIT = 32 << 20


damping = 0.9
scaling = 0.25
epsilon = 1e-06


def vmem(x):
    return pltpu.with_memory_space_constraint(x, pltpu.VMEM)


def call(body, out_shapes, *operands, hbm_out=False):
    whole = pl.BlockSpec(memory_space=pltpu.VMEM)
    outs = [jax.ShapeDtypeStruct(s, d) if hbm_out else pltpu.VMEM(s, d) for s, d in out_shapes]
    return pl.pallas_call(
        body,
        in_specs=[whole] * len(operands),
        out_specs=[whole] * len(outs),
        out_shape=outs,
        compiler_params=pltpu.CompilerParams(vmem_limit_bytes=VMEM_LIMIT),
    )(*[vmem(x) for x in operands])


def dot(x, y):
    return jnp.dot(x, y, preferred_element_type=F32)


def dot_rows(x, y):
    return lax.dot_general(x, y, (((0,), (0,)), ((), ())), preferred_element_type=F32)


def dot_wide(x16, y):
    high = y.astype(BF16)
    low = (y - high.astype(F32)).astype(BF16)
    return dot(x16, high) + dot(x16, low)


def put_norm(ref, start, norm):
    high = norm.astype(BF16).astype(F32)
    rest = norm - high
    mid = rest.astype(BF16).astype(F32)
    low = rest - mid
    rows = jnp.concatenate([high, mid, low, jnp.zeros((NORM_ROWS - 3, norm.shape[1]), F32)], 0)
    ref[start : start + NORM_ROWS] = rows.astype(BF16)


def get_norm(block):
    rows = block.astype(F32)
    return rows[0:1] + rows[1:2] + rows[2:3]


def squares(x16):
    return jnp.sum(jnp.square(x16.astype(F32)), axis=0, keepdims=True)


def terms_kernel(group, t_ref, a_ref, b_ref, c_ref, col_ref, row_ref, acc_a, acc_b, acc_c):
    rows_i, rows_j, depth = t_ref.shape
    rank = a_ref.shape[1]
    half = group // 2
    b16 = b_ref[...].astype(BF16)
    c16 = c_ref[...].astype(BF16)
    b32 = b16.astype(F32)
    zero = jnp.zeros((depth, rank), BF16)
    twice = jnp.concatenate(
        [jnp.concatenate([c16, zero], 1), jnp.concatenate([zero, c16], 1)], 0
    )
    acc_b[...] = jnp.zeros_like(acc_b)
    acc_c[...] = jnp.zeros_like(acc_c)

    def step(g, carry):
        first = pl.multiple_of(g * group, group)
        block = t_ref[pl.ds(first, group)]
        a16 = a_ref[pl.ds(first, group)].astype(BF16)
        a32 = a16.astype(F32)
        left = block[:half].reshape(half * rows_j, depth)
        right = block[half:].reshape(half * rows_j, depth)
        along = dot(jnp.concatenate([left, right], 1), twice)
        along = jnp.concatenate(
            [along[:, :rank].reshape(half, rows_j, rank), along[:, rank:].reshape(half, rows_j, rank)], 0
        )
        acc_a[pl.ds(first, group)] = jnp.sum(along * b32[None], axis=1)
        total = acc_b[...]
        for q in range(group):
            total = total + along[q] * a32[q : q + 1]
        acc_b[...] = total
        pairs = jnp.concatenate([a16[q : q + 1] * b16 for q in range(group)], 0)
        acc_c[...] += dot_rows(block.reshape(group * rows_j, depth), pairs)
        return carry

    lax.fori_loop(0, rows_i // group, step, 0)
    a16 = a_ref[...].astype(BF16)
    gram_a = dot_rows(a16, a16)
    gram_b = dot_rows(b16, b16)
    gram_c = dot_rows(c16, c16)
    col_ref[:rows_i] = (acc_a[...] - dot_wide(a16, gram_b * gram_c)).astype(BF16)
    col_ref[rows_i : rows_i + depth] = (acc_c[...] - dot_wide(c16, gram_a * gram_b)).astype(BF16)
    put_norm(col_ref, rows_i + depth, squares(b16))
    row_ref[:rows_j] = (acc_b[...] - dot_wide(b16, gram_a * gram_c)).astype(BF16)
    put_norm(row_ref, rows_j, squares(a16))


def local_terms(block, a, b, c):
    rows_i, rows_j, depth = block.shape
    rank = a.shape[1]
    group = next(g for g in (64, 32, 16, 8, 4, 2) if rows_i % g == 0)
    whole = pl.BlockSpec(memory_space=pltpu.VMEM)
    return pl.pallas_call(
        functools.partial(terms_kernel, group),
        in_specs=[whole] * 4,
        out_specs=[whole] * 2,
        out_shape=[
            pltpu.VMEM((rows_i + depth + NORM_ROWS, rank), BF16),
            pltpu.VMEM((rows_j + NORM_ROWS, rank), BF16),
        ],
        scratch_shapes=[
            pltpu.VMEM((rows_i, rank), F32),
            pltpu.VMEM((rows_j, rank), F32),
            pltpu.VMEM((depth, rank), F32),
        ],
        compiler_params=pltpu.CompilerParams(vmem_limit_bytes=VMEM_LIMIT),
    )(vmem(block), vmem(a), vmem(b), vmem(c))


def add_kernel(norm_at, x_ref, y_ref, o_ref):
    o_ref[...] = (x_ref[...].astype(F32) + y_ref[...].astype(F32)).astype(BF16)
    at = slice(norm_at, norm_at + NORM_ROWS)
    put_norm(o_ref, norm_at, get_norm(x_ref[at]) + get_norm(y_ref[at]))


def exchange_sum(x, axis, norm_at):
    n = lax.axis_size(axis)
    d = 1
    while d < n:
        y = lax.ppermute(x, axis, [(i, i ^ d) for i in range(n)])
        (x,) = call(functools.partial(add_kernel, norm_at), [(x.shape, BF16)], x, y)
        d *= 2
    return x


def update_kernel(col_ref, row_ref, a_ref, b_ref, c_ref, new_a, new_b, new_c):
    rows_i, rows_j, depth = a_ref.shape[0], b_ref.shape[0], c_ref.shape[0]
    norm_b = get_norm(col_ref[rows_i + depth :])
    norm_a = get_norm(row_ref[rows_j : rows_j + NORM_ROWS])
    norm_c = squares(c_ref[...].astype(BF16))
    step_a = scaling / (norm_b * norm_c + epsilon)
    step_b = scaling / (norm_a * norm_c + epsilon)
    step_c = scaling / (norm_a * norm_b + epsilon)
    new_a[...] = damping * a_ref[...] + step_a * col_ref[:rows_i].astype(F32)
    new_b[...] = damping * b_ref[...] + step_b * row_ref[:rows_j].astype(F32)
    new_c[...] = damping * c_ref[...] + step_c * row_ref[rows_j + NORM_ROWS :].astype(F32)


def local(tensor, factor_a, factor_b, factor_c):
    rows_i, rows_j, depth = tensor.shape
    own_i, rank = factor_a.shape
    own_j = factor_b.shape[0]
    n_row = lax.axis_size("row")
    tensor = vmem(tensor)
    spread = jnp.broadcast_to(factor_b[None], (n_row, own_j, rank))
    b = lax.all_to_all(spread, "row", 0, 0).reshape(rows_j, rank)
    a = lax.all_gather(factor_a, "col", axis=0, tiled=True)
    c = factor_c
    for step in range(STEPS):
        to_col, to_row = local_terms(tensor, a, b, c)
        to_col = exchange_sum(to_col, "col", rows_i + depth)
        to_row = jnp.concatenate([to_row, to_col[rows_i : rows_i + depth]], 0)
        to_row = exchange_sum(to_row, "row", rows_j)
        a, b, c = call(
            update_kernel,
            [(a.shape, F32), (b.shape, F32), (c.shape, F32)],
            to_col, to_row, a, b, c,
        )
    new_a = lax.dynamic_slice_in_dim(a, lax.axis_index("col") * own_i, own_i, 0)
    new_b = lax.dynamic_slice_in_dim(b, lax.axis_index("row") * own_j, own_j, 0)
    return (new_a, new_b, c)


def solution(mesh):
    return jax.shard_map(
        local,
        mesh=mesh,
        in_specs=(P("row", "col", None), P(("row", "col"), None), P(("col", "row"), None), P()),
        out_specs=(P(("row", "col"), None), P(("col", "row"), None), P()),
        check_vma=False,
    )
```

time: 349 us -> 77 us (0.22)
  blocking collectives: 234 us -> 5.62 us
  matrix products: 53.1 us -> 0 us
  other arithmetic: 32.9 us -> 0.01 us
  waiting for transfers between devices: 6.8 us -> 34 us
  starting transfers between devices: 0.46 us -> 16.6 us
  between operations: 14.2 us -> 0.73 us
  Pallas kernels: 0 us -> 12.3 us
    psum x4 -> x0, blocking collectives: 150 us -> none  [the longest x2 76.7 us: local(): lax.psum((column_squares(a_mine16), column_squares(b_mine16)), ('row', 'c...]
    all_gather x6 -> x1, blocking collectives: 83.6 us -> 5.62 us  [local(): a = lax.all_gather(factor_a, 'col', axis=0, tiled=True)]
    dot_general x6 -> x0, matrix products: 53.1 us -> none  [the longest x2 24.1 us: local_terms(): jnp.dot(resid, c16, preferred_element_type=jnp.float32)]
    ppermute x0 -> x10, waiting for transfers between devices: none -> 32.7 us  [exchange_sum(): y = lax.ppermute(x, axis, [(i, i ^ d) for i in range(n)])]
    reduce_sum x8 -> x0, other arithmetic: 19 us -> none  [the longest x2 16 us: local_terms(): grad_b = jnp.sum(along * tile_a.astype(jnp.float32)[:, None, :], axis=0)]
    pallas_call x0 -> x14, Pallas kernels: none -> 12.3 us  [the longest x2 11.9 us: local_terms(): pl.pallas_call(functools.partial(terms_kernel, group), in_specs=[whole] *...]
    convert_element_type x6 -> x0, other arithmetic: 11.3 us -> none  [the longest x2 11.2 us: local_terms(): pairs = (tile_a.astype(jnp.float32)[:, None, :] * tile_b.astype(jnp.float...]
    ppermute x0 -> x10, starting transfers between devices: none -> 9.37 us  [exchange_sum(): y = lax.ppermute(x, axis, [(i, i ^ d) for i in range(n)])]
  transfers between devices with their start and end apart: 6 -> 11, of which waited for: 1 -> 11; matrix products, arithmetic and copies ran while one was open for 9% -> 0% of each run, Pallas kernels for 0% -> 0%
where the time goes in v1:
time: 77 us; the launch traced here: 76.7 us
  waiting for transfers between devices  34 us (44%)
  starting transfers between devices  16.6 us (22%)
  Pallas kernels  12.3 us (16%)
  local copies, waits for them, and re-layouts  7.41 us (10%)
  blocking collectives  5.62 us (7%)
    ppermute x10, waiting for transfers between devices, exchange_sum(): y = lax.ppermute(x, axis, [(i, i ^ d) for i in range(n)])  32.7 us
    pallas_call x2, Pallas kernels, local_terms(): pl.pallas_call(functools.partial(terms_kernel, group), in_specs=[whole] *...  11.9 us
    ppermute x10, starting transfers between devices, exchange_sum(): y = lax.ppermute(x, axis, [(i, i ^ d) for i in range(n)])  9.37 us
    all_to_all x1, starting transfers between devices, local(): b = lax.all_to_all(spread, 'row', 0, 0).reshape(rows_j, rank)  7.25 us
    all_gather x1, blocking collectives, local(): a = lax.all_gather(factor_a, 'col', axis=0, tiled=True)  5.62 us
    unnamed x7, local copies, waits for them, and re-layouts  4.86 us
  transfers between devices with their start and end apart: 11, of which 11 were waited for; matrix products, arithmetic and copies ran while one was open for 0% of the time, Pallas kernels for 0%

profile of v1, /device:TPU:0, one launch (start us, length us, event | category | flops | bytes accessed | tf_op | source)
XLA Modules:
  0.0 76.7 jit_solution(10064658649635512500)
XLA Ops:
  0.6 1.3 %broadcast_in_dim.2 = f32[8,16,128]{2,1,0:T(8,128)} broadcast(f32[16,128]{1,0:T(8,128)} %param.6), dimensions={1,2} | broadcast | bytes 73728 | tf_op jit(solution)/shard_map/broadcast_in_dim | solution.py:173
  2.0 7.3 %all-to-all-start = ((f32[8,16,128]{2,1,0:T(8,128)}), f32[8,16,128]{2,1,0:T(8,128)S(1)}, u32[]{:S(2)}, u32[]{:S(2)}) async-start(f32[8,16,128]{2,1,0:T(8,128)} %broadcast_in_dim.2), calls=%async_computation | async-start | bytes 131072 | tf_op jit(solution)/shard_map/all_to_all | solution.py:174
  9.2 5.6 %all_gather.3.a_ref = f32[256,128]{1,0:T(8,128)S(1)} all-gather(f32[64,128]{1,0:T(8,128)} %param.5), channel_id=1, replica_groups=mesh['row'=8,'col'=4] {'col'}, dimensions={0}, use_global_device_ids=true | all-gather | bytes 163840 | tf_op jit(solution)/shard_map/all_gather | solution.py:175
  14.8 1.3 %all-to-all-done = f32[8,16,128]{2,1,0:T(8,128)S(1)} async-done(((f32[8,16,128]{2,1,0:T(8,128)}), f32[8,16,128]{2,1,0:T(8,128)S(1)}, u32[]{:S(2)}, u32[]{:S(2)}) %all-to-all-start) | async-done | bytes 65568 | tf_op jit(solution)/shard_map/all_to_all | solution.py:174
  16.1 3.4 %copy-done = bf16[256,128,128]{2,1,0:T(8,128)(2,1)S(1)} copy-done((bf16[256,128,128]{2,1,0:T(8,128)(2,1)S(1)}, bf16[256,128,128]{2,1,0:T(8,128)(2,1)}, u32[]{:S(2)}) %copy-start) | copy-done | bytes 8388632
  19.5 0.8 %copy-done.2 = f32[128,128]{1,0:T(8,128)S(1)} copy-done((f32[128,128]{1,0:T(8,128)S(1)}, f32[128,128]{1,0:T(8,128)}, u32[]{:S(2)}) %copy-start.2) | copy-done | bytes 65560
  20.3 5.9 %shard_map.67 = (bf16[400,128]{1,0:T(8,128)(2,1)S(1)}, bf16[144,128]{1,0:T(8,128)(2,1)S(1)}) custom-call(bf16[256,128,128]{2,1,0:T(8,128)(2,1)S(1)} %copy-done, f32[256,128]{1,0:T(8,128)S(1)} %all_gather.3.a_ref, f32[128,128]{1,0:T(8,128)S(1)} %bitcast.1, f32[128,128]{1,0:T(8,128)S(1)} %copy-done.2), custom_call_target="tpu_custom_call" | custom-call | tf_op jit(solution)/shard_map/pallas_call | solution.py:121
  26.3 1.3 %collective-permute-done.y_ref = bf16[400,128]{1,0:T(8,128)(2,1)S(1)} collective-permute-done((bf16[400,128]{1,0:T(8,128)(2,1)S(1)}, bf16[400,128]{1,0:T(8,128)(2,1)S(1)}, u32[]{:S(2)}, u32[]{:S(2)}) %collective-permute-start) | collective-permute-done | bytes 102432 | tf_op jit(solution)/shard_map/ppermute | solution.py:148
  27.6 1.6 %collective-permute-start.1 = (bf16[400,128]{1,0:T(8,128)(2,1)S(1)}, bf16[400,128]{1,0:T(8,128)(2,1)S(1)}, u32[]{:S(2)}, u32[]{:S(2)}) collective-permute-start(bf16[400,128]{1,0:T(8,128)(2,1)S(1)} %shard_map.68.x_ref), channel_id=1, source_target_pairs={{0,2},{1,3},{2,0},{3,1},{4,6},{5,7},{6,4},{7,5},{8,10},{9,11},{10,... | collective-permute-start | bytes 307208 | tf_op jit(solution)/shard_map/ppermute | solution.py:148
  29.2 3.4 %collective-permute-done.1.y_ref = bf16[400,128]{1,0:T(8,128)(2,1)S(1)} collective-permute-done((bf16[400,128]{1,0:T(8,128)(2,1)S(1)}, bf16[400,128]{1,0:T(8,128)(2,1)S(1)}, u32[]{:S(2)}, u32[]{:S(2)}) %collective-permute-start.1) | collective-permute-done | bytes 102432 | tf_op jit(solution)/shard_map/ppermute | solution.py:148
  32.7 1.0 %collective-permute-start.2 = (bf16[272,128]{1,0:T(8,128)(2,1)S(1)}, bf16[272,128]{1,0:T(8,128)(2,1)S(1)}, u32[]{:S(2)}, u32[]{:S(2)}) collective-permute-start(bf16[272,128]{1,0:T(8,128)(2,1)S(1)} %pad_maximum_fusion.x_ref), channel_id=1, source_target_pairs={{0,4},{4,0},{8,12},{12,8},{16,20},{20,16},{24,28},{28,24},{1,5},{5... | collective-permute-start | bytes 208904 | tf_op jit(solution)/shard_map/ppermute | solution.py:148
  33.7 3.4 %collective-permute-done.2.y_ref = bf16[272,128]{1,0:T(8,128)(2,1)S(1)} collective-permute-done((bf16[272,128]{1,0:T(8,128)(2,1)S(1)}, bf16[272,128]{1,0:T(8,128)(2,1)S(1)}, u32[]{:S(2)}, u32[]{:S(2)}) %collective-permute-start.2) | collective-permute-done | bytes 69664 | tf_op jit(solution)/shard_map/ppermute | solution.py:148
  37.1 1.0 %collective-permute-start.3 = (bf16[272,128]{1,0:T(8,128)(2,1)S(1)}, bf16[272,128]{1,0:T(8,128)(2,1)S(1)}, u32[]{:S(2)}, u32[]{:S(2)}) collective-permute-start(bf16[272,128]{1,0:T(8,128)(2,1)S(1)} %shard_map.70.x_ref), channel_id=1, source_target_pairs={{0,8},{4,12},{8,0},{12,4},{16,24},{20,28},{24,16},{28,20},{1,9},{5... | collective-permute-start | bytes 208904 | tf_op jit(solution)/shard_map/ppermute | solution.py:148
  38.1 3.4 %collective-permute-done.3.y_ref = bf16[272,128]{1,0:T(8,128)(2,1)S(1)} collective-permute-done((bf16[272,128]{1,0:T(8,128)(2,1)S(1)}, bf16[272,128]{1,0:T(8,128)(2,1)S(1)}, u32[]{:S(2)}, u32[]{:S(2)}) %collective-permute-start.3) | collective-permute-done | bytes 69664 | tf_op jit(solution)/shard_map/ppermute | solution.py:148
  41.5 2.0 %collective-permute-start.4 = (bf16[272,128]{1,0:T(8,128)(2,1)S(1)}, bf16[272,128]{1,0:T(8,128)(2,1)S(1)}, u32[]{:S(2)}, u32[]{:S(2)}) collective-permute-start(bf16[272,128]{1,0:T(8,128)(2,1)S(1)} %shard_map.71.x_ref), channel_id=1, source_target_pairs={{0,16},{4,20},{8,24},{12,28},{16,0},{20,4},{24,8},{28,12},{1,17},{... | collective-permute-start | bytes 208904 | tf_op jit(solution)/shard_map/ppermute | solution.py:148
  43.5 4.0 %collective-permute-done.4.y_ref = bf16[272,128]{1,0:T(8,128)(2,1)S(1)} collective-permute-done((bf16[272,128]{1,0:T(8,128)(2,1)S(1)}, bf16[272,128]{1,0:T(8,128)(2,1)S(1)}, u32[]{:S(2)}, u32[]{:S(2)}) %collective-permute-start.4) | collective-permute-done | bytes 69664 | tf_op jit(solution)/shard_map/ppermute | solution.py:148
  47.6 6.0 %shard_map.74 = (bf16[400,128]{1,0:T(8,128)(2,1)S(1)}, bf16[144,128]{1,0:T(8,128)(2,1)S(1)}) custom-call(bf16[256,128,128]{2,1,0:T(8,128)(2,1)S(1)} %copy-done.1, f32[256,128]{1,0:T(8,128)S(1)} %get-tuple-element.15.a_ref, f32[128,128]{1,0:T(8,128)S(1)} %get-tuple-element.16.b_ref, f32[128,128]{1,0:T(8,128)S(1)} %get-tuple-element.17.c_ref), custom_call_target="tpu_custom_call" | custom-call | tf_op jit(solution)/shard_map/pallas_call | solution.py:121
  53.7 1.3 %collective-permute-done.5.y_ref = bf16[400,128]{1,0:T(8,128)(2,1)S(1)} collective-permute-done((bf16[400,128]{1,0:T(8,128)(2,1)S(1)}, bf16[400,128]{1,0:T(8,128)(2,1)S(1)}, u32[]{:S(2)}, u32[]{:S(2)}) %collective-permute-start.5) | collective-permute-done | bytes 102432 | tf_op jit(solution)/shard_map/ppermute | solution.py:148
  55.1 1.6 %collective-permute-start.6 = (bf16[400,128]{1,0:T(8,128)(2,1)S(1)}, bf16[400,128]{1,0:T(8,128)(2,1)S(1)}, u32[]{:S(2)}, u32[]{:S(2)}) collective-permute-start(bf16[400,128]{1,0:T(8,128)(2,1)S(1)} %shard_map.75.x_ref), channel_id=1, source_target_pairs={{0,2},{1,3},{2,0},{3,1},{4,6},{5,7},{6,4},{7,5},{8,10},{9,11},{10,... | collective-permute-start | bytes 307208 | tf_op jit(solution)/shard_map/ppermute | solution.py:148
  56.6 3.4 %collective-permute-done.6.y_ref = bf16[400,128]{1,0:T(8,128)(2,1)S(1)} collective-permute-done((bf16[400,128]{1,0:T(8,128)(2,1)S(1)}, bf16[400,128]{1,0:T(8,128)(2,1)S(1)}, u32[]{:S(2)}, u32[]{:S(2)}) %collective-permute-start.6) | collective-permute-done | bytes 102432 | tf_op jit(solution)/shard_map/ppermute | solution.py:148
  60.4 4.1 %collective-permute-done.7.y_ref = bf16[272,128]{1,0:T(8,128)(2,1)S(1)} collective-permute-done((bf16[272,128]{1,0:T(8,128)(2,1)S(1)}, bf16[272,128]{1,0:T(8,128)(2,1)S(1)}, u32[]{:S(2)}, u32[]{:S(2)}) %collective-permute-start.7) | collective-permute-done | bytes 69664 | tf_op jit(solution)/shard_map/ppermute | solution.py:148
  64.9 4.0 %collective-permute-done.8.y_ref = bf16[272,128]{1,0:T(8,128)(2,1)S(1)} collective-permute-done((bf16[272,128]{1,0:T(8,128)(2,1)S(1)}, bf16[272,128]{1,0:T(8,128)(2,1)S(1)}, u32[]{:S(2)}, u32[]{:S(2)}) %collective-permute-start.8) | collective-permute-done | bytes 69664 | tf_op jit(solution)/shard_map/ppermute | solution.py:148
  68.9 1.4 %collective-permute-start.9 = (bf16[272,128]{1,0:T(8,128)(2,1)S(1)}, bf16[272,128]{1,0:T(8,128)(2,1)S(1)}, u32[]{:S(2)}, u32[]{:S(2)}) collective-permute-start(bf16[272,128]{1,0:T(8,128)(2,1)S(1)} %shard_map.78.x_ref), channel_id=1, source_target_pairs={{0,16},{4,20},{8,24},{12,28},{16,0},{20,4},{24,8},{28,12},{1,17},{... | collective-permute-start | bytes 208904 | tf_op jit(solution)/shard_map/ppermute | solution.py:148
  70.4 4.4 %collective-permute-done.9.y_ref = bf16[272,128]{1,0:T(8,128)(2,1)S(1)} collective-permute-done((bf16[272,128]{1,0:T(8,128)(2,1)S(1)}, bf16[272,128]{1,0:T(8,128)(2,1)S(1)}, u32[]{:S(2)}, u32[]{:S(2)}) %collective-permute-start.9) | collective-permute-done | bytes 69664 | tf_op jit(solution)/shard_map/ppermute | solution.py:148
  (27 shorter events, 3.1 us)
Async XLA Ops:
  2.0 14.2 %all-to-all-start = ((f32[8,16,128]{2,1,0:T(8,128)}), f32[8,16,128]{2,1,0:T(8,128)S(1)}, u32[]{:S(2)}, u32[]{:S(2)}) async-start(f32[8,16,128]{2,1,0:T(8,128)} %broadcast_in_dim.2), calls=%async_computation | async-start | bytes 131072 | tf_op jit(solution)/shard_map/all_to_all | solution.py:174
  16.1 3.4 %copy-start = (bf16[256,128,128]{2,1,0:T(8,128)(2,1)S(1)}, bf16[256,128,128]{2,1,0:T(8,128)(2,1)}, u32[]{:S(2)}) copy-start(bf16[256,128,128]{2,1,0:T(8,128)(2,1)} %t_ref.3) | copy-start | bytes 25165828
  19.5 0.8 %copy-start.2 = (f32[128,128]{1,0:T(8,128)S(1)}, f32[128,128]{1,0:T(8,128)}, u32[]{:S(2)}) copy-start(f32[128,128]{1,0:T(8,128)} %c_ref.3) | copy-start | bytes 196612
  20.3 27.3 %copy-start.1 = (bf16[256,128,128]{2,1,0:T(8,128)(2,1)S(1)}, bf16[256,128,128]{2,1,0:T(8,128)(2,1)}, u32[]{:S(2)}) copy-start(bf16[256,128,128]{2,1,0:T(8,128)(2,1)} %t_ref.3) | copy-start | bytes 25165828
  26.2 1.4 %collective-permute-start = (bf16[400,128]{1,0:T(8,128)(2,1)S(1)}, bf16[400,128]{1,0:T(8,128)(2,1)S(1)}, u32[]{:S(2)}, u32[]{:S(2)}) collective-permute-start(bf16[400,128]{1,0:T(8,128)(2,1)S(1)} %get-tuple-element.13.x_ref), channel_id=1, source_target_pairs={{0,1},{1,0},{2,3},{3,2},{4,5},{5,4},{6,7},{7,6},{8,9},{9,8},{10,11... | collective-permute-start | bytes 307208 | tf_op jit(solution)/shard_map/ppermute | solution.py:148
  27.6 5.0 %collective-permute-start.1 = (bf16[400,128]{1,0:T(8,128)(2,1)S(1)}, bf16[400,128]{1,0:T(8,128)(2,1)S(1)}, u32[]{:S(2)}, u32[]{:S(2)}) collective-permute-start(bf16[400,128]{1,0:T(8,128)(2,1)S(1)} %shard_map.68.x_ref), channel_id=1, source_target_pairs={{0,2},{1,3},{2,0},{3,1},{4,6},{5,7},{6,4},{7,5},{8,10},{9,11},{10,... | collective-permute-start | bytes 307208 | tf_op jit(solution)/shard_map/ppermute | solution.py:148
  32.7 4.4 %collective-permute-start.2 = (bf16[272,128]{1,0:T(8,128)(2,1)S(1)}, bf16[272,128]{1,0:T(8,128)(2,1)S(1)}, u32[]{:S(2)}, u32[]{:S(2)}) collective-permute-start(bf16[272,128]{1,0:T(8,128)(2,1)S(1)} %pad_maximum_fusion.x_ref), channel_id=1, source_target_pairs={{0,4},{4,0},{8,12},{12,8},{16,20},{20,16},{24,28},{28,24},{1,5},{5... | collective-permute-start | bytes 208904 | tf_op jit(solution)/shard_map/ppermute | solution.py:148
  37.1 4.4 %collective-permute-start.3 = (bf16[272,128]{1,0:T(8,128)(2,1)S(1)}, bf16[272,128]{1,0:T(8,128)(2,1)S(1)}, u32[]{:S(2)}, u32[]{:S(2)}) collective-permute-start(bf16[272,128]{1,0:T(8,128)(2,1)S(1)} %shard_map.70.x_ref), channel_id=1, source_target_pairs={{0,8},{4,12},{8,0},{12,4},{16,24},{20,28},{24,16},{28,20},{1,9},{5... | collective-permute-start | bytes 208904 | tf_op jit(solution)/shard_map/ppermute | solution.py:148
  41.5 6.0 %collective-permute-start.4 = (bf16[272,128]{1,0:T(8,128)(2,1)S(1)}, bf16[272,128]{1,0:T(8,128)(2,1)S(1)}, u32[]{:S(2)}, u32[]{:S(2)}) collective-permute-start(bf16[272,128]{1,0:T(8,128)(2,1)S(1)} %shard_map.71.x_ref), channel_id=1, source_target_pairs={{0,16},{4,20},{8,24},{12,28},{16,0},{20,4},{24,8},{28,12},{1,17},{... | collective-permute-start | bytes 208904 | tf_op jit(solution)/shard_map/ppermute | solution.py:148
  53.6 1.4 %collective-permute-start.5 = (bf16[400,128]{1,0:T(8,128)(2,1)S(1)}, bf16[400,128]{1,0:T(8,128)(2,1)S(1)}, u32[]{:S(2)}, u32[]{:S(2)}) collective-permute-start(bf16[400,128]{1,0:T(8,128)(2,1)S(1)} %get-tuple-element.18.x_ref), channel_id=1, source_target_pairs={{0,1},{1,0},{2,3},{3,2},{4,5},{5,4},{6,7},{7,6},{8,9},{9,8},{10,11... | collective-permute-start | bytes 307208 | tf_op jit(solution)/shard_map/ppermute | solution.py:148
  55.1 5.0 %collective-permute-start.6 = (bf16[400,128]{1,0:T(8,128)(2,1)S(1)}, bf16[400,128]{1,0:T(8,128)(2,1)S(1)}, u32[]{:S(2)}, u32[]{:S(2)}) collective-permute-start(bf16[400,128]{1,0:T(8,128)(2,1)S(1)} %shard_map.75.x_ref), channel_id=1, source_target_pairs={{0,2},{1,3},{2,0},{3,1},{4,6},{5,7},{6,4},{7,5},{8,10},{9,11},{10,... | collective-permute-start | bytes 307208 | tf_op jit(solution)/shard_map/ppermute | solution.py:148
  60.1 4.4 %collective-permute-start.7 = (bf16[272,128]{1,0:T(8,128)(2,1)S(1)}, bf16[272,128]{1,0:T(8,128)(2,1)S(1)}, u32[]{:S(2)}, u32[]{:S(2)}) collective-permute-start(bf16[272,128]{1,0:T(8,128)(2,1)S(1)} %pad_maximum_fusion.1.x_ref), channel_id=1, source_target_pairs={{0,4},{4,0},{8,12},{12,8},{16,20},{20,16},{24,28},{28,24},{1,5},{5... | collective-permute-start | bytes 208904 | tf_op jit(solution)/shard_map/ppermute | solution.py:148
  64.5 4.4 %collective-permute-start.8 = (bf16[272,128]{1,0:T(8,128)(2,1)S(1)}, bf16[272,128]{1,0:T(8,128)(2,1)S(1)}, u32[]{:S(2)}, u32[]{:S(2)}) collective-permute-start(bf16[272,128]{1,0:T(8,128)(2,1)S(1)} %shard_map.77.x_ref), channel_id=1, source_target_pairs={{0,8},{4,12},{8,0},{12,4},{16,24},{20,28},{24,16},{28,20},{1,9},{5... | collective-permute-start | bytes 208904 | tf_op jit(solution)/shard_map/ppermute | solution.py:148
  68.9 5.8 %collective-permute-start.9 = (bf16[272,128]{1,0:T(8,128)(2,1)S(1)}, bf16[272,128]{1,0:T(8,128)(2,1)S(1)}, u32[]{:S(2)}, u32[]{:S(2)}) collective-permute-start(bf16[272,128]{1,0:T(8,128)(2,1)S(1)} %shard_map.78.x_ref), channel_id=1, source_target_pairs={{0,16},{4,20},{8,24},{12,28},{16,0},{20,4},{24,8},{28,12},{1,17},{... | collective-permute-start | bytes 208904 | tf_op jit(solution)/shard_map/ppermute | solution.py:148

commit v2 on v1

v2 whole, which is shorter than its diff:
```python
import functools

import jax
import jax.numpy as jnp
from jax import lax
from jax.experimental import pallas as pl
from jax.experimental.pallas import tpu as pltpu
from jax.sharding import PartitionSpec as P

F32 = jnp.float32
BF16 = jnp.bfloat16
NORM_ROWS = 16
VMEM_LIMIT = 24 << 20
PLACE_FLOPS = 4 * 10**9


damping = 0.9
scaling = 0.25
epsilon = 1e-06


def vmem(x):
    return pltpu.with_memory_space_constraint(x, pltpu.VMEM)


def call(body, outs, *operands, scratch=(), hbm_out=False, flops=0):
    whole = pl.BlockSpec(memory_space=pltpu.VMEM)
    place = jax.ShapeDtypeStruct if hbm_out else pltpu.VMEM
    return pl.pallas_call(
        body,
        in_specs=[whole] * len(operands),
        out_specs=[whole] * len(outs),
        out_shape=[place(s, d) for s, d in outs],
        scratch_shapes=scratch,
        cost_estimate=pl.CostEstimate(flops=flops, bytes_accessed=0, transcendentals=0),
        compiler_params=pltpu.CompilerParams(vmem_limit_bytes=VMEM_LIMIT),
    )(*[vmem(x) for x in operands])


def divisor(n, most):
    return next(g for g in (64, 32, 16, 8, 4, 2) if g <= most and n % g == 0)


def dot(x, y):
    return jnp.dot(x, y, preferred_element_type=F32)


def dot_rows(x, y):
    return lax.dot_general(x, y, (((0,), (0,)), ((), ())), preferred_element_type=F32)


def gram(x16):
    return dot_rows(x16, x16)


def dot_wide(x16, y):
    high = y.astype(BF16)
    low = (y - high.astype(F32)).astype(BF16)
    return dot(x16, high) + dot(x16, low)


def put_norm(ref, start, norm):
    high = norm.astype(BF16).astype(F32)
    rest = norm - high
    mid = rest.astype(BF16).astype(F32)
    low = rest - mid
    rows = jnp.concatenate([high, mid, low, jnp.zeros((NORM_ROWS - 3, norm.shape[1]), F32)], 0)
    ref[start : start + NORM_ROWS] = rows.astype(BF16)


def get_norm(ref, start):
    rows = ref[start : start + NORM_ROWS].astype(F32)
    return rows[0:1] + rows[1:2] + rows[2:3]


def squares(x16):
    return jnp.sum(jnp.square(x16.astype(F32)), axis=0, keepdims=True)


def tree(parts):
    while len(parts) > 1:
        parts = [parts[q] + parts[q + 1] for q in range(0, len(parts), 2)]
    return parts[0]


def sum_rows(refs, start, rows):
    return tree([r[start : start + rows].astype(F32) for r in refs])


def sum_norm(refs, start):
    return tree([get_norm(r, start) for r in refs])


def digits(n):
    weight = 1
    while weight < n:
        radix = 4 if (n // weight) % 4 == 0 else 2
        yield weight, radix
        weight *= radix


def digit_of(axis, weight, radix):
    return lax.rem(lax.div(lax.axis_index(axis), weight), radix)


def swap(x, axis, weight, q):
    return lax.ppermute(x, axis, [(i, i ^ (q * weight)) for i in range(lax.axis_size(axis))])


def twice(c16):
    zero = jnp.zeros_like(c16)
    return jnp.concatenate(
        [jnp.concatenate([c16, zero], 1), jnp.concatenate([zero, c16], 1)], 0
    )


def times_c(block, pair_c):
    group, rows_j, depth = block.shape
    rank = pair_c.shape[1] // 2
    half = group // 2
    left = block[:half].reshape(half * rows_j, depth)
    right = block[half:].reshape(half * rows_j, depth)
    out = dot(jnp.concatenate([left, right], 1), pair_c)
    return jnp.concatenate(
        [out[:, :rank].reshape(half, rows_j, rank), out[:, rank:].reshape(half, rows_j, rank)], 0
    )


def place_kernel(axis, weight, *refs):
    *ins, out = refs
    rows = ins[0].shape[0]
    digit = digit_of(axis, weight, len(ins))
    for q, ref in enumerate(ins):
        out[pl.ds(pl.multiple_of((digit ^ q) * rows, rows), rows)] = ref[...]


def gather_digit(x, axis, weight, radix):
    got = [swap(x, axis, weight, q) for q in range(1, radix)]
    (x,) = call(
        functools.partial(place_kernel, axis, weight),
        [((x.shape[0] * radix, x.shape[1]), x.dtype)],
        x, *got,
        flops=PLACE_FLOPS,
    )
    return x


def gather(x, axis):
    for weight, radix in digits(lax.axis_size(axis)):
        x = gather_digit(x, axis, weight, radix)
    return x


def add_kernel(norm_at, *refs):
    *ins, out = refs
    out[...] = sum_rows(ins, 0, out.shape[0]).astype(BF16)
    if norm_at is not None:
        put_norm(out, norm_at, sum_norm(ins, norm_at))


def sum_parts(x, axis, norm_at=None):
    parts = [x]
    for weight, radix in digits(lax.axis_size(axis)):
        if len(parts) > 1:
            (x,) = call(functools.partial(add_kernel, norm_at), [(x.shape, BF16)], *parts)
        parts = [x] + [swap(x, axis, weight, q) for q in range(1, radix)]
    return parts


def sum_c(t_ref, a_ref, b16, acc):
    rows_i, rows_j, depth = t_ref.shape
    group = divisor(rows_i, 32)
    acc[...] = jnp.zeros_like(acc)

    def step(g, carry):
        at = pl.ds(pl.multiple_of(g * group, group), group)
        a16 = a_ref[at].astype(BF16)
        pairs = jnp.concatenate([a16[q : q + 1] * b16 for q in range(group)], 0)
        acc[...] += dot_rows(t_ref[at].reshape(group * rows_j, depth), pairs)
        return carry

    lax.fori_loop(0, rows_i // group, step, 0)


def first_kernel(t_ref, a_ref, b_ref, c_ref, row_ref, col_ref, acc_a, acc_b, acc_c):
    rows_i, rows_j, depth = t_ref.shape
    group = divisor(rows_i, 64)
    a16 = a_ref[...].astype(BF16)
    b16 = b_ref[...].astype(BF16)
    c16 = c_ref[...].astype(BF16)
    b32 = b16.astype(F32)
    pair_c = twice(c16)
    acc_b[...] = jnp.zeros_like(acc_b)
    acc_c[...] = jnp.zeros_like(acc_c)

    def step(g, carry):
        at = pl.ds(pl.multiple_of(g * group, group), group)
        part16 = a_ref[at].astype(BF16)
        part32 = part16.astype(F32)
        block = t_ref[at]
        along = times_c(block, pair_c)
        acc_a[at] = jnp.sum(along * b32[None], axis=1)
        total = acc_b[...]
        for q in range(group):
            total = total + along[q] * part32[q : q + 1]
        acc_b[...] = total
        pairs = jnp.concatenate([part16[q : q + 1] * b16 for q in range(group)], 0)
        acc_c[...] += dot_rows(block.reshape(group * rows_j, depth), pairs)
        return carry

    lax.fori_loop(0, rows_i // group, step, 0)
    gram_a, gram_b, gram_c = gram(a16), gram(b16), gram(c16)
    row_ref[:rows_j] = (acc_b[...] - dot_wide(b16, gram_a * gram_c)).astype(BF16)
    row_ref[rows_j : rows_j + depth] = (acc_c[...] - dot_wide(c16, gram_a * gram_b)).astype(BF16)
    put_norm(row_ref, rows_j + depth, squares(a16))
    col_ref[:rows_i] = (acc_a[...] - dot_wide(a16, gram_b * gram_c)).astype(BF16)
    put_norm(col_ref, rows_i, squares(b16))


def middle_kernel(n_row, n_col, *refs):
    rows, refs = refs[:n_row], refs[n_row:]
    cols, refs = refs[:n_col], refs[n_col:]
    a_ref, b_ref, c_ref, new_a, new_b, part_c, step_c = refs
    rows_i, rows_j, depth = a_ref.shape[0], b_ref.shape[0], c_ref.shape[0]
    norm_a = sum_norm(rows, rows_j + depth)
    norm_b = sum_norm(cols, rows_i)
    norm_c = squares(c_ref[...].astype(BF16))
    step_a = scaling / (norm_b * norm_c + epsilon)
    step_b = scaling / (norm_a * norm_c + epsilon)
    new_a[...] = damping * a_ref[...] + step_a * sum_rows(cols, 0, rows_i)
    new_b[...] = damping * b_ref[...] + step_b * sum_rows(rows, 0, rows_j)
    part_c[...] = sum_rows(rows, rows_j, depth).astype(BF16)
    step_c[...] = jnp.broadcast_to(scaling / (norm_a * norm_b + epsilon), step_c.shape)


def second_c_kernel(t_ref, a_ref, b_ref, sum_ref, gram_ref):
    a16 = a_ref[...].astype(BF16)
    b16 = b_ref[...].astype(BF16)
    sum_c(t_ref, a_ref, b16, sum_ref)
    gram_ref[...] = gram(a16) * gram(b16)


def second_model_kernel(n_col, *refs):
    parts, refs = refs[:n_col], refs[n_col:]
    step_ref, c_ref, sum_ref, gram_ref, new_c, out_ref = refs
    c2 = damping * c_ref[...] + step_ref[0:1] * sum_rows(parts, 0, c_ref.shape[0])
    new_c[...] = c2
    out_ref[...] = (sum_ref[...] - dot_wide(c2.astype(BF16), gram_ref[...])).astype(BF16)


def second_ab_kernel(t_ref, a_ref, b_ref, c_ref, col_ref, grad_b, acc_a):
    rows_i, rows_j, depth = t_ref.shape
    group = divisor(rows_i, 32)
    a16 = a_ref[...].astype(BF16)
    b16 = b_ref[...].astype(BF16)
    c16 = c_ref[...].astype(BF16)
    b32 = b16.astype(F32)
    pair_c = twice(c16)
    grad_b[...] = jnp.zeros_like(grad_b)

    def step(g, carry):
        at = pl.ds(pl.multiple_of(g * group, group), group)
        a32 = a_ref[at].astype(BF16).astype(F32)
        along = times_c(t_ref[at], pair_c)
        acc_a[at] = jnp.sum(along * b32[None], axis=1)
        total = grad_b[...]
        for q in range(group):
            total = total + along[q] * a32[q : q + 1]
        grad_b[...] = total
        return carry

    lax.fori_loop(0, rows_i // group, step, 0)
    gram_c = gram(c16)
    col_ref[:rows_i] = (acc_a[...] - dot_wide(a16, gram(b16) * gram_c)).astype(BF16)
    put_norm(col_ref, rows_i, squares(b16))
    grad_b[...] -= dot_wide(b16, gram(a16) * gram_c)


def put_shares(weight, own_j, shared, norm, grad_b, outs):
    radix = len(outs)
    depth = shared.shape[0]
    blocks = grad_b.shape[0] // own_j
    digit = digit_of("row", weight, radix)
    for q, out in enumerate(outs):
        out[:depth] = shared
        put_norm(out, depth, norm)
        first = [(high * radix + (digit ^ q)) * own_j for high in range(blocks // radix)]
        rows = [grad_b[pl.ds(pl.multiple_of(at, own_j), own_j)] for at in first]
        out[depth + NORM_ROWS :] = jnp.concatenate(rows, 0).astype(BF16)


def shares_kernel(n_col, own_j, radix, *refs):
    parts, refs = refs[:n_col], refs[n_col:]
    a_ref, grad_b, outs = refs[0], refs[1], refs[2:]
    shared = sum_rows(parts, 0, parts[0].shape[0]).astype(BF16)
    put_shares(1, own_j, shared, squares(a_ref[...].astype(BF16)), grad_b, outs)


def next_shares_kernel(n_row, weight, own_j, depth, *refs):
    parts, outs, grad_b = refs[:n_row], refs[n_row:-1], refs[-1]
    shared = sum_rows(parts, 0, depth).astype(BF16)
    grad_b[...] = sum_rows(parts, depth + NORM_ROWS, grad_b.shape[0])
    put_shares(weight, own_j, shared, sum_norm(parts, depth), grad_b, outs)


def sum_shares(col_parts, a, grad_b, own_j):
    depth, rank = col_parts[0].shape
    stages = list(digits(lax.axis_size("row")))
    held = grad_b.shape[0]
    parts = None
    for weight, radix in stages:
        shape = (depth + NORM_ROWS + held // radix, rank)
        outs = [(shape, BF16)] * radix
        if parts is None:
            sent = call(
                functools.partial(shares_kernel, len(col_parts), own_j, radix),
                outs, *col_parts, a, grad_b,
            )
        else:
            sent = call(
                functools.partial(next_shares_kernel, len(parts), weight, own_j, depth),
                outs, *parts,
                scratch=[pltpu.VMEM((held, rank), F32)],
            )
        held //= radix
        parts = [sent[0]] + [swap(sent[q], "row", weight, q) for q in range(1, radix)]
    return parts


def last_kernel(n_row, n_col, *refs):
    rows, refs = refs[:n_row], refs[n_row:]
    cols, refs = refs[:n_col], refs[n_col:]
    a_ref, b_ref, c_ref, out_a, out_b, out_c, grad_a = refs
    rows_i, depth = a_ref.shape[0], c_ref.shape[0]
    own_i, own_j = out_a.shape[0], out_b.shape[0]
    norm_a = sum_norm(rows, depth)
    norm_b = sum_norm(cols, rows_i)
    norm_c = squares(c_ref[...].astype(BF16))
    step_a = scaling / (norm_b * norm_c + epsilon)
    step_b = scaling / (norm_a * norm_c + epsilon)
    step_c = scaling / (norm_a * norm_b + epsilon)
    grad_a[...] = sum_rows(cols, 0, rows_i)
    at_i = pl.ds(pl.multiple_of(lax.axis_index("col") * own_i, own_i), own_i)
    at_j = pl.ds(pl.multiple_of(lax.axis_index("row") * own_j, own_j), own_j)
    out_a[...] = damping * a_ref[at_i] + step_a * grad_a[at_i]
    out_b[...] = damping * b_ref[at_j] + step_b * sum_rows(rows, depth + NORM_ROWS, own_j)
    out_c[...] = damping * c_ref[...] + step_c * sum_rows(rows, 0, depth)


def local(tensor, factor_a, factor_b, factor_c):
    rows_i, rows_j, depth = tensor.shape
    rank = factor_a.shape[1]
    own_j = factor_b.shape[0]
    c = factor_c
    b = gather(factor_b, "row")
    a = gather(factor_a, "col")

    to_row, to_col = call(
        first_kernel,
        [((rows_j + depth + NORM_ROWS, rank), BF16), ((rows_i + NORM_ROWS, rank), BF16)],
        tensor, a, b, c,
        scratch=[pltpu.VMEM((n, rank), F32) for n in (rows_i, rows_j, depth)],
        flops=6 * tensor.size * rank,
    )
    rows = sum_parts(to_row, "row", rows_j + depth)
    cols = sum_parts(to_col, "col", rows_i)
    a, b, part_c, step_c = call(
        functools.partial(middle_kernel, len(rows), len(cols)),
        [(a.shape, F32), (b.shape, F32), (c.shape, BF16), ((8, rank), F32)],
        *rows, *cols, a, b, c,
    )

    parts = sum_parts(part_c, "col")
    sum_t, gram_ab = call(
        second_c_kernel,
        [(c.shape, F32), ((rank, rank), F32)],
        tensor, a, b,
        flops=2 * tensor.size * rank,
    )
    c, to_col = call(
        functools.partial(second_model_kernel, len(parts)),
        [(c.shape, F32), (c.shape, BF16)],
        *parts, step_c, c, sum_t, gram_ab,
    )
    parts = sum_parts(to_col, "col")
    to_col, grad_b = call(
        second_ab_kernel,
        [((rows_i + NORM_ROWS, rank), BF16), ((rows_j, rank), F32)],
        tensor, a, b, c,
        scratch=[pltpu.VMEM((rows_i, rank), F32)],
        flops=2 * tensor.size * rank,
    )
    rows = sum_shares(parts, a, grad_b, own_j)
    cols = sum_parts(to_col, "col", rows_i)
    return call(
        functools.partial(last_kernel, len(rows), len(cols)),
        [(factor_a.shape, F32), (factor_b.shape, F32), (c.shape, F32)],
        *rows, *cols, a, b, c,
        scratch=[pltpu.VMEM((rows_i, rank), F32)],
        hbm_out=True,
    )


def solution(mesh):
    return jax.shard_map(
        local,
        mesh=mesh,
        in_specs=(P("row", "col", None), P(("row", "col"), None), P(("col", "row"), None), P()),
        out_specs=(P(("row", "col"), None), P(("col", "row"), None), P()),
        check_vma=False,
    )
```

time: 77 us -> 60.5 us (0.79)
  waiting for transfers between devices: 34 us -> 14.3 us
  starting transfers between devices: 16.6 us -> 27.7 us
  local copies, waits for them, and re-layouts: 7.41 us -> 1.74 us
  blocking collectives: 5.62 us -> 0 us
  Pallas kernels: 12.3 us -> 15.8 us
    ppermute x10 -> x27, waiting for transfers between devices: 32.7 us -> 14.3 us  [swap(): lax.ppermute(x, axis, [(i, i ^ q * weight) for i in range(lax.axis_size(a...]
    ppermute x10 -> x27, starting transfers between devices: 9.37 us -> 27.7 us  [swap(): lax.ppermute(x, axis, [(i, i ^ q * weight) for i in range(lax.axis_size(a...]
    pallas_call x12, Pallas kernels: 0.47 us -> 15.8 us  [call(): pl.pallas_call(body, in_specs=[whole] * len(operands), out_specs=[whole]...]
    pallas_call x2 -> x0, Pallas kernels: 11.9 us -> none  [local_terms(): pl.pallas_call(functools.partial(terms_kernel, group), in_specs=[whole] *...]
    all_to_all x1 -> x0, starting transfers between devices: 7.25 us -> none  [local(): b = lax.all_to_all(spread, 'row', 0, 0).reshape(rows_j, rank)]
    all_gather x1 -> x0, blocking collectives: 5.62 us -> none  [local(): a = lax.all_gather(factor_a, 'col', axis=0, tiled=True)]
    unnamed x7 -> x10, local copies, waits for them, and re-layouts: 4.86 us -> 1.74 us
    broadcast_in_dim x1 -> x0, local copies, waits for them, and re-layouts: 1.33 us -> none  [local(): spread = jnp.broadcast_to(factor_b[None], (n_row, own_j, rank))]
  transfers between devices with their start and end apart: 11 -> 27, of which waited for: 11 -> 11; matrix products, arithmetic and copies ran while one was open for 0% -> 0% of each run, Pallas kernels for 0% -> 14%
where the time goes in v2:
time: 60.5 us; the launch traced here: 60.3 us
  starting transfers between devices  27.7 us (46%)
  Pallas kernels  15.8 us (26%)
  waiting for transfers between devices  14.3 us (24%)
  local copies, waits for them, and re-layouts  1.74 us (3%)
  between operations  0.79 us (1%)
    ppermute x27, starting transfers between devices, swap(): lax.ppermute(x, axis, [(i, i ^ q * weight) for i in range(lax.axis_size(a...  27.7 us
    pallas_call x12, Pallas kernels, call(): pl.pallas_call(body, in_specs=[whole] * len(operands), out_specs=[whole]...  15.8 us
    ppermute x27, waiting for transfers between devices, swap(): lax.ppermute(x, axis, [(i, i ^ q * weight) for i in range(lax.axis_size(a...  14.3 us
    unnamed x10, local copies, waits for them, and re-layouts  1.74 us
  transfers between devices with their start and end apart: 27, of which 11 were waited for; matrix products, arithmetic and copies ran while one was open for 0% of the time, Pallas kernels for 14%

profile of v2, /device:TPU:0, one launch (start us, length us, event | category | flops | bytes accessed | tf_op | source)
XLA Modules:
  0.0 60.3 jit_solution(16420301241259762823)
XLA Ops:
  0.6 3.1 %collective-permute-start.4 = (f32[16,128]{1,0:T(8,128)}, f32[16,128]{1,0:T(8,128)S(1)}, u32[]{:S(2)}, u32[]{:S(2)}) collective-permute-start(f32[16,128]{1,0:T(8,128)} %refs_0_.3), channel_id=1, source_target_pairs={{0,8},{4,12},{8,0},{12,4},{16,24},{20,28},{24,16},{28,20},{1,9},{5... | collective-permute-start | bytes 24584 | tf_op jit(solution)/shard_map/ppermute | solution.py:107
  3.7 1.5 %collective-permute-start.3 = (f32[16,128]{1,0:T(8,128)}, f32[16,128]{1,0:T(8,128)S(1)}, u32[]{:S(2)}, u32[]{:S(2)}) collective-permute-start(f32[16,128]{1,0:T(8,128)} %refs_0_.3), channel_id=1, source_target_pairs={{0,4},{4,0},{8,12},{12,8},{16,20},{20,16},{24,28},{28,24},{1,5},{5... | collective-permute-start | bytes 24584 | tf_op jit(solution)/shard_map/ppermute | solution.py:107
  5.3 1.9 %collective-permute-start.1 = (f32[64,128]{1,0:T(8,128)}, f32[64,128]{1,0:T(8,128)S(1)}, u32[]{:S(2)}, u32[]{:S(2)}) collective-permute-start(f32[64,128]{1,0:T(8,128)} %refs_0_.2), channel_id=1, source_target_pairs={{0,2},{1,3},{2,0},{3,1},{4,6},{5,7},{6,4},{7,5},{8,10},{9,11},{10,... | collective-permute-start | bytes 98312 | tf_op jit(solution)/shard_map/ppermute | solution.py:107
  7.6 2.4 %collective-permute-done.5.refs_3_ = f32[16,128]{1,0:T(8,128)S(1)} collective-permute-done((f32[16,128]{1,0:T(8,128)}, f32[16,128]{1,0:T(8,128)S(1)}, u32[]{:S(2)}, u32[]{:S(2)}) %collective-permute-start.5) | collective-permute-done | bytes 8224 | tf_op jit(solution)/shard_map/ppermute | solution.py:107
  10.7 2.6 %collective-permute-start.6 = (f32[64,128]{1,0:T(8,128)S(1)}, f32[64,128]{1,0:T(8,128)S(1)}, u32[]{:S(2)}, u32[]{:S(2)}) collective-permute-start(f32[64,128]{1,0:T(8,128)S(1)} %shard_map.68.refs_0_), channel_id=1, source_target_pairs={{0,16},{4,20},{8,24},{12,28},{16,0},{20,4},{24,8},{28,12},{1,17},{... | collective-permute-start | bytes 98312 | tf_op jit(solution)/shard_map/ppermute | solution.py:107
  13.4 2.4 %collective-permute-done.6.refs_1_ = f32[64,128]{1,0:T(8,128)S(1)} collective-permute-done((f32[64,128]{1,0:T(8,128)S(1)}, f32[64,128]{1,0:T(8,128)S(1)}, u32[]{:S(2)}, u32[]{:S(2)}) %collective-permute-start.6) | collective-permute-done | bytes 32800 | tf_op jit(solution)/shard_map/ppermute | solution.py:107
  15.8 1.0 %slice-done.1 = s8[4194304]{0:T(1024)(128)(4,1)S(1)} async-done(((s8[8388608]{0:T(1024)(128)(4,1)}), s8[4194304]{0:T(1024)(128)(4,1)S(1)}, s32[]{:S(2)}) %slice-start.1) | async-done | bytes 4194328
  16.8 6.1 %shard_map.70 = (bf16[272,128]{1,0:T(8,128)(2,1)S(1)}, bf16[272,128]{1,0:T(8,128)(2,1)S(1)}) custom-call(bf16[256,128,128]{2,1,0:T(8,128)(2,1)S(1)} %bitcast.1, f32[256,128]{1,0:T(8,128)S(1)} %shard_map.67.a_ref.refs_6_, f32[128,128]{1,0:T(8,128)S(1)} %shard_map.69.b_ref.refs_7_, f32[128,128]{1,0:T(8,128)S(1)} %copy-done), custom_call_target="tpu_custom_call" | custom-call | flops 3221225472 | tf_op jit(solution)/shard_map/pallas_call | solution.py:29
  23.4 1.6 %collective-permute-start.8 = (bf16[272,128]{1,0:T(8,128)(2,1)S(1)}, bf16[272,128]{1,0:T(8,128)(2,1)S(1)}, u32[]{:S(2)}, u32[]{:S(2)}) collective-permute-start(bf16[272,128]{1,0:T(8,128)(2,1)S(1)} %get-tuple-element.21.refs_0_), channel_id=1, source_target_pairs={{0,8},{4,12},{8,0},{12,4},{16,24},{20,28},{24,16},{28,20},{1,9},{5... | collective-permute-start | bytes 208904 | tf_op jit(solution)/shard_map/ppermute | solution.py:107
  25.0 1.5 %collective-permute-start.7 = (bf16[272,128]{1,0:T(8,128)(2,1)S(1)}, bf16[272,128]{1,0:T(8,128)(2,1)S(1)}, u32[]{:S(2)}, u32[]{:S(2)}) collective-permute-start(bf16[272,128]{1,0:T(8,128)(2,1)S(1)} %get-tuple-element.21.refs_0_), channel_id=1, source_target_pairs={{0,4},{4,0},{8,12},{12,8},{16,20},{20,16},{24,28},{28,24},{1,5},{5... | collective-permute-start | bytes 208904 | tf_op jit(solution)/shard_map/ppermute | solution.py:107
  26.4 1.5 %collective-permute-start.12 = (bf16[272,128]{1,0:T(8,128)(2,1)S(1)}, bf16[272,128]{1,0:T(8,128)(2,1)S(1)}, u32[]{:S(2)}, u32[]{:S(2)}) collective-permute-start(bf16[272,128]{1,0:T(8,128)(2,1)S(1)} %get-tuple-element.22.refs_2_), channel_id=1, source_target_pairs={{0,2},{1,3},{2,0},{3,1},{4,6},{5,7},{6,4},{7,5},{8,10},{9,11},{10,... | collective-permute-start | bytes 208904 | tf_op jit(solution)/shard_map/ppermute | solution.py:107
  28.3 1.0 %collective-permute-done.7.refs_1_ = bf16[272,128]{1,0:T(8,128)(2,1)S(1)} collective-permute-done((bf16[272,128]{1,0:T(8,128)(2,1)S(1)}, bf16[272,128]{1,0:T(8,128)(2,1)S(1)}, u32[]{:S(2)}, u32[]{:S(2)}) %collective-permute-start.7) | collective-permute-done | bytes 69664 | tf_op jit(solution)/shard_map/ppermute | solution.py:107
  29.3 1.5 %collective-permute-start.10 = (bf16[272,128]{1,0:T(8,128)(2,1)S(1)}, bf16[272,128]{1,0:T(8,128)(2,1)S(1)}, u32[]{:S(2)}, u32[]{:S(2)}) collective-permute-start(bf16[272,128]{1,0:T(8,128)(2,1)S(1)} %shard_map.71.refs_0_), channel_id=1, source_target_pairs={{0,16},{4,20},{8,24},{12,28},{16,0},{20,4},{24,8},{28,12},{1,17},{... | collective-permute-start | bytes 208904 | tf_op jit(solution)/shard_map/ppermute | solution.py:107
  30.9 1.6 %collective-permute-done.12.refs_4_ = bf16[272,128]{1,0:T(8,128)(2,1)S(1)} collective-permute-done((bf16[272,128]{1,0:T(8,128)(2,1)S(1)}, bf16[272,128]{1,0:T(8,128)(2,1)S(1)}, u32[]{:S(2)}, u32[]{:S(2)}) %collective-permute-start.12) | collective-permute-done | bytes 69664 | tf_op jit(solution)/shard_map/ppermute | solution.py:107
  32.4 2.8 %collective-permute-done.10.refs_1_ = bf16[272,128]{1,0:T(8,128)(2,1)S(1)} collective-permute-done((bf16[272,128]{1,0:T(8,128)(2,1)S(1)}, bf16[272,128]{1,0:T(8,128)(2,1)S(1)}, u32[]{:S(2)}, u32[]{:S(2)}) %collective-permute-start.10) | collective-permute-done | bytes 69664 | tf_op jit(solution)/shard_map/ppermute | solution.py:107
  35.4 1.5 %collective-permute-start.15 = (bf16[128,128]{1,0:T(8,128)(2,1)S(1)}, bf16[128,128]{1,0:T(8,128)(2,1)S(1)}, u32[]{:S(2)}, u32[]{:S(2)}) collective-permute-start(bf16[128,128]{1,0:T(8,128)(2,1)S(1)} %get-tuple-element.23.refs_0_), channel_id=1, source_target_pairs={{0,2},{1,3},{2,0},{3,1},{4,6},{5,7},{6,4},{7,5},{8,10},{9,11},{10,... | collective-permute-start | bytes 98312 | tf_op jit(solution)/shard_map/ppermute | solution.py:107
  37.3 4.0 %shard_map.73 = (f32[128,128]{1,0:T(8,128)S(1)}, f32[128,128]{1,0:T(8,128)S(1)}) custom-call(bf16[256,128,128]{2,1,0:T(8,128)(2,1)S(1)} %bitcast.1, f32[256,128]{1,0:T(8,128)S(1)} %get-tuple-element.25.a_ref.refs_4_.refs_6_, f32[128,128]{1,0:T(8,128)S(1)} %get-tuple-element.26.b_ref.refs_7_), custom_call_target="tpu_custom_call" | custom-call | flops 1073741824 | tf_op jit(solution)/shard_map/pallas_call | solution.py:29
  41.5 1.1 %collective-permute-start.19 = (bf16[128,128]{1,0:T(8,128)(2,1)S(1)}, bf16[128,128]{1,0:T(8,128)(2,1)S(1)}, u32[]{:S(2)}, u32[]{:S(2)}) collective-permute-start(bf16[128,128]{1,0:T(8,128)(2,1)S(1)} %get-tuple-element.29.refs_0_), channel_id=1, source_target_pairs={{0,3},{1,2},{2,1},{3,0},{4,7},{5,6},{6,5},{7,4},{8,11},{9,10},{10,... | collective-permute-start | bytes 98312 | tf_op jit(solution)/shard_map/ppermute | solution.py:107
  43.4 4.5 %shard_map.75 = (bf16[272,128]{1,0:T(8,128)(2,1)S(1)}, f32[128,128]{1,0:T(8,128)S(1)}) custom-call(bf16[256,128,128]{2,1,0:T(8,128)(2,1)S(1)} %bitcast.1, f32[256,128]{1,0:T(8,128)S(1)} %get-tuple-element.25.a_ref.refs_4_.refs_6_, f32[128,128]{1,0:T(8,128)S(1)} %get-tuple-element.26.b_ref.refs_7_, f32[128,128]{1,0:T(8,128)S(1)} %get-tuple-element.30.c_ref.refs_8_), custom_call_target="tpu_custom_call" | custom-call | flops 1073741824 | tf_op jit(solution)/shard_map/pallas_call | solution.py:29
  48.0 1.5 %collective-permute-start.20 = (bf16[176,128]{1,0:T(8,128)(2,1)S(1)}, bf16[176,128]{1,0:T(8,128)(2,1)S(1)}, u32[]{:S(2)}, u32[]{:S(2)}) collective-permute-start(bf16[176,128]{1,0:T(8,128)(2,1)S(1)} %get-tuple-element.33), channel_id=1, source_target_pairs={{0,4},{4,0},{8,12},{12,8},{16,20},{20,16},{24,28},{28,24},{1,5},{5... | collective-permute-start | bytes 135176 | tf_op jit(solution)/shard_map/ppermute | solution.py:107
  49.5 2.0 %collective-permute-start.22 = (bf16[176,128]{1,0:T(8,128)(2,1)S(1)}, bf16[176,128]{1,0:T(8,128)(2,1)S(1)}, u32[]{:S(2)}, u32[]{:S(2)}) collective-permute-start(bf16[176,128]{1,0:T(8,128)(2,1)S(1)} %get-tuple-element.35), channel_id=1, source_target_pairs={{0,12},{4,8},{8,4},{12,0},{16,28},{20,24},{24,20},{28,16},{1,13},{... | collective-permute-start | bytes 135176 | tf_op jit(solution)/shard_map/ppermute | solution.py:107
  52.1 1.0 %collective-permute-start.25 = (bf16[272,128]{1,0:T(8,128)(2,1)S(1)}, bf16[272,128]{1,0:T(8,128)(2,1)S(1)}, u32[]{:S(2)}, u32[]{:S(2)}) collective-permute-start(bf16[272,128]{1,0:T(8,128)(2,1)S(1)} %get-tuple-element.38.refs_2_), channel_id=1, source_target_pairs={{0,2},{1,3},{2,0},{3,1},{4,6},{5,7},{6,4},{7,5},{8,10},{9,11},{10,... | collective-permute-start | bytes 208904 | tf_op jit(solution)/shard_map/ppermute | solution.py:107
  54.6 2.4 %collective-permute-start.23 = (bf16[160,128]{1,0:T(8,128)(2,1)S(1)}, bf16[160,128]{1,0:T(8,128)(2,1)S(1)}, u32[]{:S(2)}, u32[]{:S(2)}) collective-permute-start(bf16[160,128]{1,0:T(8,128)(2,1)S(1)} %get-tuple-element.37), channel_id=1, source_target_pairs={{0,16},{4,20},{8,24},{12,28},{16,0},{20,4},{24,8},{28,12},{1,17},{... | collective-permute-start | bytes 122888 | tf_op jit(solution)/shard_map/ppermute | solution.py:107
  57.5 2.0 %collective-permute-done.23.refs_1_ = bf16[160,128]{1,0:T(8,128)(2,1)S(1)} collective-permute-done((bf16[160,128]{1,0:T(8,128)(2,1)S(1)}, bf16[160,128]{1,0:T(8,128)(2,1)S(1)}, u32[]{:S(2)}, u32[]{:S(2)}) %collective-permute-start.23) | collective-permute-done | bytes 40992 | tf_op jit(solution)/shard_map/ppermute | solution.py:107
  (53 shorter events, 7.0 us)
Async XLA Ops:
  0.6 6.5 %collective-permute-start.4 = (f32[16,128]{1,0:T(8,128)}, f32[16,128]{1,0:T(8,128)S(1)}, u32[]{:S(2)}, u32[]{:S(2)}) collective-permute-start(f32[16,128]{1,0:T(8,128)} %refs_0_.3), channel_id=1, source_target_pairs={{0,8},{4,12},{8,0},{12,4},{16,24},{20,28},{24,16},{28,20},{1,9},{5... | collective-permute-start | bytes 24584 | tf_op jit(solution)/shard_map/ppermute | solution.py:107
  5.2 4.8 %collective-permute-start.5 = (f32[16,128]{1,0:T(8,128)}, f32[16,128]{1,0:T(8,128)S(1)}, u32[]{:S(2)}, u32[]{:S(2)}) collective-permute-start(f32[16,128]{1,0:T(8,128)} %refs_0_.3), channel_id=1, source_target_pairs={{0,12},{4,8},{8,4},{12,0},{16,28},{20,24},{24,20},{28,16},{1,13},{... | collective-permute-start | bytes 24584 | tf_op jit(solution)/shard_map/ppermute | solution.py:107
  5.3 8.0 %collective-permute-start.1 = (f32[64,128]{1,0:T(8,128)}, f32[64,128]{1,0:T(8,128)S(1)}, u32[]{:S(2)}, u32[]{:S(2)}) collective-permute-start(f32[64,128]{1,0:T(8,128)} %refs_0_.2), channel_id=1, source_target_pairs={{0,2},{1,3},{2,0},{3,1},{4,6},{5,7},{6,4},{7,5},{8,10},{9,11},{10,... | collective-permute-start | bytes 98312 | tf_op jit(solution)/shard_map/ppermute | solution.py:107
  7.2 6.1 %collective-permute-start = (f32[64,128]{1,0:T(8,128)}, f32[64,128]{1,0:T(8,128)S(1)}, u32[]{:S(2)}, u32[]{:S(2)}) collective-permute-start(f32[64,128]{1,0:T(8,128)} %refs_0_.2), channel_id=1, source_target_pairs={{0,1},{1,0},{2,3},{3,2},{4,5},{5,4},{6,7},{7,6},{8,9},{9,8},{10,11... | collective-permute-start | bytes 98312 | tf_op jit(solution)/shard_map/ppermute | solution.py:107
  7.2 6.1 %collective-permute-start.2 = (f32[64,128]{1,0:T(8,128)}, f32[64,128]{1,0:T(8,128)S(1)}, u32[]{:S(2)}, u32[]{:S(2)}) collective-permute-start(f32[64,128]{1,0:T(8,128)} %refs_0_.2), channel_id=1, source_target_pairs={{0,3},{1,2},{2,1},{3,0},{4,7},{5,6},{6,5},{7,4},{8,11},{9,10},{10,... | collective-permute-start | bytes 98312 | tf_op jit(solution)/shard_map/ppermute | solution.py:107
  10.7 5.1 %collective-permute-start.6 = (f32[64,128]{1,0:T(8,128)S(1)}, f32[64,128]{1,0:T(8,128)S(1)}, u32[]{:S(2)}, u32[]{:S(2)}) collective-permute-start(f32[64,128]{1,0:T(8,128)S(1)} %shard_map.68.refs_0_), channel_id=1, source_target_pairs={{0,16},{4,20},{8,24},{12,28},{16,0},{20,4},{24,8},{28,12},{1,17},{... | collective-permute-start | bytes 98312 | tf_op jit(solution)/shard_map/ppermute | solution.py:107
  22.9 5.3 %collective-permute-start.9 = (bf16[272,128]{1,0:T(8,128)(2,1)S(1)}, bf16[272,128]{1,0:T(8,128)(2,1)S(1)}, u32[]{:S(2)}, u32[]{:S(2)}) collective-permute-start(bf16[272,128]{1,0:T(8,128)(2,1)S(1)} %get-tuple-element.21.refs_0_), channel_id=1, source_target_pairs={{0,12},{4,8},{8,4},{12,0},{16,28},{20,24},{24,20},{28,16},{1,13},{... | collective-permute-start | bytes 208904 | tf_op jit(solution)/shard_map/ppermute | solution.py:107
  23.4 4.9 %collective-permute-start.8 = (bf16[272,128]{1,0:T(8,128)(2,1)S(1)}, bf16[272,128]{1,0:T(8,128)(2,1)S(1)}, u32[]{:S(2)}, u32[]{:S(2)}) collective-permute-start(bf16[272,128]{1,0:T(8,128)(2,1)S(1)} %get-tuple-element.21.refs_0_), channel_id=1, source_target_pairs={{0,8},{4,12},{8,0},{12,4},{16,24},{20,28},{24,16},{28,20},{1,9},{5... | collective-permute-start | bytes 208904 | tf_op jit(solution)/shard_map/ppermute | solution.py:107
  25.0 4.3 %collective-permute-start.7 = (bf16[272,128]{1,0:T(8,128)(2,1)S(1)}, bf16[272,128]{1,0:T(8,128)(2,1)S(1)}, u32[]{:S(2)}, u32[]{:S(2)}) collective-permute-start(bf16[272,128]{1,0:T(8,128)(2,1)S(1)} %get-tuple-element.21.refs_0_), channel_id=1, source_target_pairs={{0,4},{4,0},{8,12},{12,8},{16,20},{20,16},{24,28},{28,24},{1,5},{5... | collective-permute-start | bytes 208904 | tf_op jit(solution)/shard_map/ppermute | solution.py:107
  26.4 4.4 %collective-permute-start.13 = (bf16[272,128]{1,0:T(8,128)(2,1)S(1)}, bf16[272,128]{1,0:T(8,128)(2,1)S(1)}, u32[]{:S(2)}, u32[]{:S(2)}) collective-permute-start(bf16[272,128]{1,0:T(8,128)(2,1)S(1)} %get-tuple-element.22.refs_2_), channel_id=1, source_target_pairs={{0,3},{1,2},{2,1},{3,0},{4,7},{5,6},{6,5},{7,4},{8,11},{9,10},{10,... | collective-permute-start | bytes 208904 | tf_op jit(solution)/shard_map/ppermute | solution.py:107
  26.4 6.0 %collective-permute-start.12 = (bf16[272,128]{1,0:T(8,128)(2,1)S(1)}, bf16[272,128]{1,0:T(8,128)(2,1)S(1)}, u32[]{:S(2)}, u32[]{:S(2)}) collective-permute-start(bf16[272,128]{1,0:T(8,128)(2,1)S(1)} %get-tuple-element.22.refs_2_), channel_id=1, source_target_pairs={{0,2},{1,3},{2,0},{3,1},{4,6},{5,7},{6,4},{7,5},{8,10},{9,11},{10,... | collective-permute-start | bytes 208904 | tf_op jit(solution)/shard_map/ppermute | solution.py:107
  29.3 5.9 %collective-permute-start.10 = (bf16[272,128]{1,0:T(8,128)(2,1)S(1)}, bf16[272,128]{1,0:T(8,128)(2,1)S(1)}, u32[]{:S(2)}, u32[]{:S(2)}) collective-permute-start(bf16[272,128]{1,0:T(8,128)(2,1)S(1)} %shard_map.71.refs_0_), channel_id=1, source_target_pairs={{0,16},{4,20},{8,24},{12,28},{16,0},{20,4},{24,8},{28,12},{1,17},{... | collective-permute-start | bytes 208904 | tf_op jit(solution)/shard_map/ppermute | solution.py:107
  35.4 5.9 %collective-permute-start.16 = (bf16[128,128]{1,0:T(8,128)(2,1)S(1)}, bf16[128,128]{1,0:T(8,128)(2,1)S(1)}, u32[]{:S(2)}, u32[]{:S(2)}) collective-permute-start(bf16[128,128]{1,0:T(8,128)(2,1)S(1)} %get-tuple-element.23.refs_0_), channel_id=1, source_target_pairs={{0,3},{1,2},{2,1},{3,0},{4,7},{5,6},{6,5},{7,4},{8,11},{9,10},{10,... | collective-permute-start | bytes 98312 | tf_op jit(solution)/shard_map/ppermute | solution.py:107
  35.4 5.8 %collective-permute-start.15 = (bf16[128,128]{1,0:T(8,128)(2,1)S(1)}, bf16[128,128]{1,0:T(8,128)(2,1)S(1)}, u32[]{:S(2)}, u32[]{:S(2)}) collective-permute-start(bf16[128,128]{1,0:T(8,128)(2,1)S(1)} %get-tuple-element.23.refs_0_), channel_id=1, source_target_pairs={{0,2},{1,3},{2,0},{3,1},{4,6},{5,7},{6,4},{7,5},{8,10},{9,11},{10,... | collective-permute-start | bytes 98312 | tf_op jit(solution)/shard_map/ppermute | solution.py:107
  37.0 4.3 %collective-permute-start.14 = (bf16[128,128]{1,0:T(8,128)(2,1)S(1)}, bf16[128,128]{1,0:T(8,128)(2,1)S(1)}, u32[]{:S(2)}, u32[]{:S(2)}) collective-permute-start(bf16[128,128]{1,0:T(8,128)(2,1)S(1)} %get-tuple-element.23.refs_0_), channel_id=1, source_target_pairs={{0,1},{1,0},{2,3},{3,2},{4,5},{5,4},{6,7},{7,6},{8,9},{9,8},{10,11... | collective-permute-start | bytes 98312 | tf_op jit(solution)/shard_map/ppermute | solution.py:107
  41.5 6.4 %collective-permute-start.19 = (bf16[128,128]{1,0:T(8,128)(2,1)S(1)}, bf16[128,128]{1,0:T(8,128)(2,1)S(1)}, u32[]{:S(2)}, u32[]{:S(2)}) collective-permute-start(bf16[128,128]{1,0:T(8,128)(2,1)S(1)} %get-tuple-element.29.refs_0_), channel_id=1, source_target_pairs={{0,3},{1,2},{2,1},{3,0},{4,7},{5,6},{6,5},{7,4},{8,11},{9,10},{10,... | collective-permute-start | bytes 98312 | tf_op jit(solution)/shard_map/ppermute | solution.py:107
  42.6 5.3 %collective-permute-start.18 = (bf16[128,128]{1,0:T(8,128)(2,1)S(1)}, bf16[128,128]{1,0:T(8,128)(2,1)S(1)}, u32[]{:S(2)}, u32[]{:S(2)}) collective-permute-start(bf16[128,128]{1,0:T(8,128)(2,1)S(1)} %get-tuple-element.29.refs_0_), channel_id=1, source_target_pairs={{0,2},{1,3},{2,0},{3,1},{4,6},{5,7},{6,4},{7,5},{8,10},{9,11},{10,... | collective-permute-start | bytes 98312 | tf_op jit(solution)/shard_map/ppermute | solution.py:107
  43.4 4.6 %collective-permute-start.17 = (bf16[128,128]{1,0:T(8,128)(2,1)S(1)}, bf16[128,128]{1,0:T(8,128)(2,1)S(1)}, u32[]{:S(2)}, u32[]{:S(2)}) collective-permute-start(bf16[128,128]{1,0:T(8,128)(2,1)S(1)} %get-tuple-element.29.refs_0_), channel_id=1, source_target_pairs={{0,1},{1,0},{2,3},{3,2},{4,5},{5,4},{6,7},{7,6},{8,9},{9,8},{10,11... | collective-permute-start | bytes 98312 | tf_op jit(solution)/shard_map/ppermute | solution.py:107
  48.0 5.1 %collective-permute-start.20 = (bf16[176,128]{1,0:T(8,128)(2,1)S(1)}, bf16[176,128]{1,0:T(8,128)(2,1)S(1)}, u32[]{:S(2)}, u32[]{:S(2)}) collective-permute-start(bf16[176,128]{1,0:T(8,128)(2,1)S(1)} %get-tuple-element.33), channel_id=1, source_target_pairs={{0,4},{4,0},{8,12},{12,8},{16,20},{20,16},{24,28},{28,24},{1,5},{5... | collective-permute-start | bytes 135176 | tf_op jit(solution)/shard_map/ppermute | solution.py:107
  49.5 5.0 %collective-permute-start.22 = (bf16[176,128]{1,0:T(8,128)(2,1)S(1)}, bf16[176,128]{1,0:T(8,128)(2,1)S(1)}, u32[]{:S(2)}, u32[]{:S(2)}) collective-permute-start(bf16[176,128]{1,0:T(8,128)(2,1)S(1)} %get-tuple-element.35), channel_id=1, source_target_pairs={{0,12},{4,8},{8,4},{12,0},{16,28},{20,24},{24,20},{28,16},{1,13},{... | collective-permute-start | bytes 135176 | tf_op jit(solution)/shard_map/ppermute | solution.py:107
  51.6 5.4 %collective-permute-start.26 = (bf16[272,128]{1,0:T(8,128)(2,1)S(1)}, bf16[272,128]{1,0:T(8,128)(2,1)S(1)}, u32[]{:S(2)}, u32[]{:S(2)}) collective-permute-start(bf16[272,128]{1,0:T(8,128)(2,1)S(1)} %get-tuple-element.38.refs_2_), channel_id=1, source_target_pairs={{0,3},{1,2},{2,1},{3,0},{4,7},{5,6},{6,5},{7,4},{8,11},{9,10},{10,... | collective-permute-start | bytes 208904 | tf_op jit(solution)/shard_map/ppermute | solution.py:107
  52.1 5.4 %collective-permute-start.25 = (bf16[272,128]{1,0:T(8,128)(2,1)S(1)}, bf16[272,128]{1,0:T(8,128)(2,1)S(1)}, u32[]{:S(2)}, u32[]{:S(2)}) collective-permute-start(bf16[272,128]{1,0:T(8,128)(2,1)S(1)} %get-tuple-element.38.refs_2_), channel_id=1, source_target_pairs={{0,2},{1,3},{2,0},{3,1},{4,6},{5,7},{6,4},{7,5},{8,10},{9,11},{10,... | collective-permute-start | bytes 208904 | tf_op jit(solution)/shard_map/ppermute | solution.py:107
  53.1 4.5 %collective-permute-start.24 = (bf16[272,128]{1,0:T(8,128)(2,1)S(1)}, bf16[272,128]{1,0:T(8,128)(2,1)S(1)}, u32[]{:S(2)}, u32[]{:S(2)}) collective-permute-start(bf16[272,128]{1,0:T(8,128)(2,1)S(1)} %get-tuple-element.38.refs_2_), channel_id=1, source_target_pairs={{0,1},{1,0},{2,3},{3,2},{4,5},{5,4},{6,7},{7,6},{8,9},{9,8},{10,11... | collective-permute-start | bytes 208904 | tf_op jit(solution)/shard_map/ppermute | solution.py:107
  54.6 5.0 %collective-permute-start.23 = (bf16[160,128]{1,0:T(8,128)(2,1)S(1)}, bf16[160,128]{1,0:T(8,128)(2,1)S(1)}, u32[]{:S(2)}, u32[]{:S(2)}) collective-permute-start(bf16[160,128]{1,0:T(8,128)(2,1)S(1)} %get-tuple-element.37), channel_id=1, source_target_pairs={{0,16},{4,20},{8,24},{12,28},{16,0},{20,4},{24,8},{28,12},{1,17},{... | collective-permute-start | bytes 122888 | tf_op jit(solution)/shard_map/ppermute | solution.py:107
  (8 other events, 35.1 us)

commit v3 on v2

--- a/solution.py
+++ b/solution.py
@@ -11,7 +11,8 @@
 BF16 = jnp.bfloat16
 NORM_ROWS = 16
 VMEM_LIMIT = 24 << 20
-PLACE_FLOPS = 4 * 10**9
+HOLD_FLOPS = 5 * 10**9
+PLACE_FLOPS = 2 * 10**9
 
 
 damping = 0.9
@@ -38,7 +39,7 @@
 
 
 def divisor(n, most):
-    return next(g for g in (64, 32, 16, 8, 4, 2) if g <= most and n % g == 0)
+    return next(g for g in (256, 128, 64, 32, 16, 8, 4, 2) if g <= most and n % g == 0)
 
 
 def dot(x, y):
@@ -114,18 +115,6 @@
     )
 
 
-def times_c(block, pair_c):
-    group, rows_j, depth = block.shape
-    rank = pair_c.shape[1] // 2
-    half = group // 2
-    left = block[:half].reshape(half * rows_j, depth)
-    right = block[half:].reshape(half * rows_j, depth)
-    out = dot(jnp.concatenate([left, right], 1), pair_c)
-    return jnp.concatenate(
-        [out[:, :rank].reshape(half, rows_j, rank), out[:, rank:].reshape(half, rows_j, rank)], 0
-    )
-
-
 def place_kernel(axis, weight, *refs):
     *ins, out = refs
     rows = ins[0].shape[0]
@@ -134,21 +123,37 @@
         out[pl.ds(pl.multiple_of((digit ^ q) * rows, rows), rows)] = ref[...]
 
 
-def gather_digit(x, axis, weight, radix):
+def gather_digit(x, own, axis, weight, radix):
     got = [swap(x, axis, weight, q) for q in range(1, radix)]
     (x,) = call(
         functools.partial(place_kernel, axis, weight),
         [((x.shape[0] * radix, x.shape[1]), x.dtype)],
-        x, *got,
+        own, *got,
         flops=PLACE_FLOPS,
     )
     return x
 
 
-def gather(x, axis):
+def gather(x, own, axis):
     for weight, radix in digits(lax.axis_size(axis)):
-        x = gather_digit(x, axis, weight, radix)
+        x = own = gather_digit(x, own, axis, weight, radix)
     return x
+
+
+def hold_kernel(*refs):
+    half = len(refs) // 2
+    for ref, out in zip(refs[:half], refs[half:]):
+        out[...] = ref[...]
+
+
+def hold(*arrays):
+    whole = pl.BlockSpec(memory_space=pltpu.VMEM)
+    return pl.pallas_call(
+        hold_kernel,
+        out_specs=[whole] * len(arrays),
+        out_shape=[pltpu.VMEM(x.shape, x.dtype) for x in arrays],
+        cost_estimate=pl.CostEstimate(flops=HOLD_FLOPS, bytes_accessed=0, transcendentals=0),
+    )(*[pltpu.with_memory_space_constraint(x, pltpu.HBM) for x in arrays])
 
 
 def add_kernel(norm_at, *refs):
@@ -169,7 +174,7 @@
 
 def sum_c(t_ref, a_ref, b16, acc):
     rows_i, rows_j, depth = t_ref.shape
-    group = divisor(rows_i, 32)
+    group = divisor(rows_i, 256)
     acc[...] = jnp.zeros_like(acc)
 
     def step(g, carry):
@@ -182,38 +187,76 @@
     lax.fori_loop(0, rows_i // group, step, 0)
 
 
-def first_kernel(t_ref, a_ref, b_ref, c_ref, row_ref, col_ref, acc_a, acc_b, acc_c):
+def sum_b(t_ref, a_ref, c16, acc):
     rows_i, rows_j, depth = t_ref.shape
-    group = divisor(rows_i, 64)
+    group = divisor(rows_i, 256)
+    acc[...] = jnp.zeros_like(acc)
+
+    def step(g, carry):
+        at = pl.ds(pl.multiple_of(g * group, group), group)
+        a16 = a_ref[at].astype(BF16)
+        pairs = jnp.concatenate([a16[q : q + 1] * c16 for q in range(group)], 0)
+        block = t_ref[at]
+        acc[...] += dot(jnp.concatenate([block[q] for q in range(group)], 1), pairs)
+        return carry
+
+    lax.fori_loop(0, rows_i // group, step, 0)
+
+
+def sum_a(t_ref, a_ref, b16, c16, acc, acc_b=None):
+    rows_i, rows_j, depth = t_ref.shape
+    rank = c16.shape[1]
+    group = divisor(rows_i, 256)
+    half = group // 2
+    b32 = b16.astype(F32)
+    pair_c = twice(c16)
+    if acc_b is not None:
+        acc_b[...] = jnp.zeros_like(acc_b)
+
+    def step(g, carry):
+        at = pl.ds(pl.multiple_of(g * group, group), group)
+        block = t_ref[at]
+        if acc_b is not None:
+            a32 = a_ref[at].astype(BF16).astype(F32)
+            total = acc_b[...]
+        sums = [None] * group
+        for q in range(half):
+            along = dot(jnp.concatenate([block[q], block[q + half]], 1), pair_c)
+            for i, part in ((q, along[:, :rank]), (q + half, along[:, rank:])):
+                sums[i] = jnp.sum(part * b32, axis=0, keepdims=True)
+                if acc_b is not None:
+                    total = total + part * a32[i : i + 1]
+        acc[at] = jnp.concatenate(sums, 0)
+        if acc_b is not None:
+            acc_b[...] = total
+        return carry
+
+    lax.fori_loop(0, rows_i // group, step, 0)
+
+
+def first_b_kernel(t_ref, a_ref, c_ref, acc):
+    sum_b(t_ref, a_ref, c_ref[...].astype(BF16), acc)
+
+
+def first_c_kernel(t_ref, a_ref, b_ref, c_ref, acc_b, row_ref, acc_c):
+    rows_j, depth = b_ref.shape[0], c_ref.shape[0]
     a16 = a_ref[...].astype(BF16)
     b16 = b_ref[...].astype(BF16)
     c16 = c_ref[...].astype(BF16)
-    b32 = b16.astype(F32)
-    pair_c = twice(c16)
-    acc_b[...] = jnp.zeros_like(acc_b)
-    acc_c[...] = jnp.zeros_like(acc_c)
-
-    def step(g, carry):
-        at = pl.ds(pl.multiple_of(g * group, group), group)
-        part16 = a_ref[at].astype(BF16)
-        part32 = part16.astype(F32)
-        block = t_ref[at]
-        along = times_c(block, pair_c)
-        acc_a[at] = jnp.sum(along * b32[None], axis=1)
-        total = acc_b[...]
-        for q in range(group):
-            total = total + along[q] * part32[q : q + 1]
-        acc_b[...] = total
-        pairs = jnp.concatenate([part16[q : q + 1] * b16 for q in range(group)], 0)
-        acc_c[...] += dot_rows(block.reshape(group * rows_j, depth), pairs)
-        return carry
-
-    lax.fori_loop(0, rows_i // group, step, 0)
+    sum_c(t_ref, a_ref, b16, acc_c)
     gram_a, gram_b, gram_c = gram(a16), gram(b16), gram(c16)
     row_ref[:rows_j] = (acc_b[...] - dot_wide(b16, gram_a * gram_c)).astype(BF16)
     row_ref[rows_j : rows_j + depth] = (acc_c[...] - dot_wide(c16, gram_a * gram_b)).astype(BF16)
     put_norm(row_ref, rows_j + depth, squares(a16))
-    col_ref[:rows_i] = (acc_a[...] - dot_wide(a16, gram_b * gram_c)).astype(BF16)
+
+
+def first_a_kernel(t_ref, a_ref, b_ref, c_ref, col_ref, acc_a):
+    rows_i = a_ref.shape[0]
+    a16 = a_ref[...].astype(BF16)
+    b16 = b_ref[...].astype(BF16)
+    c16 = c_ref[...].astype(BF16)
+    sum_a(t_ref, a_ref, b16, c16, acc_a)
+    col_ref[:rows_i] = (acc_a[...] - dot_wide(a16, gram(b16) * gram(c16))).astype(BF16)
     put_norm(col_ref, rows_i, squares(b16))
 
 
@@ -249,27 +292,11 @@
 
 
 def second_ab_kernel(t_ref, a_ref, b_ref, c_ref, col_ref, grad_b, acc_a):
-    rows_i, rows_j, depth = t_ref.shape
-    group = divisor(rows_i, 32)
+    rows_i = a_ref.shape[0]
     a16 = a_ref[...].astype(BF16)
     b16 = b_ref[...].astype(BF16)
     c16 = c_ref[...].astype(BF16)
-    b32 = b16.astype(F32)
-    pair_c = twice(c16)
-    grad_b[...] = jnp.zeros_like(grad_b)
-
-    def step(g, carry):
-        at = pl.ds(pl.multiple_of(g * group, group), group)
-        a32 = a_ref[at].astype(BF16).astype(F32)
-        along = times_c(t_ref[at], pair_c)
-        acc_a[at] = jnp.sum(along * b32[None], axis=1)
-        total = grad_b[...]
-        for q in range(group):
-            total = total + along[q] * a32[q : q + 1]
-        grad_b[...] = total
-        return carry
-
-    lax.fori_loop(0, rows_i // group, step, 0)
+    sum_a(t_ref, a_ref, b16, c16, acc_a, grad_b)
     gram_c = gram(c16)
     col_ref[:rows_i] = (acc_a[...] - dot_wide(a16, gram(b16) * gram_c)).astype(BF16)
     put_norm(col_ref, rows_i, squares(b16))
@@ -351,16 +378,26 @@
     rows_i, rows_j, depth = tensor.shape
     rank = factor_a.shape[1]
     own_j = factor_b.shape[0]
-    c = factor_c
-    b = gather(factor_b, "row")
-    a = gather(factor_a, "col")
-
-    to_row, to_col = call(
-        first_kernel,
-        [((rows_j + depth + NORM_ROWS, rank), BF16), ((rows_i + NORM_ROWS, rank), BF16)],
+    held_a, held_b, c = hold(factor_a, factor_b, factor_c)
+    b = gather(factor_b, held_b, "row")
+    a = gather(factor_a, held_a, "col")
+
+    (grad_b,) = call(
+        first_b_kernel, [(b.shape, F32)], tensor, a, c, flops=2 * tensor.size * rank
+    )
+    (to_row,) = call(
+        first_c_kernel,
+        [((rows_j + depth + NORM_ROWS, rank), BF16)],
+        tensor, a, b, c, grad_b,
+        scratch=[pltpu.VMEM(c.shape, F32)],
+        flops=2 * tensor.size * rank,
+    )
+    (to_col,) = call(
+        first_a_kernel,
+        [((rows_i + NORM_ROWS, rank), BF16)],
         tensor, a, b, c,
-        scratch=[pltpu.VMEM((n, rank), F32) for n in (rows_i, rows_j, depth)],
-        flops=6 * tensor.size * rank,
+        scratch=[pltpu.VMEM(a.shape, F32)],
+        flops=2 * tensor.size * rank,
     )
     rows = sum_parts(to_row, "row", rows_j + depth)
     cols = sum_parts(to_col, "col", rows_i)

time: 60.5 us -> 55.5 us (0.917)
  waiting for transfers between devices: 14.3 us -> 8.95 us
  starting transfers between devices: 27.7 us -> 30.3 us
  local copies, waits for them, and re-layouts: 1.74 us -> 0.01 us
    ppermute x27, waiting for transfers between devices: 14.3 us -> 8.95 us  [swap(): lax.ppermute(x, axis, [(i, i ^ q * weight) for i in range(lax.axis_size(a...]
    ppermute x27, starting transfers between devices: 27.7 us -> 30.3 us  [swap(): lax.ppermute(x, axis, [(i, i ^ q * weight) for i in range(lax.axis_size(a...]
    unnamed x10 -> x4, local copies, waits for them, and re-layouts: 1.74 us -> 0.01 us
    pallas_call x12 -> x14, Pallas kernels: 15.8 us -> 14.4 us  [call(): pl.pallas_call(body, in_specs=[whole] * len(operands), out_specs=[whole]...]
    pallas_call x0 -> x1, Pallas kernels: none -> 0.88 us  [hold(): pl.pallas_call(hold_kernel, out_specs=[whole] * len(arrays), out_shape=[p...]
  transfers between devices with their start and end apart: 27 -> 27, of which waited for: 11 -> 8; matrix products, arithmetic and copies ran while one was open for 0% -> 0% of each run, Pallas kernels for 14% -> 21%
where the time goes in v3:
time: 55.5 us; the launch traced here: 55.3 us
  starting transfers between devices  30.3 us (55%)
  Pallas kernels  15.3 us (28%)
  waiting for transfers between devices  8.95 us (16%)
  between operations  0.81 us (1%)
    ppermute x27, starting transfers between devices, swap(): lax.ppermute(x, axis, [(i, i ^ q * weight) for i in range(lax.axis_size(a...  30.3 us
    pallas_call x14, Pallas kernels, call(): pl.pallas_call(body, in_specs=[whole] * len(operands), out_specs=[whole]...  14.4 us
    ppermute x27, waiting for transfers between devices, swap(): lax.ppermute(x, axis, [(i, i ^ q * weight) for i in range(lax.axis_size(a...  8.95 us
  transfers between devices with their start and end apart: 27, of which 8 were waited for; matrix products, arithmetic and copies ran while one was open for 0% of the time, Pallas kernels for 21%

profile of v3, /device:TPU:0, one launch (start us, length us, event | category | flops | bytes accessed | tf_op | source)
XLA Modules:
  0.0 55.3 jit_solution(3200307205773907388)
XLA Ops:
  0.6 3.0 %collective-permute-start.3 = (f32[16,128]{1,0:T(8,128)}, f32[16,128]{1,0:T(8,128)S(1)}, u32[]{:S(2)}, u32[]{:S(2)}) collective-permute-start(f32[16,128]{1,0:T(8,128)} %refs_1_.1), channel_id=1, source_target_pairs={{0,4},{4,0},{8,12},{12,8},{16,20},{20,16},{24,28},{28,24},{1,5},{5... | collective-permute-start | bytes 24584 | tf_op jit(solution)/shard_map/ppermute | solution.py:108
  3.6 1.5 %collective-permute-start.5 = (f32[16,128]{1,0:T(8,128)}, f32[16,128]{1,0:T(8,128)S(1)}, u32[]{:S(2)}, u32[]{:S(2)}) collective-permute-start(f32[16,128]{1,0:T(8,128)} %refs_1_.1), channel_id=1, source_target_pairs={{0,12},{4,8},{8,4},{12,0},{16,28},{20,24},{24,20},{28,16},{1,13},{... | collective-permute-start | bytes 24584 | tf_op jit(solution)/shard_map/ppermute | solution.py:108
  5.2 2.0 %collective-permute-start.2 = (f32[64,128]{1,0:T(8,128)}, f32[64,128]{1,0:T(8,128)S(1)}, u32[]{:S(2)}, u32[]{:S(2)}) collective-permute-start(f32[64,128]{1,0:T(8,128)} %refs_0_.1), channel_id=1, source_target_pairs={{0,3},{1,2},{2,1},{3,0},{4,7},{5,6},{6,5},{7,4},{8,11},{9,10},{10,... | collective-permute-start | bytes 98312 | tf_op jit(solution)/shard_map/ppermute | solution.py:108
  7.3 0.9 %shard_map.67 = (f32[64,128]{1,0:T(8,128)S(1)}, f32[16,128]{1,0:T(8,128)S(1)}, f32[128,128]{1,0:T(8,128)S(1)}) custom-call(f32[64,128]{1,0:T(8,128)} %refs_0_.1, f32[16,128]{1,0:T(8,128)} %refs_1_.1, f32[128,128]{1,0:T(8,128)} %refs_2_.1), custom_call_target="tpu_custom_call" | custom-call | flops 5000000000 | tf_op jit(solution)/shard_map/pallas_call | solution.py:151
  9.1 2.6 %collective-permute-start.6 = (f32[64,128]{1,0:T(8,128)S(1)}, f32[64,128]{1,0:T(8,128)S(1)}, u32[]{:S(2)}, u32[]{:S(2)}) collective-permute-start(f32[64,128]{1,0:T(8,128)S(1)} %shard_map.69.refs_0_), channel_id=1, source_target_pairs={{0,16},{4,20},{8,24},{12,28},{16,0},{20,4},{24,8},{28,12},{1,17},{... | collective-permute-start | bytes 98312 | tf_op jit(solution)/shard_map/ppermute | solution.py:108
  12.2 2.3 %shard_map.71.acc_b = f32[128,128]{1,0:T(8,128)S(1)} custom-call(bf16[256,128,128]{2,1,0:T(8,128)(2,1)S(1)} %copy-done, f32[256,128]{1,0:T(8,128)S(1)} %shard_map.68.a_ref.refs_6_, f32[128,128]{1,0:T(8,128)S(1)} %get-tuple-element.24.c_ref.refs_8_.refs_5_), custom_call_target="tpu_custom_call" | custom-call | flops 1073741824 | tf_op jit(solution)/shard_map/pallas_call | solution.py:30
  14.6 2.6 %shard_map.72.refs_0_ = bf16[272,128]{1,0:T(8,128)(2,1)S(1)} custom-call(bf16[256,128,128]{2,1,0:T(8,128)(2,1)S(1)} %copy-done, f32[256,128]{1,0:T(8,128)S(1)} %shard_map.68.a_ref.refs_6_, f32[128,128]{1,0:T(8,128)S(1)} %shard_map.70.b_ref.refs_7_, f32[128,128]{1,0:T(8,128)S(1)} %get-tuple-element.24.c_ref.refs_8_.refs_5_, f32[128,128]{1,0:T(8,128)S(1)} %shard_map.71.acc_b), custom_call_target="tpu_custom_call" | custom-call | flops 1073741824 | tf_op jit(solution)/shard_map/pallas_call | solution.py:30
  17.2 2.6 %collective-permute-start.9 = (bf16[272,128]{1,0:T(8,128)(2,1)S(1)}, bf16[272,128]{1,0:T(8,128)(2,1)S(1)}, u32[]{:S(2)}, u32[]{:S(2)}) collective-permute-start(bf16[272,128]{1,0:T(8,128)(2,1)S(1)} %shard_map.72.refs_0_), channel_id=1, source_target_pairs={{0,12},{4,8},{8,4},{12,0},{16,28},{20,24},{24,20},{28,16},{1,13},{... | collective-permute-start | bytes 208904 | tf_op jit(solution)/shard_map/ppermute | solution.py:108
  20.7 2.6 %shard_map.74.refs_2_ = bf16[272,128]{1,0:T(8,128)(2,1)S(1)} custom-call(bf16[256,128,128]{2,1,0:T(8,128)(2,1)S(1)} %copy-done, f32[256,128]{1,0:T(8,128)S(1)} %shard_map.68.a_ref.refs_6_, f32[128,128]{1,0:T(8,128)S(1)} %shard_map.70.b_ref.refs_7_, f32[128,128]{1,0:T(8,128)S(1)} %get-tuple-element.24.c_ref.refs_8_.refs_5_), custom_call_target="tpu_custom_call" | custom-call | flops 1073741824 | tf_op jit(solution)/shard_map/pallas_call | solution.py:30
  23.4 1.1 %collective-permute-start.12 = (bf16[272,128]{1,0:T(8,128)(2,1)S(1)}, bf16[272,128]{1,0:T(8,128)(2,1)S(1)}, u32[]{:S(2)}, u32[]{:S(2)}) collective-permute-start(bf16[272,128]{1,0:T(8,128)(2,1)S(1)} %shard_map.74.refs_2_), channel_id=1, source_target_pairs={{0,2},{1,3},{2,0},{3,1},{4,6},{5,7},{6,4},{7,5},{8,10},{9,11},{10,... | collective-permute-start | bytes 208904 | tf_op jit(solution)/shard_map/ppermute | solution.py:108
  24.5 0.8 %collective-permute-start.11 = (bf16[272,128]{1,0:T(8,128)(2,1)S(1)}, bf16[272,128]{1,0:T(8,128)(2,1)S(1)}, u32[]{:S(2)}, u32[]{:S(2)}) collective-permute-start(bf16[272,128]{1,0:T(8,128)(2,1)S(1)} %shard_map.74.refs_2_), channel_id=1, source_target_pairs={{0,1},{1,0},{2,3},{3,2},{4,5},{5,4},{6,7},{7,6},{8,9},{9,8},{10,11... | collective-permute-start | bytes 208904 | tf_op jit(solution)/shard_map/ppermute | solution.py:108
  25.3 2.7 %collective-permute-start.10 = (bf16[272,128]{1,0:T(8,128)(2,1)S(1)}, bf16[272,128]{1,0:T(8,128)(2,1)S(1)}, u32[]{:S(2)}, u32[]{:S(2)}) collective-permute-start(bf16[272,128]{1,0:T(8,128)(2,1)S(1)} %shard_map.73.refs_0_), channel_id=1, source_target_pairs={{0,16},{4,20},{8,24},{12,28},{16,0},{20,4},{24,8},{28,12},{1,17},{... | collective-permute-start | bytes 208904 | tf_op jit(solution)/shard_map/ppermute | solution.py:108
  28.6 3.5 %collective-permute-done.10.refs_1_ = bf16[272,128]{1,0:T(8,128)(2,1)S(1)} collective-permute-done((bf16[272,128]{1,0:T(8,128)(2,1)S(1)}, bf16[272,128]{1,0:T(8,128)(2,1)S(1)}, u32[]{:S(2)}, u32[]{:S(2)}) %collective-permute-start.10) | collective-permute-done | bytes 69664 | tf_op jit(solution)/shard_map/ppermute | solution.py:108
  32.3 1.0 %collective-permute-start.15 = (bf16[128,128]{1,0:T(8,128)(2,1)S(1)}, bf16[128,128]{1,0:T(8,128)(2,1)S(1)}, u32[]{:S(2)}, u32[]{:S(2)}) collective-permute-start(bf16[128,128]{1,0:T(8,128)(2,1)S(1)} %get-tuple-element.25.refs_0_), channel_id=1, source_target_pairs={{0,2},{1,3},{2,0},{3,1},{4,6},{5,7},{6,4},{7,5},{8,10},{9,11},{10,... | collective-permute-start | bytes 98312 | tf_op jit(solution)/shard_map/ppermute | solution.py:108
  33.3 0.8 %collective-permute-start.14 = (bf16[128,128]{1,0:T(8,128)(2,1)S(1)}, bf16[128,128]{1,0:T(8,128)(2,1)S(1)}, u32[]{:S(2)}, u32[]{:S(2)}) collective-permute-start(bf16[128,128]{1,0:T(8,128)(2,1)S(1)} %get-tuple-element.25.refs_0_), channel_id=1, source_target_pairs={{0,1},{1,0},{2,3},{3,2},{4,5},{5,4},{6,7},{7,6},{8,9},{9,8},{10,11... | collective-permute-start | bytes 98312 | tf_op jit(solution)/shard_map/ppermute | solution.py:108
  34.1 2.4 %shard_map.76 = (f32[128,128]{1,0:T(8,128)S(1)}, f32[128,128]{1,0:T(8,128)S(1)}) custom-call(bf16[256,128,128]{2,1,0:T(8,128)(2,1)S(1)} %copy-done, f32[256,128]{1,0:T(8,128)S(1)} %get-tuple-element.27.a_ref.refs_4_.refs_6_, f32[128,128]{1,0:T(8,128)S(1)} %get-tuple-element.28.b_ref.refs_7_), custom_call_target="tpu_custom_call" | custom-call | flops 1073741824 | tf_op jit(solution)/shard_map/pallas_call | solution.py:30
  37.4 1.1 %collective-permute-start.18 = (bf16[128,128]{1,0:T(8,128)(2,1)S(1)}, bf16[128,128]{1,0:T(8,128)(2,1)S(1)}, u32[]{:S(2)}, u32[]{:S(2)}) collective-permute-start(bf16[128,128]{1,0:T(8,128)(2,1)S(1)} %get-tuple-element.31.refs_0_), channel_id=1, source_target_pairs={{0,2},{1,3},{2,0},{3,1},{4,6},{5,7},{6,4},{7,5},{8,10},{9,11},{10,... | collective-permute-start | bytes 98312 | tf_op jit(solution)/shard_map/ppermute | solution.py:108
  38.7 3.3 %shard_map.78 = (bf16[272,128]{1,0:T(8,128)(2,1)S(1)}, f32[128,128]{1,0:T(8,128)S(1)}) custom-call(bf16[256,128,128]{2,1,0:T(8,128)(2,1)S(1)} %copy-done, f32[256,128]{1,0:T(8,128)S(1)} %get-tuple-element.27.a_ref.refs_4_.refs_6_, f32[128,128]{1,0:T(8,128)S(1)} %get-tuple-element.28.b_ref.refs_7_, f32[128,128]{1,0:T(8,128)S(1)} %get-tuple-element.32.c_ref.refs_8_), custom_call_target="tpu_custom_call" | custom-call | flops 1073741824 | tf_op jit(solution)/shard_map/pallas_call | solution.py:30
  42.1 1.6 %collective-permute-start.20 = (bf16[176,128]{1,0:T(8,128)(2,1)S(1)}, bf16[176,128]{1,0:T(8,128)(2,1)S(1)}, u32[]{:S(2)}, u32[]{:S(2)}) collective-permute-start(bf16[176,128]{1,0:T(8,128)(2,1)S(1)} %get-tuple-element.35), channel_id=1, source_target_pairs={{0,4},{4,0},{8,12},{12,8},{16,20},{20,16},{24,28},{28,24},{1,5},{5... | collective-permute-start | bytes 135176 | tf_op jit(solution)/shard_map/ppermute | solution.py:108
  44.2 1.5 %collective-permute-start.22 = (bf16[176,128]{1,0:T(8,128)(2,1)S(1)}, bf16[176,128]{1,0:T(8,128)(2,1)S(1)}, u32[]{:S(2)}, u32[]{:S(2)}) collective-permute-start(bf16[176,128]{1,0:T(8,128)(2,1)S(1)} %get-tuple-element.37), channel_id=1, source_target_pairs={{0,12},{4,8},{8,4},{12,0},{16,28},{20,24},{24,20},{28,16},{1,13},{... | collective-permute-start | bytes 135176 | tf_op jit(solution)/shard_map/ppermute | solution.py:108
  45.7 1.1 %collective-permute-start.25 = (bf16[272,128]{1,0:T(8,128)(2,1)S(1)}, bf16[272,128]{1,0:T(8,128)(2,1)S(1)}, u32[]{:S(2)}, u32[]{:S(2)}) collective-permute-start(bf16[272,128]{1,0:T(8,128)(2,1)S(1)} %get-tuple-element.40.refs_2_), channel_id=1, source_target_pairs={{0,2},{1,3},{2,0},{3,1},{4,6},{5,7},{6,4},{7,5},{8,10},{9,11},{10,... | collective-permute-start | bytes 208904 | tf_op jit(solution)/shard_map/ppermute | solution.py:108
  47.8 1.4 %collective-permute-done.22.refs_3_ = bf16[176,128]{1,0:T(8,128)(2,1)S(1)} collective-permute-done((bf16[176,128]{1,0:T(8,128)(2,1)S(1)}, bf16[176,128]{1,0:T(8,128)(2,1)S(1)}, u32[]{:S(2)}, u32[]{:S(2)}) %collective-permute-start.22) | collective-permute-done | bytes 45088 | tf_op jit(solution)/shard_map/ppermute | solution.py:108
  49.2 3.5 %collective-permute-start.23 = (bf16[160,128]{1,0:T(8,128)(2,1)S(1)}, bf16[160,128]{1,0:T(8,128)(2,1)S(1)}, u32[]{:S(2)}, u32[]{:S(2)}) collective-permute-start(bf16[160,128]{1,0:T(8,128)(2,1)S(1)} %get-tuple-element.39), channel_id=1, source_target_pairs={{0,16},{4,20},{8,24},{12,28},{16,0},{20,4},{24,8},{28,12},{1,17},{... | collective-permute-start | bytes 122888 | tf_op jit(solution)/shard_map/ppermute | solution.py:108
  52.6 2.0 %collective-permute-done.23.refs_1_ = bf16[160,128]{1,0:T(8,128)(2,1)S(1)} collective-permute-done((bf16[160,128]{1,0:T(8,128)(2,1)S(1)}, bf16[160,128]{1,0:T(8,128)(2,1)S(1)}, u32[]{:S(2)}, u32[]{:S(2)}) %collective-permute-start.23) | collective-permute-done | bytes 40992 | tf_op jit(solution)/shard_map/ppermute | solution.py:108
  (49 shorter events, 6.7 us)
Async XLA Ops:
  0.6 7.5 %collective-permute-start.3 = (f32[16,128]{1,0:T(8,128)}, f32[16,128]{1,0:T(8,128)S(1)}, u32[]{:S(2)}, u32[]{:S(2)}) collective-permute-start(f32[16,128]{1,0:T(8,128)} %refs_1_.1), channel_id=1, source_target_pairs={{0,4},{4,0},{8,12},{12,8},{16,20},{20,16},{24,28},{28,24},{1,5},{5... | collective-permute-start | bytes 24584 | tf_op jit(solution)/shard_map/ppermute | solution.py:108
  3.6 4.8 %collective-permute-start.5 = (f32[16,128]{1,0:T(8,128)}, f32[16,128]{1,0:T(8,128)S(1)}, u32[]{:S(2)}, u32[]{:S(2)}) collective-permute-start(f32[16,128]{1,0:T(8,128)} %refs_1_.1), channel_id=1, source_target_pairs={{0,12},{4,8},{8,4},{12,0},{16,28},{20,24},{24,20},{28,16},{1,13},{... | collective-permute-start | bytes 24584 | tf_op jit(solution)/shard_map/ppermute | solution.py:108
  5.2 6.4 %collective-permute-start = (f32[64,128]{1,0:T(8,128)}, f32[64,128]{1,0:T(8,128)S(1)}, u32[]{:S(2)}, u32[]{:S(2)}) collective-permute-start(f32[64,128]{1,0:T(8,128)} %refs_0_.1), channel_id=1, source_target_pairs={{0,1},{1,0},{2,3},{3,2},{4,5},{5,4},{6,7},{7,6},{8,9},{9,8},{10,11... | collective-permute-start | bytes 98312 | tf_op jit(solution)/shard_map/ppermute | solution.py:108
  5.2 6.4 %collective-permute-start.2 = (f32[64,128]{1,0:T(8,128)}, f32[64,128]{1,0:T(8,128)S(1)}, u32[]{:S(2)}, u32[]{:S(2)}) collective-permute-start(f32[64,128]{1,0:T(8,128)} %refs_0_.1), channel_id=1, source_target_pairs={{0,3},{1,2},{2,1},{3,0},{4,7},{5,6},{6,5},{7,4},{8,11},{9,10},{10,... | collective-permute-start | bytes 98312 | tf_op jit(solution)/shard_map/ppermute | solution.py:108
  8.2 4.0 %collective-permute-start.1 = (f32[64,128]{1,0:T(8,128)S(1)}, f32[64,128]{1,0:T(8,128)S(1)}, u32[]{:S(2)}, u32[]{:S(2)}) collective-permute-start(f32[64,128]{1,0:T(8,128)S(1)} %copy-done.1), channel_id=1, source_target_pairs={{0,2},{1,3},{2,0},{3,1},{4,6},{5,7},{6,4},{7,5},{8,10},{9,11},{10,... | collective-permute-start | bytes 98312 | tf_op jit(solution)/shard_map/ppermute | solution.py:108
  9.1 5.5 %collective-permute-start.6 = (f32[64,128]{1,0:T(8,128)S(1)}, f32[64,128]{1,0:T(8,128)S(1)}, u32[]{:S(2)}, u32[]{:S(2)}) collective-permute-start(f32[64,128]{1,0:T(8,128)S(1)} %shard_map.69.refs_0_), channel_id=1, source_target_pairs={{0,16},{4,20},{8,24},{12,28},{16,0},{20,4},{24,8},{28,12},{1,17},{... | collective-permute-start | bytes 98312 | tf_op jit(solution)/shard_map/ppermute | solution.py:108
  17.2 7.3 %collective-permute-start.9 = (bf16[272,128]{1,0:T(8,128)(2,1)S(1)}, bf16[272,128]{1,0:T(8,128)(2,1)S(1)}, u32[]{:S(2)}, u32[]{:S(2)}) collective-permute-start(bf16[272,128]{1,0:T(8,128)(2,1)S(1)} %shard_map.72.refs_0_), channel_id=1, source_target_pairs={{0,12},{4,8},{8,4},{12,0},{16,28},{20,24},{24,20},{28,16},{1,13},{... | collective-permute-start | bytes 208904 | tf_op jit(solution)/shard_map/ppermute | solution.py:108
  19.8 5.5 %collective-permute-start.8 = (bf16[272,128]{1,0:T(8,128)(2,1)S(1)}, bf16[272,128]{1,0:T(8,128)(2,1)S(1)}, u32[]{:S(2)}, u32[]{:S(2)}) collective-permute-start(bf16[272,128]{1,0:T(8,128)(2,1)S(1)} %shard_map.72.refs_0_), channel_id=1, source_target_pairs={{0,8},{4,12},{8,0},{12,4},{16,24},{20,28},{24,16},{28,20},{1,9},{5... | collective-permute-start | bytes 208904 | tf_op jit(solution)/shard_map/ppermute | solution.py:108
  20.2 5.1 %collective-permute-start.7 = (bf16[272,128]{1,0:T(8,128)(2,1)S(1)}, bf16[272,128]{1,0:T(8,128)(2,1)S(1)}, u32[]{:S(2)}, u32[]{:S(2)}) collective-permute-start(bf16[272,128]{1,0:T(8,128)(2,1)S(1)} %shard_map.72.refs_0_), channel_id=1, source_target_pairs={{0,4},{4,0},{8,12},{12,8},{16,20},{20,16},{24,28},{28,24},{1,5},{5... | collective-permute-start | bytes 208904 | tf_op jit(solution)/shard_map/ppermute | solution.py:108
  23.3 4.7 %collective-permute-start.13 = (bf16[272,128]{1,0:T(8,128)(2,1)S(1)}, bf16[272,128]{1,0:T(8,128)(2,1)S(1)}, u32[]{:S(2)}, u32[]{:S(2)}) collective-permute-start(bf16[272,128]{1,0:T(8,128)(2,1)S(1)} %shard_map.74.refs_2_), channel_id=1, source_target_pairs={{0,3},{1,2},{2,1},{3,0},{4,7},{5,6},{6,5},{7,4},{8,11},{9,10},{10,... | collective-permute-start | bytes 208904 | tf_op jit(solution)/shard_map/ppermute | solution.py:108
  23.4 5.2 %collective-permute-start.12 = (bf16[272,128]{1,0:T(8,128)(2,1)S(1)}, bf16[272,128]{1,0:T(8,128)(2,1)S(1)}, u32[]{:S(2)}, u32[]{:S(2)}) collective-permute-start(bf16[272,128]{1,0:T(8,128)(2,1)S(1)} %shard_map.74.refs_2_), channel_id=1, source_target_pairs={{0,2},{1,3},{2,0},{3,1},{4,6},{5,7},{6,4},{7,5},{8,10},{9,11},{10,... | collective-permute-start | bytes 208904 | tf_op jit(solution)/shard_map/ppermute | solution.py:108
  24.5 4.1 %collective-permute-start.11 = (bf16[272,128]{1,0:T(8,128)(2,1)S(1)}, bf16[272,128]{1,0:T(8,128)(2,1)S(1)}, u32[]{:S(2)}, u32[]{:S(2)}) collective-permute-start(bf16[272,128]{1,0:T(8,128)(2,1)S(1)} %shard_map.74.refs_2_), channel_id=1, source_target_pairs={{0,1},{1,0},{2,3},{3,2},{4,5},{5,4},{6,7},{7,6},{8,9},{9,8},{10,11... | collective-permute-start | bytes 208904 | tf_op jit(solution)/shard_map/ppermute | solution.py:108
  25.3 6.8 %collective-permute-start.10 = (bf16[272,128]{1,0:T(8,128)(2,1)S(1)}, bf16[272,128]{1,0:T(8,128)(2,1)S(1)}, u32[]{:S(2)}, u32[]{:S(2)}) collective-permute-start(bf16[272,128]{1,0:T(8,128)(2,1)S(1)} %shard_map.73.refs_0_), channel_id=1, source_target_pairs={{0,16},{4,20},{8,24},{12,28},{16,0},{20,4},{24,8},{28,12},{1,17},{... | collective-permute-start | bytes 208904 | tf_op jit(solution)/shard_map/ppermute | solution.py:108
  32.2 4.3 %collective-permute-start.16 = (bf16[128,128]{1,0:T(8,128)(2,1)S(1)}, bf16[128,128]{1,0:T(8,128)(2,1)S(1)}, u32[]{:S(2)}, u32[]{:S(2)}) collective-permute-start(bf16[128,128]{1,0:T(8,128)(2,1)S(1)} %get-tuple-element.25.refs_0_), channel_id=1, source_target_pairs={{0,3},{1,2},{2,1},{3,0},{4,7},{5,6},{6,5},{7,4},{8,11},{9,10},{10,... | collective-permute-start | bytes 98312 | tf_op jit(solution)/shard_map/ppermute | solution.py:108
  32.3 4.3 %collective-permute-start.15 = (bf16[128,128]{1,0:T(8,128)(2,1)S(1)}, bf16[128,128]{1,0:T(8,128)(2,1)S(1)}, u32[]{:S(2)}, u32[]{:S(2)}) collective-permute-start(bf16[128,128]{1,0:T(8,128)(2,1)S(1)} %get-tuple-element.25.refs_0_), channel_id=1, source_target_pairs={{0,2},{1,3},{2,0},{3,1},{4,6},{5,7},{6,4},{7,5},{8,10},{9,11},{10,... | collective-permute-start | bytes 98312 | tf_op jit(solution)/shard_map/ppermute | solution.py:108
  36.7 5.2 %collective-permute-start.19 = (bf16[128,128]{1,0:T(8,128)(2,1)S(1)}, bf16[128,128]{1,0:T(8,128)(2,1)S(1)}, u32[]{:S(2)}, u32[]{:S(2)}) collective-permute-start(bf16[128,128]{1,0:T(8,128)(2,1)S(1)} %get-tuple-element.31.refs_0_), channel_id=1, source_target_pairs={{0,3},{1,2},{2,1},{3,0},{4,7},{5,6},{6,5},{7,4},{8,11},{9,10},{10,... | collective-permute-start | bytes 98312 | tf_op jit(solution)/shard_map/ppermute | solution.py:108
  37.4 4.6 %collective-permute-start.18 = (bf16[128,128]{1,0:T(8,128)(2,1)S(1)}, bf16[128,128]{1,0:T(8,128)(2,1)S(1)}, u32[]{:S(2)}, u32[]{:S(2)}) collective-permute-start(bf16[128,128]{1,0:T(8,128)(2,1)S(1)} %get-tuple-element.31.refs_0_), channel_id=1, source_target_pairs={{0,2},{1,3},{2,0},{3,1},{4,6},{5,7},{6,4},{7,5},{8,10},{9,11},{10,... | collective-permute-start | bytes 98312 | tf_op jit(solution)/shard_map/ppermute | solution.py:108
  42.1 4.7 %collective-permute-start.20 = (bf16[176,128]{1,0:T(8,128)(2,1)S(1)}, bf16[176,128]{1,0:T(8,128)(2,1)S(1)}, u32[]{:S(2)}, u32[]{:S(2)}) collective-permute-start(bf16[176,128]{1,0:T(8,128)(2,1)S(1)} %get-tuple-element.35), channel_id=1, source_target_pairs={{0,4},{4,0},{8,12},{12,8},{16,20},{20,16},{24,28},{28,24},{1,5},{5... | collective-permute-start | bytes 135176 | tf_op jit(solution)/shard_map/ppermute | solution.py:108
  43.7 4.1 %collective-permute-start.21 = (bf16[176,128]{1,0:T(8,128)(2,1)S(1)}, bf16[176,128]{1,0:T(8,128)(2,1)S(1)}, u32[]{:S(2)}, u32[]{:S(2)}) collective-permute-start(bf16[176,128]{1,0:T(8,128)(2,1)S(1)} %get-tuple-element.36), channel_id=1, source_target_pairs={{0,8},{4,12},{8,0},{12,4},{16,24},{20,28},{24,16},{28,20},{1,9},{5... | collective-permute-start | bytes 135176 | tf_op jit(solution)/shard_map/ppermute | solution.py:108
  44.2 4.9 %collective-permute-start.22 = (bf16[176,128]{1,0:T(8,128)(2,1)S(1)}, bf16[176,128]{1,0:T(8,128)(2,1)S(1)}, u32[]{:S(2)}, u32[]{:S(2)}) collective-permute-start(bf16[176,128]{1,0:T(8,128)(2,1)S(1)} %get-tuple-element.37), channel_id=1, source_target_pairs={{0,12},{4,8},{8,4},{12,0},{16,28},{20,24},{24,20},{28,16},{1,13},{... | collective-permute-start | bytes 135176 | tf_op jit(solution)/shard_map/ppermute | solution.py:108
  45.6 7.0 %collective-permute-start.26 = (bf16[272,128]{1,0:T(8,128)(2,1)S(1)}, bf16[272,128]{1,0:T(8,128)(2,1)S(1)}, u32[]{:S(2)}, u32[]{:S(2)}) collective-permute-start(bf16[272,128]{1,0:T(8,128)(2,1)S(1)} %get-tuple-element.40.refs_2_), channel_id=1, source_target_pairs={{0,3},{1,2},{2,1},{3,0},{4,7},{5,6},{6,5},{7,4},{8,11},{9,10},{10,... | collective-permute-start | bytes 208904 | tf_op jit(solution)/shard_map/ppermute | solution.py:108
  45.7 7.0 %collective-permute-start.25 = (bf16[272,128]{1,0:T(8,128)(2,1)S(1)}, bf16[272,128]{1,0:T(8,128)(2,1)S(1)}, u32[]{:S(2)}, u32[]{:S(2)}) collective-permute-start(bf16[272,128]{1,0:T(8,128)(2,1)S(1)} %get-tuple-element.40.refs_2_), channel_id=1, source_target_pairs={{0,2},{1,3},{2,0},{3,1},{4,6},{5,7},{6,4},{7,5},{8,10},{9,11},{10,... | collective-permute-start | bytes 208904 | tf_op jit(solution)/shard_map/ppermute | solution.py:108
  46.8 5.8 %collective-permute-start.24 = (bf16[272,128]{1,0:T(8,128)(2,1)S(1)}, bf16[272,128]{1,0:T(8,128)(2,1)S(1)}, u32[]{:S(2)}, u32[]{:S(2)}) collective-permute-start(bf16[272,128]{1,0:T(8,128)(2,1)S(1)} %get-tuple-element.40.refs_2_), channel_id=1, source_target_pairs={{0,1},{1,0},{2,3},{3,2},{4,5},{5,4},{6,7},{7,6},{8,9},{9,8},{10,11... | collective-permute-start | bytes 208904 | tf_op jit(solution)/shard_map/ppermute | solution.py:108
  49.2 5.4 %collective-permute-start.23 = (bf16[160,128]{1,0:T(8,128)(2,1)S(1)}, bf16[160,128]{1,0:T(8,128)(2,1)S(1)}, u32[]{:S(2)}, u32[]{:S(2)}) collective-permute-start(bf16[160,128]{1,0:T(8,128)(2,1)S(1)} %get-tuple-element.39), channel_id=1, source_target_pairs={{0,16},{4,20},{8,24},{12,28},{16,0},{20,4},{24,8},{28,12},{1,17},{... | collective-permute-start | bytes 122888 | tf_op jit(solution)/shard_map/ppermute | solution.py:108
  (5 other events, 22.2 us)

commit v4 on v3

--- a/solution.py
+++ b/solution.py
@@ -92,10 +92,10 @@
     return tree([get_norm(r, start) for r in refs])
 
 
-def digits(n):
+def digits(n, most=4):
     weight = 1
     while weight < n:
-        radix = 4 if (n // weight) % 4 == 0 else 2
+        radix = 4 if most == 4 and (n // weight) % 4 == 0 else 2
         yield weight, radix
         weight *= radix
 
@@ -106,6 +106,10 @@
 
 def swap(x, axis, weight, q):
     return lax.ppermute(x, axis, [(i, i ^ (q * weight)) for i in range(lax.axis_size(axis))])
+
+
+def turns(radix):
+    return [0] + list(range(radix - 1, 0, -1))
 
 
 def twice(c16):
@@ -119,12 +123,12 @@
     *ins, out = refs
     rows = ins[0].shape[0]
     digit = digit_of(axis, weight, len(ins))
-    for q, ref in enumerate(ins):
+    for q, ref in zip(turns(len(ins)), ins):
         out[pl.ds(pl.multiple_of((digit ^ q) * rows, rows), rows)] = ref[...]
 
 
 def gather_digit(x, own, axis, weight, radix):
-    got = [swap(x, axis, weight, q) for q in range(1, radix)]
+    got = [swap(x, axis, weight, q) for q in turns(radix)[1:]]
     (x,) = call(
         functools.partial(place_kernel, axis, weight),
         [((x.shape[0] * radix, x.shape[1]), x.dtype)],
@@ -163,9 +167,10 @@
         put_norm(out, norm_at, sum_norm(ins, norm_at))
 
 
-def sum_parts(x, axis, norm_at=None):
+def sum_parts(x, axis, norm_at=None, most=4, high_first=False):
     parts = [x]
-    for weight, radix in digits(lax.axis_size(axis)):
+    order = list(digits(lax.axis_size(axis), most))
+    for weight, radix in reversed(order) if high_first else order:
         if len(parts) > 1:
             (x,) = call(functools.partial(add_kernel, norm_at), [(x.shape, BF16)], *parts)
         parts = [x] + [swap(x, axis, weight, q) for q in range(1, radix)]
@@ -291,85 +296,92 @@
     out_ref[...] = (sum_ref[...] - dot_wide(c2.astype(BF16), gram_ref[...])).astype(BF16)
 
 
-def second_ab_kernel(t_ref, a_ref, b_ref, c_ref, col_ref, grad_b, acc_a):
-    rows_i = a_ref.shape[0]
+def second_b_kernel(t_ref, a_ref, b_ref, c_ref, grad_b):
     a16 = a_ref[...].astype(BF16)
+    c16 = c_ref[...].astype(BF16)
+    sum_b(t_ref, a_ref, c16, grad_b)
+    grad_b[...] -= dot_wide(b_ref[...].astype(BF16), gram(a16) * gram(c16))
+
+
+def second_a_kernel(weight, own_i, t_ref, a_ref, b_ref, c_ref, *refs):
+    *outs, acc_a = refs
     b16 = b_ref[...].astype(BF16)
     c16 = c_ref[...].astype(BF16)
-    sum_a(t_ref, a_ref, b16, c16, acc_a, grad_b)
-    gram_c = gram(c16)
-    col_ref[:rows_i] = (acc_a[...] - dot_wide(a16, gram(b16) * gram_c)).astype(BF16)
-    put_norm(col_ref, rows_i, squares(b16))
-    grad_b[...] -= dot_wide(b16, gram(a16) * gram_c)
-
-
-def put_shares(weight, own_j, shared, norm, grad_b, outs):
+    sum_a(t_ref, a_ref, b16, c16, acc_a)
+    acc_a[...] -= dot_wide(a_ref[...].astype(BF16), gram(b16) * gram(c16))
+    put_shares("col", weight, own_i, None, squares(b16), acc_a, outs)
+
+
+def put_shares(axis, weight, own, shared, norm, grad, outs):
     radix = len(outs)
-    depth = shared.shape[0]
-    blocks = grad_b.shape[0] // own_j
-    digit = digit_of("row", weight, radix)
-    for q, out in enumerate(outs):
-        out[:depth] = shared
+    depth = 0 if shared is None else shared.shape[0]
+    blocks = grad.shape[0] // own
+    digit = digit_of(axis, weight, radix)
+    for q, out in zip(turns(radix), outs):
+        if depth:
+            out[:depth] = shared
         put_norm(out, depth, norm)
-        first = [(high * radix + (digit ^ q)) * own_j for high in range(blocks // radix)]
-        rows = [grad_b[pl.ds(pl.multiple_of(at, own_j), own_j)] for at in first]
+        first = [(high * radix + (digit ^ q)) * own for high in range(blocks // radix)]
+        rows = [grad[pl.ds(pl.multiple_of(at, own), own)] for at in first]
         out[depth + NORM_ROWS :] = jnp.concatenate(rows, 0).astype(BF16)
 
 
-def shares_kernel(n_col, own_j, radix, *refs):
+def shares_kernel(n_col, own_j, weight, *refs):
     parts, refs = refs[:n_col], refs[n_col:]
     a_ref, grad_b, outs = refs[0], refs[1], refs[2:]
     shared = sum_rows(parts, 0, parts[0].shape[0]).astype(BF16)
-    put_shares(1, own_j, shared, squares(a_ref[...].astype(BF16)), grad_b, outs)
-
-
-def next_shares_kernel(n_row, weight, own_j, depth, *refs):
-    parts, outs, grad_b = refs[:n_row], refs[n_row:-1], refs[-1]
-    shared = sum_rows(parts, 0, depth).astype(BF16)
-    grad_b[...] = sum_rows(parts, depth + NORM_ROWS, grad_b.shape[0])
-    put_shares(weight, own_j, shared, sum_norm(parts, depth), grad_b, outs)
-
-
-def sum_shares(col_parts, a, grad_b, own_j):
-    depth, rank = col_parts[0].shape
-    stages = list(digits(lax.axis_size("row")))
-    held = grad_b.shape[0]
+    put_shares("row", weight, own_j, shared, squares(a_ref[...].astype(BF16)), grad_b, outs)
+
+
+def next_shares_kernel(axis, weight, own, depth, n_parts, *refs):
+    parts, outs, grad = refs[:n_parts], refs[n_parts:-1], refs[-1]
+    shared = sum_rows(parts, 0, depth).astype(BF16) if depth else None
+    grad[...] = sum_rows(parts, depth + NORM_ROWS, grad.shape[0])
+    put_shares(axis, weight, own, shared, sum_norm(parts, depth), grad, outs)
+
+
+def first_digit(axis):
+    return next(digits(lax.axis_size(axis)))
+
+
+def messages(depth, rows, rank, radix):
+    return [((depth + NORM_ROWS + rows // radix, rank), BF16)] * radix
+
+
+def sum_shares(sent, axis, own, depth, beside=None):
+    rank = sent[0].shape[1]
     parts = None
-    for weight, radix in stages:
-        shape = (depth + NORM_ROWS + held // radix, rank)
-        outs = [(shape, BF16)] * radix
-        if parts is None:
+    for weight, radix in digits(lax.axis_size(axis)):
+        if parts is not None:
+            held = parts[0].shape[0] - depth - NORM_ROWS
             sent = call(
-                functools.partial(shares_kernel, len(col_parts), own_j, radix),
-                outs, *col_parts, a, grad_b,
-            )
-        else:
-            sent = call(
-                functools.partial(next_shares_kernel, len(parts), weight, own_j, depth),
-                outs, *parts,
+                functools.partial(next_shares_kernel, axis, weight, own, depth, len(parts)),
+                messages(depth, held, rank, radix),
+                *parts,
                 scratch=[pltpu.VMEM((held, rank), F32)],
             )
-        held //= radix
-        parts = [sent[0]] + [swap(sent[q], "row", weight, q) for q in range(1, radix)]
-    return parts
+            if beside is not None:
+                sent, beside = lax.optimization_barrier((sent, beside))
+        got = [swap(x, axis, weight, q) for q, x in zip(turns(radix)[1:], sent[1:])]
+        parts = [sent[0]] + got
+    return parts if beside is None else (parts, beside)
 
 
 def last_kernel(n_row, n_col, *refs):
     rows, refs = refs[:n_row], refs[n_row:]
     cols, refs = refs[:n_col], refs[n_col:]
-    a_ref, b_ref, c_ref, out_a, out_b, out_c, grad_a = refs
-    rows_i, depth = a_ref.shape[0], c_ref.shape[0]
+    a_ref, b_ref, c_ref, out_a, out_b, out_c = refs
+    depth = c_ref.shape[0]
     own_i, own_j = out_a.shape[0], out_b.shape[0]
     norm_a = sum_norm(rows, depth)
-    norm_b = sum_norm(cols, rows_i)
+    norm_b = sum_norm(cols, 0)
     norm_c = squares(c_ref[...].astype(BF16))
     step_a = scaling / (norm_b * norm_c + epsilon)
     step_b = scaling / (norm_a * norm_c + epsilon)
     step_c = scaling / (norm_a * norm_b + epsilon)
-    grad_a[...] = sum_rows(cols, 0, rows_i)
     at_i = pl.ds(pl.multiple_of(lax.axis_index("col") * own_i, own_i), own_i)
     at_j = pl.ds(pl.multiple_of(lax.axis_index("row") * own_j, own_j), own_j)
-    out_a[...] = damping * a_ref[at_i] + step_a * grad_a[at_i]
+    out_a[...] = damping * a_ref[at_i] + step_a * sum_rows(cols, NORM_ROWS, own_i)
     out_b[...] = damping * b_ref[at_j] + step_b * sum_rows(rows, depth + NORM_ROWS, own_j)
     out_c[...] = damping * c_ref[...] + step_c * sum_rows(rows, 0, depth)
 
@@ -377,7 +389,6 @@
 def local(tensor, factor_a, factor_b, factor_c):
     rows_i, rows_j, depth = tensor.shape
     rank = factor_a.shape[1]
-    own_j = factor_b.shape[0]
     held_a, held_b, c = hold(factor_a, factor_b, factor_c)
     b = gather(factor_b, held_b, "row")
     a = gather(factor_a, held_a, "col")
@@ -399,7 +410,7 @@
         scratch=[pltpu.VMEM(a.shape, F32)],
         flops=2 * tensor.size * rank,
     )
-    rows = sum_parts(to_row, "row", rows_j + depth)
+    rows = sum_parts(to_row, "row", rows_j + depth, high_first=True)
     cols = sum_parts(to_col, "col", rows_i)
     a, b, part_c, step_c = call(
         functools.partial(middle_kernel, len(rows), len(cols)),
@@ -420,20 +431,29 @@
         *parts, step_c, c, sum_t, gram_ab,
     )
     parts = sum_parts(to_col, "col")
-    to_col, grad_b = call(
-        second_ab_kernel,
-        [((rows_i + NORM_ROWS, rank), BF16), ((rows_j, rank), F32)],
+    (grad_b,) = call(
+        second_b_kernel, [(b.shape, F32)], tensor, a, b, c, flops=2 * tensor.size * rank
+    )
+    weight, radix = first_digit("row")
+    to_row = call(
+        functools.partial(shares_kernel, len(parts), factor_b.shape[0], weight),
+        messages(depth, rows_j, rank, radix),
+        *parts, a, grad_b,
+    )
+    weight, radix = first_digit("col")
+    to_col = call(
+        functools.partial(second_a_kernel, weight, factor_a.shape[0]),
+        messages(0, rows_i, rank, radix),
         tensor, a, b, c,
         scratch=[pltpu.VMEM((rows_i, rank), F32)],
         flops=2 * tensor.size * rank,
     )
-    rows = sum_shares(parts, a, grad_b, own_j)
-    cols = sum_parts(to_col, "col", rows_i)
+    rows, to_col = sum_shares(to_row, "row", factor_b.shape[0], depth, to_col)
+    cols = sum_shares(to_col, "col", factor_a.shape[0], 0)
     return call(
         functools.partial(last_kernel, len(rows), len(cols)),
         [(factor_a.shape, F32), (factor_b.shape, F32), (c.shape, F32)],
         *rows, *cols, a, b, c,
-        scratch=[pltpu.VMEM((rows_i, rank), F32)],
         hbm_out=True,
     )
 

time: 55.5 us -> 53.6 us (0.966)
  starting transfers between devices: 30.3 us -> 27.9 us
  Pallas kernels: 15.3 us -> 17.3 us
  waiting for transfers between devices: 8.95 us -> 7.42 us
    ppermute x27, starting transfers between devices: 30.3 us -> 27.9 us  [swap(): lax.ppermute(x, axis, [(i, i ^ q * weight) for i in range(lax.axis_size(a...]
    pallas_call x14 -> x15, Pallas kernels: 14.4 us -> 16.4 us  [call(): pl.pallas_call(body, in_specs=[whole] * len(operands), out_specs=[whole]...]
    ppermute x27, waiting for transfers between devices: 8.95 us -> 7.42 us  [swap(): lax.ppermute(x, axis, [(i, i ^ q * weight) for i in range(lax.axis_size(a...]
  transfers between devices with their start and end apart: 27 -> 27, of which waited for: 8 -> 11; matrix products, arithmetic and copies ran while one was open for 0% -> 0% of each run, Pallas kernels for 21% -> 26%
where the time goes in v4:
time: 53.6 us; the launch traced here: 53.4 us
  starting transfers between devices  27.9 us (52%)
  Pallas kernels  17.3 us (32%)
  waiting for transfers between devices  7.42 us (14%)
  between operations  0.81 us (2%)
    ppermute x27, starting transfers between devices, swap(): lax.ppermute(x, axis, [(i, i ^ q * weight) for i in range(lax.axis_size(a...  27.9 us
    pallas_call x15, Pallas kernels, call(): pl.pallas_call(body, in_specs=[whole] * len(operands), out_specs=[whole]...  16.4 us
    ppermute x27, waiting for transfers between devices, swap(): lax.ppermute(x, axis, [(i, i ^ q * weight) for i in range(lax.axis_size(a...  7.42 us
  transfers between devices with their start and end apart: 27, of which 11 were waited for; matrix products, arithmetic and copies ran while one was open for 0% of the time, Pallas kernels for 26%

profile of v4, /device:TPU:0, one launch (start us, length us, event | category | flops | bytes accessed | tf_op | source)
XLA Modules:
  0.0 53.4 jit_solution(1174693488913485139)
XLA Ops:
  0.6 4.0 %collective-permute-start.3 = (f32[16,128]{1,0:T(8,128)}, f32[16,128]{1,0:T(8,128)S(1)}, u32[]{:S(2)}, u32[]{:S(2)}) collective-permute-start(f32[16,128]{1,0:T(8,128)} %refs_1_.1), channel_id=1, source_target_pairs={{0,12},{4,8},{8,4},{12,0},{16,28},{20,24},{24,20},{28,16},{1,13},{... | collective-permute-start | bytes 24584 | tf_op jit(solution)/shard_map/ppermute | solution.py:108
  5.8 1.5 %collective-permute-start.2 = (f32[64,128]{1,0:T(8,128)}, f32[64,128]{1,0:T(8,128)S(1)}, u32[]{:S(2)}, u32[]{:S(2)}) collective-permute-start(f32[64,128]{1,0:T(8,128)} %refs_0_.1), channel_id=1, source_target_pairs={{0,1},{1,0},{2,3},{3,2},{4,5},{5,4},{6,7},{7,6},{8,9},{9,8},{10,11... | collective-permute-start | bytes 98312 | tf_op jit(solution)/shard_map/ppermute | solution.py:108
  7.3 0.9 %shard_map.67 = (f32[64,128]{1,0:T(8,128)S(1)}, f32[16,128]{1,0:T(8,128)S(1)}, f32[128,128]{1,0:T(8,128)S(1)}) custom-call(f32[64,128]{1,0:T(8,128)} %refs_0_.1, f32[16,128]{1,0:T(8,128)} %refs_1_.1, f32[128,128]{1,0:T(8,128)} %refs_2_.1), custom_call_target="tpu_custom_call" | custom-call | flops 5000000000 | tf_op jit(solution)/shard_map/pallas_call | solution.py:155
  9.1 2.6 %collective-permute-start.6 = (f32[64,128]{1,0:T(8,128)S(1)}, f32[64,128]{1,0:T(8,128)S(1)}, u32[]{:S(2)}, u32[]{:S(2)}) collective-permute-start(f32[64,128]{1,0:T(8,128)S(1)} %shard_map.69.refs_0_), channel_id=1, source_target_pairs={{0,16},{4,20},{8,24},{12,28},{16,0},{20,4},{24,8},{28,12},{1,17},{... | collective-permute-start | bytes 98312 | tf_op jit(solution)/shard_map/ppermute | solution.py:108
  12.2 2.3 %shard_map.71.acc_b = f32[128,128]{1,0:T(8,128)S(1)} custom-call(bf16[256,128,128]{2,1,0:T(8,128)(2,1)S(1)} %copy-done, f32[256,128]{1,0:T(8,128)S(1)} %shard_map.68.a_ref.refs_8_, f32[128,128]{1,0:T(8,128)S(1)} %get-tuple-element.32.c_ref.refs_10_.refs_5_), custom_call_target="tpu_custom_call" | custom-call | flops 1073741824 | tf_op jit(solution)/shard_map/pallas_call | solution.py:30
  14.6 2.6 %shard_map.72.refs_0_ = bf16[272,128]{1,0:T(8,128)(2,1)S(1)} custom-call(bf16[256,128,128]{2,1,0:T(8,128)(2,1)S(1)} %copy-done, f32[256,128]{1,0:T(8,128)S(1)} %shard_map.68.a_ref.refs_8_, f32[128,128]{1,0:T(8,128)S(1)} %shard_map.70.b_ref.refs_9_, f32[128,128]{1,0:T(8,128)S(1)} %get-tuple-element.32.c_ref.refs_10_.refs_5_, f32[128,128]{1,0:T(8,128)S(1)} %shard_map.71.acc_b), custom_call_target="tpu_custom_call" | custom-call | flops 1073741824 | tf_op jit(solution)/shard_map/pallas_call | solution.py:30
  17.2 2.7 %collective-permute-start.7 = (bf16[272,128]{1,0:T(8,128)(2,1)S(1)}, bf16[272,128]{1,0:T(8,128)(2,1)S(1)}, u32[]{:S(2)}, u32[]{:S(2)}) collective-permute-start(bf16[272,128]{1,0:T(8,128)(2,1)S(1)} %shard_map.72.refs_0_), channel_id=1, source_target_pairs={{0,16},{4,20},{8,24},{12,28},{16,0},{20,4},{24,8},{28,12},{1,17},{... | collective-permute-start | bytes 208904 | tf_op jit(solution)/shard_map/ppermute | solution.py:108
  19.8 2.6 %shard_map.74.refs_4_ = bf16[272,128]{1,0:T(8,128)(2,1)S(1)} custom-call(bf16[256,128,128]{2,1,0:T(8,128)(2,1)S(1)} %copy-done, f32[256,128]{1,0:T(8,128)S(1)} %shard_map.68.a_ref.refs_8_, f32[128,128]{1,0:T(8,128)S(1)} %shard_map.70.b_ref.refs_9_, f32[128,128]{1,0:T(8,128)S(1)} %get-tuple-element.32.c_ref.refs_10_.refs_5_), custom_call_target="tpu_custom_call" | custom-call | flops 1073741824 | tf_op jit(solution)/shard_map/pallas_call | solution.py:30
  22.5 1.0 %collective-permute-start.12 = (bf16[272,128]{1,0:T(8,128)(2,1)S(1)}, bf16[272,128]{1,0:T(8,128)(2,1)S(1)}, u32[]{:S(2)}, u32[]{:S(2)}) collective-permute-start(bf16[272,128]{1,0:T(8,128)(2,1)S(1)} %shard_map.74.refs_4_), channel_id=1, source_target_pairs={{0,2},{1,3},{2,0},{3,1},{4,6},{5,7},{6,4},{7,5},{8,10},{9,11},{10,... | collective-permute-start | bytes 208904 | tf_op jit(solution)/shard_map/ppermute | solution.py:108
  23.5 0.9 %collective-permute-start.11 = (bf16[272,128]{1,0:T(8,128)(2,1)S(1)}, bf16[272,128]{1,0:T(8,128)(2,1)S(1)}, u32[]{:S(2)}, u32[]{:S(2)}) collective-permute-start(bf16[272,128]{1,0:T(8,128)(2,1)S(1)} %shard_map.74.refs_4_), channel_id=1, source_target_pairs={{0,1},{1,0},{2,3},{3,2},{4,5},{5,4},{6,7},{7,6},{8,9},{9,8},{10,11... | collective-permute-start | bytes 208904 | tf_op jit(solution)/shard_map/ppermute | solution.py:108
  24.4 2.6 %collective-permute-start.10 = (bf16[272,128]{1,0:T(8,128)(2,1)S(1)}, bf16[272,128]{1,0:T(8,128)(2,1)S(1)}, u32[]{:S(2)}, u32[]{:S(2)}) collective-permute-start(bf16[272,128]{1,0:T(8,128)(2,1)S(1)} %shard_map.73.refs_0_), channel_id=1, source_target_pairs={{0,12},{4,8},{8,4},{12,0},{16,28},{20,24},{24,20},{28,16},{1,13},{... | collective-permute-start | bytes 208904 | tf_op jit(solution)/shard_map/ppermute | solution.py:108
  27.4 0.9 %collective-permute-start.8 = (bf16[272,128]{1,0:T(8,128)(2,1)S(1)}, bf16[272,128]{1,0:T(8,128)(2,1)S(1)}, u32[]{:S(2)}, u32[]{:S(2)}) collective-permute-start(bf16[272,128]{1,0:T(8,128)(2,1)S(1)} %shard_map.73.refs_0_), channel_id=1, source_target_pairs={{0,4},{4,0},{8,12},{12,8},{16,20},{20,16},{24,28},{28,24},{1,5},{5... | collective-permute-start | bytes 208904 | tf_op jit(solution)/shard_map/ppermute | solution.py:108
  28.3 1.8 %collective-permute-done.10.refs_3_ = bf16[272,128]{1,0:T(8,128)(2,1)S(1)} collective-permute-done((bf16[272,128]{1,0:T(8,128)(2,1)S(1)}, bf16[272,128]{1,0:T(8,128)(2,1)S(1)}, u32[]{:S(2)}, u32[]{:S(2)}) %collective-permute-start.10) | collective-permute-done | bytes 69664 | tf_op jit(solution)/shard_map/ppermute | solution.py:108
  30.1 1.2 %collective-permute-done.9.refs_2_ = bf16[272,128]{1,0:T(8,128)(2,1)S(1)} collective-permute-done((bf16[272,128]{1,0:T(8,128)(2,1)S(1)}, bf16[272,128]{1,0:T(8,128)(2,1)S(1)}, u32[]{:S(2)}, u32[]{:S(2)}) %collective-permute-start.9) | collective-permute-done | bytes 69664 | tf_op jit(solution)/shard_map/ppermute | solution.py:108
  31.9 1.0 %collective-permute-start.15 = (bf16[128,128]{1,0:T(8,128)(2,1)S(1)}, bf16[128,128]{1,0:T(8,128)(2,1)S(1)}, u32[]{:S(2)}, u32[]{:S(2)}) collective-permute-start(bf16[128,128]{1,0:T(8,128)(2,1)S(1)} %get-tuple-element.33.refs_0_), channel_id=1, source_target_pairs={{0,2},{1,3},{2,0},{3,1},{4,6},{5,7},{6,4},{7,5},{8,10},{9,11},{10,... | collective-permute-start | bytes 98312 | tf_op jit(solution)/shard_map/ppermute | solution.py:108
  32.9 0.9 %collective-permute-start.14 = (bf16[128,128]{1,0:T(8,128)(2,1)S(1)}, bf16[128,128]{1,0:T(8,128)(2,1)S(1)}, u32[]{:S(2)}, u32[]{:S(2)}) collective-permute-start(bf16[128,128]{1,0:T(8,128)(2,1)S(1)} %get-tuple-element.33.refs_0_), channel_id=1, source_target_pairs={{0,1},{1,0},{2,3},{3,2},{4,5},{5,4},{6,7},{7,6},{8,9},{9,8},{10,11... | collective-permute-start | bytes 98312 | tf_op jit(solution)/shard_map/ppermute | solution.py:108
  33.8 2.4 %shard_map.76 = (f32[128,128]{1,0:T(8,128)S(1)}, f32[128,128]{1,0:T(8,128)S(1)}) custom-call(bf16[256,128,128]{2,1,0:T(8,128)(2,1)S(1)} %copy-done, f32[256,128]{1,0:T(8,128)S(1)} %get-tuple-element.35.a_ref.refs_4_.refs_6_, f32[128,128]{1,0:T(8,128)S(1)} %get-tuple-element.36.b_ref.refs_7_), custom_call_target="tpu_custom_call" | custom-call | flops 1073741824 | tf_op jit(solution)/shard_map/pallas_call | solution.py:30
  37.0 1.2 %collective-permute-start.18 = (bf16[128,128]{1,0:T(8,128)(2,1)S(1)}, bf16[128,128]{1,0:T(8,128)(2,1)S(1)}, u32[]{:S(2)}, u32[]{:S(2)}) collective-permute-start(bf16[128,128]{1,0:T(8,128)(2,1)S(1)} %get-tuple-element.39.refs_0_), channel_id=1, source_target_pairs={{0,2},{1,3},{2,0},{3,1},{4,6},{5,7},{6,4},{7,5},{8,10},{9,11},{10,... | collective-permute-start | bytes 98312 | tf_op jit(solution)/shard_map/ppermute | solution.py:108
  38.4 2.7 %shard_map.78.refs_5_ = f32[128,128]{1,0:T(8,128)S(1)} custom-call(bf16[256,128,128]{2,1,0:T(8,128)(2,1)S(1)} %copy-done, f32[256,128]{1,0:T(8,128)S(1)} %get-tuple-element.35.a_ref.refs_4_.refs_6_, f32[128,128]{1,0:T(8,128)S(1)} %get-tuple-element.36.b_ref.refs_7_, f32[128,128]{1,0:T(8,128)S(1)} %get-tuple-element.40.c_ref.refs_8_), custom_call_target="tpu_custom_call" | custom-call | flops 1073741824 | tf_op jit(solution)/shard_map/pallas_call | solution.py:30
  41.2 2.1 %collective-permute-start.20 = (bf16[176,128]{1,0:T(8,128)(2,1)S(1)}, bf16[176,128]{1,0:T(8,128)(2,1)S(1)}, u32[]{:S(2)}, u32[]{:S(2)}) collective-permute-start(bf16[176,128]{1,0:T(8,128)(2,1)S(1)} %get-tuple-element.42), channel_id=1, source_target_pairs={{0,12},{4,8},{8,4},{12,0},{16,28},{20,24},{24,20},{28,16},{1,13},{... | collective-permute-start | bytes 135176 | tf_op jit(solution)/shard_map/ppermute | solution.py:108
  43.7 1.1 %collective-permute-start.22 = (bf16[176,128]{1,0:T(8,128)(2,1)S(1)}, bf16[176,128]{1,0:T(8,128)(2,1)S(1)}, u32[]{:S(2)}, u32[]{:S(2)}) collective-permute-start(bf16[176,128]{1,0:T(8,128)(2,1)S(1)} %get-tuple-element.44), channel_id=1, source_target_pairs={{0,4},{4,0},{8,12},{12,8},{16,20},{20,16},{24,28},{28,24},{1,5},{5... | collective-permute-start | bytes 135176 | tf_op jit(solution)/shard_map/ppermute | solution.py:108
  44.8 2.6 %shard_map.81 = (bf16[80,128]{1,0:T(8,128)(2,1)S(1)}, bf16[80,128]{1,0:T(8,128)(2,1)S(1)}, bf16[80,128]{1,0:T(8,128)(2,1)S(1)}, bf16[80,128]{1,0:T(8,128)(2,1)S(1)}) custom-call(bf16[256,128,128]{2,1,0:T(8,128)(2,1)S(1)} %copy-done, f32[256,128]{1,0:T(8,128)S(1)} %get-tuple-element.35.a_ref.refs_4_.refs_6_, f32[128,128]{1,0:T(8,128)S(1)} %get-tuple-element.36.b_ref.refs_7_, ...), custom_call_target="tpu_custom_call" | custom-call | flops 1073741824 | tf_op jit(solution)/shard_map/pallas_call | solution.py:30
  48.4 1.1 %collective-permute-start.25 = (bf16[80,128]{1,0:T(8,128)(2,1)S(1)}, bf16[80,128]{1,0:T(8,128)(2,1)S(1)}, u32[]{:S(2)}, u32[]{:S(2)}) collective-permute-start(bf16[80,128]{1,0:T(8,128)(2,1)S(1)} %get-tuple-element.55), channel_id=1, source_target_pairs={{0,2},{1,3},{2,0},{3,1},{4,6},{5,7},{6,4},{7,5},{8,10},{9,11},{10,... | collective-permute-start | bytes 61448 | tf_op jit(solution)/shard_map/ppermute | solution.py:108
  50.3 1.3 %collective-permute-done.24.refs_3_ = bf16[80,128]{1,0:T(8,128)(2,1)S(1)} collective-permute-done((bf16[80,128]{1,0:T(8,128)(2,1)S(1)}, bf16[80,128]{1,0:T(8,128)(2,1)S(1)}, u32[]{:S(2)}, u32[]{:S(2)}) %collective-permute-start.24) | collective-permute-done | bytes 20512 | tf_op jit(solution)/shard_map/ppermute | solution.py:108
  (50 shorter events, 8.7 us)
Async XLA Ops:
  0.6 7.5 %collective-permute-start.3 = (f32[16,128]{1,0:T(8,128)}, f32[16,128]{1,0:T(8,128)S(1)}, u32[]{:S(2)}, u32[]{:S(2)}) collective-permute-start(f32[16,128]{1,0:T(8,128)} %refs_1_.1), channel_id=1, source_target_pairs={{0,12},{4,8},{8,4},{12,0},{16,28},{20,24},{24,20},{28,16},{1,13},{... | collective-permute-start | bytes 24584 | tf_op jit(solution)/shard_map/ppermute | solution.py:108
  4.7 3.9 %collective-permute-start.5 = (f32[16,128]{1,0:T(8,128)}, f32[16,128]{1,0:T(8,128)S(1)}, u32[]{:S(2)}, u32[]{:S(2)}) collective-permute-start(f32[16,128]{1,0:T(8,128)} %refs_1_.1), channel_id=1, source_target_pairs={{0,4},{4,0},{8,12},{12,8},{16,20},{20,16},{24,28},{28,24},{1,5},{5... | collective-permute-start | bytes 24584 | tf_op jit(solution)/shard_map/ppermute | solution.py:108
  5.2 3.9 %collective-permute-start.4 = (f32[16,128]{1,0:T(8,128)}, f32[16,128]{1,0:T(8,128)S(1)}, u32[]{:S(2)}, u32[]{:S(2)}) collective-permute-start(f32[16,128]{1,0:T(8,128)} %refs_1_.1), channel_id=1, source_target_pairs={{0,8},{4,12},{8,0},{12,4},{16,24},{20,28},{24,16},{28,20},{1,9},{5... | collective-permute-start | bytes 24584 | tf_op jit(solution)/shard_map/ppermute | solution.py:108
  5.3 6.4 %collective-permute-start = (f32[64,128]{1,0:T(8,128)}, f32[64,128]{1,0:T(8,128)S(1)}, u32[]{:S(2)}, u32[]{:S(2)}) collective-permute-start(f32[64,128]{1,0:T(8,128)} %refs_0_.1), channel_id=1, source_target_pairs={{0,3},{1,2},{2,1},{3,0},{4,7},{5,6},{6,5},{7,4},{8,11},{9,10},{10,... | collective-permute-start | bytes 98312 | tf_op jit(solution)/shard_map/ppermute | solution.py:108
  5.8 5.9 %collective-permute-start.2 = (f32[64,128]{1,0:T(8,128)}, f32[64,128]{1,0:T(8,128)S(1)}, u32[]{:S(2)}, u32[]{:S(2)}) collective-permute-start(f32[64,128]{1,0:T(8,128)} %refs_0_.1), channel_id=1, source_target_pairs={{0,1},{1,0},{2,3},{3,2},{4,5},{5,4},{6,7},{7,6},{8,9},{9,8},{10,11... | collective-permute-start | bytes 98312 | tf_op jit(solution)/shard_map/ppermute | solution.py:108
  8.2 4.0 %collective-permute-start.1 = (f32[64,128]{1,0:T(8,128)S(1)}, f32[64,128]{1,0:T(8,128)S(1)}, u32[]{:S(2)}, u32[]{:S(2)}) collective-permute-start(f32[64,128]{1,0:T(8,128)S(1)} %copy-done.1), channel_id=1, source_target_pairs={{0,2},{1,3},{2,0},{3,1},{4,6},{5,7},{6,4},{7,5},{8,10},{9,11},{10,... | collective-permute-start | bytes 98312 | tf_op jit(solution)/shard_map/ppermute | solution.py:108
  9.1 5.5 %collective-permute-start.6 = (f32[64,128]{1,0:T(8,128)S(1)}, f32[64,128]{1,0:T(8,128)S(1)}, u32[]{:S(2)}, u32[]{:S(2)}) collective-permute-start(f32[64,128]{1,0:T(8,128)S(1)} %shard_map.69.refs_0_), channel_id=1, source_target_pairs={{0,16},{4,20},{8,24},{12,28},{16,0},{20,4},{24,8},{28,12},{1,17},{... | collective-permute-start | bytes 98312 | tf_op jit(solution)/shard_map/ppermute | solution.py:108
  17.2 7.2 %collective-permute-start.7 = (bf16[272,128]{1,0:T(8,128)(2,1)S(1)}, bf16[272,128]{1,0:T(8,128)(2,1)S(1)}, u32[]{:S(2)}, u32[]{:S(2)}) collective-permute-start(bf16[272,128]{1,0:T(8,128)(2,1)S(1)} %shard_map.72.refs_0_), channel_id=1, source_target_pairs={{0,16},{4,20},{8,24},{12,28},{16,0},{20,4},{24,8},{28,12},{1,17},{... | collective-permute-start | bytes 208904 | tf_op jit(solution)/shard_map/ppermute | solution.py:108
  22.4 5.0 %collective-permute-start.13 = (bf16[272,128]{1,0:T(8,128)(2,1)S(1)}, bf16[272,128]{1,0:T(8,128)(2,1)S(1)}, u32[]{:S(2)}, u32[]{:S(2)}) collective-permute-start(bf16[272,128]{1,0:T(8,128)(2,1)S(1)} %shard_map.74.refs_4_), channel_id=1, source_target_pairs={{0,3},{1,2},{2,1},{3,0},{4,7},{5,6},{6,5},{7,4},{8,11},{9,10},{10,... | collective-permute-start | bytes 208904 | tf_op jit(solution)/shard_map/ppermute | solution.py:108
  22.5 5.8 %collective-permute-start.12 = (bf16[272,128]{1,0:T(8,128)(2,1)S(1)}, bf16[272,128]{1,0:T(8,128)(2,1)S(1)}, u32[]{:S(2)}, u32[]{:S(2)}) collective-permute-start(bf16[272,128]{1,0:T(8,128)(2,1)S(1)} %shard_map.74.refs_4_), channel_id=1, source_target_pairs={{0,2},{1,3},{2,0},{3,1},{4,6},{5,7},{6,4},{7,5},{8,10},{9,11},{10,... | collective-permute-start | bytes 208904 | tf_op jit(solution)/shard_map/ppermute | solution.py:108
  23.5 4.8 %collective-permute-start.11 = (bf16[272,128]{1,0:T(8,128)(2,1)S(1)}, bf16[272,128]{1,0:T(8,128)(2,1)S(1)}, u32[]{:S(2)}, u32[]{:S(2)}) collective-permute-start(bf16[272,128]{1,0:T(8,128)(2,1)S(1)} %shard_map.74.refs_4_), channel_id=1, source_target_pairs={{0,1},{1,0},{2,3},{3,2},{4,5},{5,4},{6,7},{7,6},{8,9},{9,8},{10,11... | collective-permute-start | bytes 208904 | tf_op jit(solution)/shard_map/ppermute | solution.py:108
  24.4 5.7 %collective-permute-start.10 = (bf16[272,128]{1,0:T(8,128)(2,1)S(1)}, bf16[272,128]{1,0:T(8,128)(2,1)S(1)}, u32[]{:S(2)}, u32[]{:S(2)}) collective-permute-start(bf16[272,128]{1,0:T(8,128)(2,1)S(1)} %shard_map.73.refs_0_), channel_id=1, source_target_pairs={{0,12},{4,8},{8,4},{12,0},{16,28},{20,24},{24,20},{28,16},{1,13},{... | collective-permute-start | bytes 208904 | tf_op jit(solution)/shard_map/ppermute | solution.py:108
  27.0 4.3 %collective-permute-start.9 = (bf16[272,128]{1,0:T(8,128)(2,1)S(1)}, bf16[272,128]{1,0:T(8,128)(2,1)S(1)}, u32[]{:S(2)}, u32[]{:S(2)}) collective-permute-start(bf16[272,128]{1,0:T(8,128)(2,1)S(1)} %shard_map.73.refs_0_), channel_id=1, source_target_pairs={{0,8},{4,12},{8,0},{12,4},{16,24},{20,28},{24,16},{28,20},{1,9},{5... | collective-permute-start | bytes 208904 | tf_op jit(solution)/shard_map/ppermute | solution.py:108
  27.4 4.3 %collective-permute-start.8 = (bf16[272,128]{1,0:T(8,128)(2,1)S(1)}, bf16[272,128]{1,0:T(8,128)(2,1)S(1)}, u32[]{:S(2)}, u32[]{:S(2)}) collective-permute-start(bf16[272,128]{1,0:T(8,128)(2,1)S(1)} %shard_map.73.refs_0_), channel_id=1, source_target_pairs={{0,4},{4,0},{8,12},{12,8},{16,20},{20,16},{24,28},{28,24},{1,5},{5... | collective-permute-start | bytes 208904 | tf_op jit(solution)/shard_map/ppermute | solution.py:108
  31.9 4.3 %collective-permute-start.16 = (bf16[128,128]{1,0:T(8,128)(2,1)S(1)}, bf16[128,128]{1,0:T(8,128)(2,1)S(1)}, u32[]{:S(2)}, u32[]{:S(2)}) collective-permute-start(bf16[128,128]{1,0:T(8,128)(2,1)S(1)} %get-tuple-element.33.refs_0_), channel_id=1, source_target_pairs={{0,3},{1,2},{2,1},{3,0},{4,7},{5,6},{6,5},{7,4},{8,11},{9,10},{10,... | collective-permute-start | bytes 98312 | tf_op jit(solution)/shard_map/ppermute | solution.py:108
  31.9 4.3 %collective-permute-start.15 = (bf16[128,128]{1,0:T(8,128)(2,1)S(1)}, bf16[128,128]{1,0:T(8,128)(2,1)S(1)}, u32[]{:S(2)}, u32[]{:S(2)}) collective-permute-start(bf16[128,128]{1,0:T(8,128)(2,1)S(1)} %get-tuple-element.33.refs_0_), channel_id=1, source_target_pairs={{0,2},{1,3},{2,0},{3,1},{4,6},{5,7},{6,4},{7,5},{8,10},{9,11},{10,... | collective-permute-start | bytes 98312 | tf_op jit(solution)/shard_map/ppermute | solution.py:108
  32.9 3.3 %collective-permute-start.14 = (bf16[128,128]{1,0:T(8,128)(2,1)S(1)}, bf16[128,128]{1,0:T(8,128)(2,1)S(1)}, u32[]{:S(2)}, u32[]{:S(2)}) collective-permute-start(bf16[128,128]{1,0:T(8,128)(2,1)S(1)} %get-tuple-element.33.refs_0_), channel_id=1, source_target_pairs={{0,1},{1,0},{2,3},{3,2},{4,5},{5,4},{6,7},{7,6},{8,9},{9,8},{10,11... | collective-permute-start | bytes 98312 | tf_op jit(solution)/shard_map/ppermute | solution.py:108
  36.4 4.7 %collective-permute-start.19 = (bf16[128,128]{1,0:T(8,128)(2,1)S(1)}, bf16[128,128]{1,0:T(8,128)(2,1)S(1)}, u32[]{:S(2)}, u32[]{:S(2)}) collective-permute-start(bf16[128,128]{1,0:T(8,128)(2,1)S(1)} %get-tuple-element.39.refs_0_), channel_id=1, source_target_pairs={{0,3},{1,2},{2,1},{3,0},{4,7},{5,6},{6,5},{7,4},{8,11},{9,10},{10,... | collective-permute-start | bytes 98312 | tf_op jit(solution)/shard_map/ppermute | solution.py:108
  37.0 4.1 %collective-permute-start.18 = (bf16[128,128]{1,0:T(8,128)(2,1)S(1)}, bf16[128,128]{1,0:T(8,128)(2,1)S(1)}, u32[]{:S(2)}, u32[]{:S(2)}) collective-permute-start(bf16[128,128]{1,0:T(8,128)(2,1)S(1)} %get-tuple-element.39.refs_0_), channel_id=1, source_target_pairs={{0,2},{1,3},{2,0},{3,1},{4,6},{5,7},{6,4},{7,5},{8,10},{9,11},{10,... | collective-permute-start | bytes 98312 | tf_op jit(solution)/shard_map/ppermute | solution.py:108
  41.2 6.2 %collective-permute-start.20 = (bf16[176,128]{1,0:T(8,128)(2,1)S(1)}, bf16[176,128]{1,0:T(8,128)(2,1)S(1)}, u32[]{:S(2)}, u32[]{:S(2)}) collective-permute-start(bf16[176,128]{1,0:T(8,128)(2,1)S(1)} %get-tuple-element.42), channel_id=1, source_target_pairs={{0,12},{4,8},{8,4},{12,0},{16,28},{20,24},{24,20},{28,16},{1,13},{... | collective-permute-start | bytes 135176 | tf_op jit(solution)/shard_map/ppermute | solution.py:108
  43.3 4.1 %collective-permute-start.21 = (bf16[176,128]{1,0:T(8,128)(2,1)S(1)}, bf16[176,128]{1,0:T(8,128)(2,1)S(1)}, u32[]{:S(2)}, u32[]{:S(2)}) collective-permute-start(bf16[176,128]{1,0:T(8,128)(2,1)S(1)} %get-tuple-element.43), channel_id=1, source_target_pairs={{0,8},{4,12},{8,0},{12,4},{16,24},{20,28},{24,16},{28,20},{1,9},{5... | collective-permute-start | bytes 135176 | tf_op jit(solution)/shard_map/ppermute | solution.py:108
  43.7 4.0 %collective-permute-start.22 = (bf16[176,128]{1,0:T(8,128)(2,1)S(1)}, bf16[176,128]{1,0:T(8,128)(2,1)S(1)}, u32[]{:S(2)}, u32[]{:S(2)}) collective-permute-start(bf16[176,128]{1,0:T(8,128)(2,1)S(1)} %get-tuple-element.44), channel_id=1, source_target_pairs={{0,4},{4,0},{8,12},{12,8},{16,20},{20,16},{24,28},{28,24},{1,5},{5... | collective-permute-start | bytes 135176 | tf_op jit(solution)/shard_map/ppermute | solution.py:108
  47.8 5.0 %collective-permute-start.23 = (bf16[160,128]{1,0:T(8,128)(2,1)S(1)}, bf16[160,128]{1,0:T(8,128)(2,1)S(1)}, u32[]{:S(2)}, u32[]{:S(2)}) collective-permute-start(bf16[160,128]{1,0:T(8,128)(2,1)S(1)} %get-tuple-element.52), channel_id=1, source_target_pairs={{0,16},{4,20},{8,24},{12,28},{16,0},{20,4},{24,8},{28,12},{1,17},{... | collective-permute-start | bytes 122888 | tf_op jit(solution)/shard_map/ppermute | solution.py:108
  48.4 3.9 %collective-permute-start.25 = (bf16[80,128]{1,0:T(8,128)(2,1)S(1)}, bf16[80,128]{1,0:T(8,128)(2,1)S(1)}, u32[]{:S(2)}, u32[]{:S(2)}) collective-permute-start(bf16[80,128]{1,0:T(8,128)(2,1)S(1)} %get-tuple-element.55), channel_id=1, source_target_pairs={{0,2},{1,3},{2,0},{3,1},{4,6},{5,7},{6,4},{7,5},{8,10},{9,11},{10,... | collective-permute-start | bytes 61448 | tf_op jit(solution)/shard_map/ppermute | solution.py:108
  (5 other events, 20.5 us)

commit v5 on v4

--- a/solution.py
+++ b/solution.py
@@ -10,7 +10,7 @@
 F32 = jnp.float32
 BF16 = jnp.bfloat16
 NORM_ROWS = 16
-VMEM_LIMIT = 24 << 20
+VMEM_LIMIT = 4 << 20
 HOLD_FLOPS = 5 * 10**9
 PLACE_FLOPS = 2 * 10**9
 
@@ -66,7 +66,7 @@
     mid = rest.astype(BF16).astype(F32)
     low = rest - mid
     rows = jnp.concatenate([high, mid, low, jnp.zeros((NORM_ROWS - 3, norm.shape[1]), F32)], 0)
-    ref[start : start + NORM_ROWS] = rows.astype(BF16)
+    ref[start : start + NORM_ROWS] = rows.astype(ref.dtype)
 
 
 def get_norm(ref, start):
@@ -92,10 +92,10 @@
     return tree([get_norm(r, start) for r in refs])
 
 
-def digits(n, most=4):
+def digits(n):
     weight = 1
     while weight < n:
-        radix = 4 if most == 4 and (n // weight) % 4 == 0 else 2
+        radix = 4 if (n // weight) % 4 == 0 else 2
         yield weight, radix
         weight *= radix
 
@@ -167,13 +167,13 @@
         put_norm(out, norm_at, sum_norm(ins, norm_at))
 
 
-def sum_parts(x, axis, norm_at=None, most=4, high_first=False):
+def sum_parts(x, axis, norm_at=None, high_first=False):
     parts = [x]
-    order = list(digits(lax.axis_size(axis), most))
+    order = list(digits(lax.axis_size(axis)))
     for weight, radix in reversed(order) if high_first else order:
         if len(parts) > 1:
             (x,) = call(functools.partial(add_kernel, norm_at), [(x.shape, BF16)], *parts)
-        parts = [x] + [swap(x, axis, weight, q) for q in range(1, radix)]
+        parts = [x] + [swap(x, axis, weight, q) for q in turns(radix)[1:]]
     return parts
 
 
@@ -192,55 +192,53 @@
     lax.fori_loop(0, rows_i // group, step, 0)
 
 
-def sum_b(t_ref, a_ref, c16, acc):
-    rows_i, rows_j, depth = t_ref.shape
-    group = divisor(rows_i, 256)
-    acc[...] = jnp.zeros_like(acc)
-
-    def step(g, carry):
-        at = pl.ds(pl.multiple_of(g * group, group), group)
-        a16 = a_ref[at].astype(BF16)
-        pairs = jnp.concatenate([a16[q : q + 1] * c16 for q in range(group)], 0)
-        block = t_ref[at]
-        acc[...] += dot(jnp.concatenate([block[q] for q in range(group)], 1), pairs)
-        return carry
-
-    lax.fori_loop(0, rows_i // group, step, 0)
-
-
-def sum_a(t_ref, a_ref, b16, c16, acc, acc_b=None):
+def sum_b(t_ref, a_ref, c16, acc, low, high):
     rows_i, rows_j, depth = t_ref.shape
     rank = c16.shape[1]
-    group = divisor(rows_i, 256)
-    half = group // 2
+    half = rows_i // 2
+    group = divisor(half, 128)
+    pair_c = twice(c16)
+    acc[...] = jnp.zeros_like(acc)
+
+    def step(g, carry):
+        first = pl.multiple_of(g * group, group)
+        left, right = t_ref[pl.ds(first, group)], t_ref[pl.ds(half + first, group)]
+        a_left = a_ref[pl.ds(first, group)].astype(BF16).astype(F32)
+        a_right = a_ref[pl.ds(half + first, group)].astype(BF16).astype(F32)
+        total = acc[...]
+        for q in range(group):
+            along = dot(jnp.concatenate([left[q], right[q]], 1), pair_c)
+            for part, kept, a32 in ((along[:, :rank], low, a_left), (along[:, rank:], high, a_right)):
+                kept[first + q] = part
+                total = total + part * a32[q : q + 1]
+        acc[...] = total
+        return carry
+
+    lax.fori_loop(0, half // group, step, 0)
+
+
+def sum_a(low, high, b16, acc):
+    half = low.shape[0]
+    group = divisor(half, 128)
     b32 = b16.astype(F32)
-    pair_c = twice(c16)
-    if acc_b is not None:
-        acc_b[...] = jnp.zeros_like(acc_b)
 
     def step(g, carry):
-        at = pl.ds(pl.multiple_of(g * group, group), group)
-        block = t_ref[at]
-        if acc_b is not None:
-            a32 = a_ref[at].astype(BF16).astype(F32)
-            total = acc_b[...]
-        sums = [None] * group
-        for q in range(half):
-            along = dot(jnp.concatenate([block[q], block[q + half]], 1), pair_c)
-            for i, part in ((q, along[:, :rank]), (q + half, along[:, rank:])):
-                sums[i] = jnp.sum(part * b32, axis=0, keepdims=True)
-                if acc_b is not None:
-                    total = total + part * a32[i : i + 1]
-        acc[at] = jnp.concatenate(sums, 0)
-        if acc_b is not None:
-            acc_b[...] = total
+        first = pl.multiple_of(g * group, group)
+        for start, kept in ((first, low), (half + first, high)):
+            sums = [jnp.sum(kept[first + q] * b32, axis=0, keepdims=True) for q in range(group)]
+            acc[pl.ds(start, group)] = jnp.concatenate(sums, 0)
         return carry
 
-    lax.fori_loop(0, rows_i // group, step, 0)
-
-
-def first_b_kernel(t_ref, a_ref, c_ref, acc):
-    sum_b(t_ref, a_ref, c_ref[...].astype(BF16), acc)
+    lax.fori_loop(0, half // group, step, 0)
+
+
+def kept_shapes(tensor, rank):
+    rows_i, rows_j, _ = tensor.shape
+    return [((rows_i // 2, rows_j, rank), F32)] * 2
+
+
+def first_b_kernel(t_ref, a_ref, c_ref, acc, low, high):
+    sum_b(t_ref, a_ref, c_ref[...].astype(BF16), acc, low, high)
 
 
 def first_c_kernel(t_ref, a_ref, b_ref, c_ref, acc_b, row_ref, acc_c):
@@ -255,13 +253,12 @@
     put_norm(row_ref, rows_j + depth, squares(a16))
 
 
-def first_a_kernel(t_ref, a_ref, b_ref, c_ref, col_ref, acc_a):
+def first_a_kernel(low, high, a_ref, b_ref, c_ref, col_ref, acc_a):
     rows_i = a_ref.shape[0]
-    a16 = a_ref[...].astype(BF16)
     b16 = b_ref[...].astype(BF16)
-    c16 = c_ref[...].astype(BF16)
-    sum_a(t_ref, a_ref, b16, c16, acc_a)
-    col_ref[:rows_i] = (acc_a[...] - dot_wide(a16, gram(b16) * gram(c16))).astype(BF16)
+    sum_a(low, high, b16, acc_a)
+    model = dot_wide(a_ref[...].astype(BF16), gram(b16) * gram(c_ref[...].astype(BF16)))
+    col_ref[:rows_i] = (acc_a[...] - model).astype(BF16)
     put_norm(col_ref, rows_i, squares(b16))
 
 
@@ -296,19 +293,18 @@
     out_ref[...] = (sum_ref[...] - dot_wide(c2.astype(BF16), gram_ref[...])).astype(BF16)
 
 
-def second_b_kernel(t_ref, a_ref, b_ref, c_ref, grad_b):
+def second_b_kernel(t_ref, a_ref, b_ref, c_ref, grad_b, low, high):
     a16 = a_ref[...].astype(BF16)
     c16 = c_ref[...].astype(BF16)
-    sum_b(t_ref, a_ref, c16, grad_b)
+    sum_b(t_ref, a_ref, c16, grad_b, low, high)
     grad_b[...] -= dot_wide(b_ref[...].astype(BF16), gram(a16) * gram(c16))
 
 
-def second_a_kernel(weight, own_i, t_ref, a_ref, b_ref, c_ref, *refs):
+def second_a_kernel(weight, own_i, low, high, a_ref, b_ref, c_ref, *refs):
     *outs, acc_a = refs
     b16 = b_ref[...].astype(BF16)
-    c16 = c_ref[...].astype(BF16)
-    sum_a(t_ref, a_ref, b16, c16, acc_a)
-    acc_a[...] -= dot_wide(a_ref[...].astype(BF16), gram(b16) * gram(c16))
+    sum_a(low, high, b16, acc_a)
+    acc_a[...] -= dot_wide(a_ref[...].astype(BF16), gram(b16) * gram(c_ref[...].astype(BF16)))
     put_shares("col", weight, own_i, None, squares(b16), acc_a, outs)
 
 
@@ -323,7 +319,7 @@
         put_norm(out, depth, norm)
         first = [(high * radix + (digit ^ q)) * own for high in range(blocks // radix)]
         rows = [grad[pl.ds(pl.multiple_of(at, own), own)] for at in first]
-        out[depth + NORM_ROWS :] = jnp.concatenate(rows, 0).astype(BF16)
+        out[depth + NORM_ROWS :] = jnp.concatenate(rows, 0).astype(out.dtype)
 
 
 def shares_kernel(n_col, own_j, weight, *refs):
@@ -344,8 +340,8 @@
     return next(digits(lax.axis_size(axis)))
 
 
-def messages(depth, rows, rank, radix):
-    return [((depth + NORM_ROWS + rows // radix, rank), BF16)] * radix
+def messages(depth, rows, rank, radix, dtype):
+    return [((depth + NORM_ROWS + rows // radix, rank), dtype)] * radix
 
 
 def sum_shares(sent, axis, own, depth, beside=None):
@@ -356,15 +352,15 @@
             held = parts[0].shape[0] - depth - NORM_ROWS
             sent = call(
                 functools.partial(next_shares_kernel, axis, weight, own, depth, len(parts)),
-                messages(depth, held, rank, radix),
+                messages(depth, held, rank, radix, sent[0].dtype),
                 *parts,
                 scratch=[pltpu.VMEM((held, rank), F32)],
             )
             if beside is not None:
-                sent, beside = lax.optimization_barrier((sent, beside))
+                sent, _ = lax.optimization_barrier((sent, beside))
         got = [swap(x, axis, weight, q) for q, x in zip(turns(radix)[1:], sent[1:])]
         parts = [sent[0]] + got
-    return parts if beside is None else (parts, beside)
+    return parts
 
 
 def last_kernel(n_row, n_col, *refs):
@@ -391,10 +387,11 @@
     rank = factor_a.shape[1]
     held_a, held_b, c = hold(factor_a, factor_b, factor_c)
     b = gather(factor_b, held_b, "row")
-    a = gather(factor_a, held_a, "col")
-
-    (grad_b,) = call(
-        first_b_kernel, [(b.shape, F32)], tensor, a, c, flops=2 * tensor.size * rank
+    a = gather(held_a, held_a, "col")
+
+    kept = kept_shapes(tensor, rank)
+    grad_b, low, high = call(
+        first_b_kernel, [(b.shape, F32)] + kept, tensor, a, c, flops=2 * tensor.size * rank
     )
     (to_row,) = call(
         first_c_kernel,
@@ -406,9 +403,9 @@
     (to_col,) = call(
         first_a_kernel,
         [((rows_i + NORM_ROWS, rank), BF16)],
-        tensor, a, b, c,
+        low, high, a, b, c,
         scratch=[pltpu.VMEM(a.shape, F32)],
-        flops=2 * tensor.size * rank,
+        flops=tensor.size * rank,
     )
     rows = sum_parts(to_row, "row", rows_j + depth, high_first=True)
     cols = sum_parts(to_col, "col", rows_i)
@@ -431,24 +428,24 @@
         *parts, step_c, c, sum_t, gram_ab,
     )
     parts = sum_parts(to_col, "col")
-    (grad_b,) = call(
-        second_b_kernel, [(b.shape, F32)], tensor, a, b, c, flops=2 * tensor.size * rank
+    grad_b, low, high = call(
+        second_b_kernel, [(b.shape, F32)] + kept, tensor, a, b, c, flops=2 * tensor.size * rank
     )
     weight, radix = first_digit("row")
     to_row = call(
         functools.partial(shares_kernel, len(parts), factor_b.shape[0], weight),
-        messages(depth, rows_j, rank, radix),
+        messages(depth, rows_j, rank, radix, BF16),
         *parts, a, grad_b,
     )
     weight, radix = first_digit("col")
     to_col = call(
         functools.partial(second_a_kernel, weight, factor_a.shape[0]),
-        messages(0, rows_i, rank, radix),
-        tensor, a, b, c,
+        messages(0, rows_i, rank, radix, F32),
+        low, high, a, b, c,
         scratch=[pltpu.VMEM((rows_i, rank), F32)],
-        flops=2 * tensor.size * rank,
-    )
-    rows, to_col = sum_shares(to_row, "row", factor_b.shape[0], depth, to_col)
+        flops=tensor.size * rank,
+    )
+    rows = sum_shares(to_row, "row", factor_b.shape[0], depth, to_col)
     cols = sum_shares(to_col, "col", factor_a.shape[0], 0)
     return call(
         functools.partial(last_kernel, len(rows), len(cols)),

time: 53.6 us -> 53 us (0.989)
  Pallas kernels: 17.3 us -> 15.2 us
  starting transfers between devices: 27.9 us -> 29.5 us
    pallas_call x15, Pallas kernels: 16.4 us -> 14.3 us  [call(): pl.pallas_call(body, in_specs=[whole] * len(operands), out_specs=[whole]...]
    ppermute x27, starting transfers between devices: 27.9 us -> 29.5 us  [swap(): lax.ppermute(x, axis, [(i, i ^ q * weight) for i in range(lax.axis_size(a...]
  transfers between devices with their start and end apart: 27 -> 27, of which waited for: 11 -> 7; matrix products, arithmetic and copies ran while one was open for 0% -> 0% of each run, Pallas kernels for 26% -> 22%
where the time goes in v5:
time: 53 us; the launch traced here: 52.8 us
  starting transfers between devices  29.5 us (56%)
  Pallas kernels  15.2 us (29%)
  waiting for transfers between devices  7.3 us (14%)
  between operations  0.75 us (1%)
    ppermute x27, starting transfers between devices, swap(): lax.ppermute(x, axis, [(i, i ^ q * weight) for i in range(lax.axis_size(a...  29.5 us
    pallas_call x15, Pallas kernels, call(): pl.pallas_call(body, in_specs=[whole] * len(operands), out_specs=[whole]...  14.3 us
    ppermute x27, waiting for transfers between devices, swap(): lax.ppermute(x, axis, [(i, i ^ q * weight) for i in range(lax.axis_size(a...  7.3 us
  transfers between devices with their start and end apart: 27, of which 7 were waited for; matrix products, arithmetic and copies ran while one was open for 0% of the time, Pallas kernels for 22%

profile of v5, /device:TPU:0, one launch (start us, length us, event | category | flops | bytes accessed | tf_op | source)
XLA Modules:
  0.0 52.8 jit_solution(14643608017774694969)
XLA Ops:
  0.6 4.0 %collective-permute-start.3 = (f32[16,128]{1,0:T(8,128)}, f32[16,128]{1,0:T(8,128)S(1)}, u32[]{:S(2)}, u32[]{:S(2)}) collective-permute-start(f32[16,128]{1,0:T(8,128)} %refs_1_.1), channel_id=1, source_target_pairs={{0,12},{4,8},{8,4},{12,0},{16,28},{20,24},{24,20},{28,16},{1,13},{... | collective-permute-start | bytes 24584 | tf_op jit(solution)/shard_map/ppermute | solution.py:108
  6.7 1.5 %collective-permute-start.1 = (f32[64,128]{1,0:T(8,128)S(1)}, f32[64,128]{1,0:T(8,128)S(1)}, u32[]{:S(2)}, u32[]{:S(2)}) collective-permute-start(f32[64,128]{1,0:T(8,128)S(1)} %get-tuple-element.32.refs_0_), channel_id=1, source_target_pairs={{0,2},{1,3},{2,0},{3,1},{4,6},{5,7},{6,4},{7,5},{8,10},{9,11},{10,... | collective-permute-start | bytes 98312 | tf_op jit(solution)/shard_map/ppermute | solution.py:108
  9.0 2.6 %collective-permute-start.6 = (f32[64,128]{1,0:T(8,128)S(1)}, f32[64,128]{1,0:T(8,128)S(1)}, u32[]{:S(2)}, u32[]{:S(2)}) collective-permute-start(f32[64,128]{1,0:T(8,128)S(1)} %shard_map.69.refs_0_), channel_id=1, source_target_pairs={{0,16},{4,20},{8,24},{12,28},{16,0},{20,4},{24,8},{28,12},{1,17},{... | collective-permute-start | bytes 98312 | tf_op jit(solution)/shard_map/ppermute | solution.py:108
  11.6 2.4 %shard_map.71 = (f32[128,128]{1,0:T(8,128)S(1)}, f32[128,128,128]{2,1,0:T(8,128)S(1)}, f32[128,128,128]{2,1,0:T(8,128)S(1)}) custom-call(bf16[256,128,128]{2,1,0:T(8,128)(2,1)S(1)} %copy-done, f32[256,128]{1,0:T(8,128)S(1)} %shard_map.68.a_ref.refs_8_, f32[128,128]{1,0:T(8,128)S(1)} %get-tuple-element.34.c_ref.refs_10_.refs_5_), custom_call_target="tpu_custom_call" | custom-call | flops 1073741824 | tf_op jit(solution)/shard_map/pallas_call | solution.py:30
  14.0 2.6 %shard_map.72.refs_0_ = bf16[272,128]{1,0:T(8,128)(2,1)S(1)} custom-call(bf16[256,128,128]{2,1,0:T(8,128)(2,1)S(1)} %copy-done, f32[256,128]{1,0:T(8,128)S(1)} %shard_map.68.a_ref.refs_8_, f32[128,128]{1,0:T(8,128)S(1)} %shard_map.70.b_ref.refs_9_, f32[128,128]{1,0:T(8,128)S(1)} %get-tuple-element.34.c_ref.refs_10_.refs_5_, ...), custom_call_target="tpu_custom_call" | custom-call | flops 1073741824 | tf_op jit(solution)/shard_map/pallas_call | solution.py:30
  16.6 2.5 %collective-permute-start.7 = (bf16[272,128]{1,0:T(8,128)(2,1)S(1)}, bf16[272,128]{1,0:T(8,128)(2,1)S(1)}, u32[]{:S(2)}, u32[]{:S(2)}) collective-permute-start(bf16[272,128]{1,0:T(8,128)(2,1)S(1)} %shard_map.72.refs_0_), channel_id=1, source_target_pairs={{0,16},{4,20},{8,24},{12,28},{16,0},{20,4},{24,8},{28,12},{1,17},{... | collective-permute-start | bytes 208904 | tf_op jit(solution)/shard_map/ppermute | solution.py:108
  19.1 1.5 %shard_map.74.refs_4_ = bf16[272,128]{1,0:T(8,128)(2,1)S(1)} custom-call(f32[128,128,128]{2,1,0:T(8,128)S(1)} %get-tuple-element.36.low, f32[128,128,128]{2,1,0:T(8,128)S(1)} %get-tuple-element.37.high, f32[256,128]{1,0:T(8,128)S(1)} %shard_map.68.a_ref.refs_8_, f32[128,128]{1,0:T(8,128)S(1)} %shard_map.70.b_ref.refs_9_, ...), custom_call_target="tpu_custom_call" | custom-call | flops 536870912 | tf_op jit(solution)/shard_map/pallas_call | solution.py:30
  20.7 1.6 %collective-permute-start.12 = (bf16[272,128]{1,0:T(8,128)(2,1)S(1)}, bf16[272,128]{1,0:T(8,128)(2,1)S(1)}, u32[]{:S(2)}, u32[]{:S(2)}) collective-permute-start(bf16[272,128]{1,0:T(8,128)(2,1)S(1)} %shard_map.74.refs_4_), channel_id=1, source_target_pairs={{0,2},{1,3},{2,0},{3,1},{4,6},{5,7},{6,4},{7,5},{8,10},{9,11},{10,... | collective-permute-start | bytes 208904 | tf_op jit(solution)/shard_map/ppermute | solution.py:108
  22.6 2.0 %collective-permute-start.10 = (bf16[272,128]{1,0:T(8,128)(2,1)S(1)}, bf16[272,128]{1,0:T(8,128)(2,1)S(1)}, u32[]{:S(2)}, u32[]{:S(2)}) collective-permute-start(bf16[272,128]{1,0:T(8,128)(2,1)S(1)} %shard_map.73.refs_0_), channel_id=1, source_target_pairs={{0,4},{4,0},{8,12},{12,8},{16,20},{20,16},{24,28},{28,24},{1,5},{5... | collective-permute-start | bytes 208904 | tf_op jit(solution)/shard_map/ppermute | solution.py:108
  24.5 1.3 %collective-permute-start.8 = (bf16[272,128]{1,0:T(8,128)(2,1)S(1)}, bf16[272,128]{1,0:T(8,128)(2,1)S(1)}, u32[]{:S(2)}, u32[]{:S(2)}) collective-permute-start(bf16[272,128]{1,0:T(8,128)(2,1)S(1)} %shard_map.73.refs_0_), channel_id=1, source_target_pairs={{0,12},{4,8},{8,4},{12,0},{16,28},{20,24},{24,20},{28,16},{1,13},{... | collective-permute-start | bytes 208904 | tf_op jit(solution)/shard_map/ppermute | solution.py:108
  25.9 1.0 %collective-permute-start.9 = (bf16[272,128]{1,0:T(8,128)(2,1)S(1)}, bf16[272,128]{1,0:T(8,128)(2,1)S(1)}, u32[]{:S(2)}, u32[]{:S(2)}) collective-permute-start(bf16[272,128]{1,0:T(8,128)(2,1)S(1)} %shard_map.73.refs_0_), channel_id=1, source_target_pairs={{0,8},{4,12},{8,0},{12,4},{16,24},{20,28},{24,16},{28,20},{1,9},{5... | collective-permute-start | bytes 208904 | tf_op jit(solution)/shard_map/ppermute | solution.py:108
  26.9 1.0 %collective-permute-done.10.refs_3_ = bf16[272,128]{1,0:T(8,128)(2,1)S(1)} collective-permute-done((bf16[272,128]{1,0:T(8,128)(2,1)S(1)}, bf16[272,128]{1,0:T(8,128)(2,1)S(1)}, u32[]{:S(2)}, u32[]{:S(2)}) %collective-permute-start.10) | collective-permute-done | bytes 69664 | tf_op jit(solution)/shard_map/ppermute | solution.py:108
  27.9 2.3 %collective-permute-done.8.refs_1_ = bf16[272,128]{1,0:T(8,128)(2,1)S(1)} collective-permute-done((bf16[272,128]{1,0:T(8,128)(2,1)S(1)}, bf16[272,128]{1,0:T(8,128)(2,1)S(1)}, u32[]{:S(2)}, u32[]{:S(2)}) %collective-permute-start.8) | collective-permute-done | bytes 69664 | tf_op jit(solution)/shard_map/ppermute | solution.py:108
  30.6 1.4 %collective-permute-start.15 = (bf16[128,128]{1,0:T(8,128)(2,1)S(1)}, bf16[128,128]{1,0:T(8,128)(2,1)S(1)}, u32[]{:S(2)}, u32[]{:S(2)}) collective-permute-start(bf16[128,128]{1,0:T(8,128)(2,1)S(1)} %get-tuple-element.38.refs_0_), channel_id=1, source_target_pairs={{0,2},{1,3},{2,0},{3,1},{4,6},{5,7},{6,4},{7,5},{8,10},{9,11},{10,... | collective-permute-start | bytes 98312 | tf_op jit(solution)/shard_map/ppermute | solution.py:108
  32.2 2.4 %shard_map.76 = (f32[128,128]{1,0:T(8,128)S(1)}, f32[128,128]{1,0:T(8,128)S(1)}) custom-call(bf16[256,128,128]{2,1,0:T(8,128)(2,1)S(1)} %copy-done, f32[256,128]{1,0:T(8,128)S(1)} %get-tuple-element.40.a_ref.refs_4_.refs_6_, f32[128,128]{1,0:T(8,128)S(1)} %get-tuple-element.41.b_ref.refs_7_), custom_call_target="tpu_custom_call" | custom-call | flops 1073741824 | tf_op jit(solution)/shard_map/pallas_call | solution.py:30
  34.9 1.2 %collective-permute-start.17 = (bf16[128,128]{1,0:T(8,128)(2,1)S(1)}, bf16[128,128]{1,0:T(8,128)(2,1)S(1)}, u32[]{:S(2)}, u32[]{:S(2)}) collective-permute-start(bf16[128,128]{1,0:T(8,128)(2,1)S(1)} %get-tuple-element.44.refs_0_), channel_id=1, source_target_pairs={{0,3},{1,2},{2,1},{3,0},{4,7},{5,6},{6,5},{7,4},{8,11},{9,10},{10,... | collective-permute-start | bytes 98312 | tf_op jit(solution)/shard_map/ppermute | solution.py:108
  36.8 2.8 %shard_map.78 = (f32[128,128]{1,0:T(8,128)S(1)}, f32[128,128,128]{2,1,0:T(8,128)S(1)}, f32[128,128,128]{2,1,0:T(8,128)S(1)}) custom-call(bf16[256,128,128]{2,1,0:T(8,128)(2,1)S(1)} %copy-done, f32[256,128]{1,0:T(8,128)S(1)} %get-tuple-element.40.a_ref.refs_4_.refs_6_, f32[128,128]{1,0:T(8,128)S(1)} %get-tuple-element.41.b_ref.refs_7_, ...), custom_call_target="tpu_custom_call" | custom-call | flops 1073741824 | tf_op jit(solution)/shard_map/pallas_call | solution.py:30
  40.0 1.7 %collective-permute-start.20 = (bf16[176,128]{1,0:T(8,128)(2,1)S(1)}, bf16[176,128]{1,0:T(8,128)(2,1)S(1)}, u32[]{:S(2)}, u32[]{:S(2)}) collective-permute-start(bf16[176,128]{1,0:T(8,128)(2,1)S(1)} %get-tuple-element.48), channel_id=1, source_target_pairs={{0,12},{4,8},{8,4},{12,0},{16,28},{20,24},{24,20},{28,16},{1,13},{... | collective-permute-start | bytes 135176 | tf_op jit(solution)/shard_map/ppermute | solution.py:108
  41.7 0.9 %collective-permute-start.21 = (bf16[176,128]{1,0:T(8,128)(2,1)S(1)}, bf16[176,128]{1,0:T(8,128)(2,1)S(1)}, u32[]{:S(2)}, u32[]{:S(2)}) collective-permute-start(bf16[176,128]{1,0:T(8,128)(2,1)S(1)} %get-tuple-element.49), channel_id=1, source_target_pairs={{0,8},{4,12},{8,0},{12,4},{16,24},{20,28},{24,16},{28,20},{1,9},{5... | collective-permute-start | bytes 135176 | tf_op jit(solution)/shard_map/ppermute | solution.py:108
  42.6 1.0 %collective-permute-start.22 = (bf16[176,128]{1,0:T(8,128)(2,1)S(1)}, bf16[176,128]{1,0:T(8,128)(2,1)S(1)}, u32[]{:S(2)}, u32[]{:S(2)}) collective-permute-start(bf16[176,128]{1,0:T(8,128)(2,1)S(1)} %get-tuple-element.50), channel_id=1, source_target_pairs={{0,4},{4,0},{8,12},{12,8},{16,20},{20,16},{24,28},{28,24},{1,5},{5... | collective-permute-start | bytes 135176 | tf_op jit(solution)/shard_map/ppermute | solution.py:108
  43.6 1.5 %shard_map.81 = (f32[80,128]{1,0:T(8,128)S(1)}, f32[80,128]{1,0:T(8,128)S(1)}, f32[80,128]{1,0:T(8,128)S(1)}, f32[80,128]{1,0:T(8,128)S(1)}) custom-call(f32[128,128,128]{2,1,0:T(8,128)S(1)} %get-tuple-element.53.low, f32[128,128,128]{2,1,0:T(8,128)S(1)} %get-tuple-element.54.high, f32[256,128]{1,0:T(8,128)S(1)} %get-tuple-element.40.a_ref.refs_4_.refs_6_, ...), custom_call_target="tpu_custom_call" | custom-call | flops 536870912 | tf_op jit(solution)/shard_map/pallas_call | solution.py:30
  45.4 1.0 %collective-permute-start.25 = (f32[80,128]{1,0:T(8,128)S(1)}, f32[80,128]{1,0:T(8,128)S(1)}, u32[]{:S(2)}, u32[]{:S(2)}) collective-permute-start(f32[80,128]{1,0:T(8,128)S(1)} %get-tuple-element.57), channel_id=1, source_target_pairs={{0,2},{1,3},{2,0},{3,1},{4,6},{5,7},{6,4},{7,5},{8,10},{9,11},{10,... | collective-permute-start | bytes 122888 | tf_op jit(solution)/shard_map/ppermute | solution.py:108
  47.1 2.2 %collective-permute-start.23 = (bf16[160,128]{1,0:T(8,128)(2,1)S(1)}, bf16[160,128]{1,0:T(8,128)(2,1)S(1)}, u32[]{:S(2)}, u32[]{:S(2)}) collective-permute-start(bf16[160,128]{1,0:T(8,128)(2,1)S(1)} %get-tuple-element.60), channel_id=1, source_target_pairs={{0,16},{4,20},{8,24},{12,28},{16,0},{20,4},{24,8},{28,12},{1,17},{... | collective-permute-start | bytes 122888 | tf_op jit(solution)/shard_map/ppermute | solution.py:108
  49.7 2.4 %collective-permute-done.23.refs_1_ = bf16[160,128]{1,0:T(8,128)(2,1)S(1)} collective-permute-done((bf16[160,128]{1,0:T(8,128)(2,1)S(1)}, bf16[160,128]{1,0:T(8,128)(2,1)S(1)}, u32[]{:S(2)}, u32[]{:S(2)}) %collective-permute-start.23) | collective-permute-done | bytes 40992 | tf_op jit(solution)/shard_map/ppermute | solution.py:108
  (48 shorter events, 7.4 us)
Async XLA Ops:
  0.6 7.6 %collective-permute-start.3 = (f32[16,128]{1,0:T(8,128)}, f32[16,128]{1,0:T(8,128)S(1)}, u32[]{:S(2)}, u32[]{:S(2)}) collective-permute-start(f32[16,128]{1,0:T(8,128)} %refs_1_.1), channel_id=1, source_target_pairs={{0,12},{4,8},{8,4},{12,0},{16,28},{20,24},{24,20},{28,16},{1,13},{... | collective-permute-start | bytes 24584 | tf_op jit(solution)/shard_map/ppermute | solution.py:108
  4.6 3.9 %collective-permute-start.4 = (f32[16,128]{1,0:T(8,128)}, f32[16,128]{1,0:T(8,128)S(1)}, u32[]{:S(2)}, u32[]{:S(2)}) collective-permute-start(f32[16,128]{1,0:T(8,128)} %refs_1_.1), channel_id=1, source_target_pairs={{0,8},{4,12},{8,0},{12,4},{16,24},{20,28},{24,16},{28,20},{1,9},{5... | collective-permute-start | bytes 24584 | tf_op jit(solution)/shard_map/ppermute | solution.py:108
  5.1 3.9 %collective-permute-start.5 = (f32[16,128]{1,0:T(8,128)}, f32[16,128]{1,0:T(8,128)S(1)}, u32[]{:S(2)}, u32[]{:S(2)}) collective-permute-start(f32[16,128]{1,0:T(8,128)} %refs_1_.1), channel_id=1, source_target_pairs={{0,4},{4,0},{8,12},{12,8},{16,20},{20,16},{24,28},{28,24},{1,5},{5... | collective-permute-start | bytes 24584 | tf_op jit(solution)/shard_map/ppermute | solution.py:108
  6.2 5.4 %collective-permute-start = (f32[64,128]{1,0:T(8,128)S(1)}, f32[64,128]{1,0:T(8,128)S(1)}, u32[]{:S(2)}, u32[]{:S(2)}) collective-permute-start(f32[64,128]{1,0:T(8,128)S(1)} %get-tuple-element.32.refs_0_), channel_id=1, source_target_pairs={{0,3},{1,2},{2,1},{3,0},{4,7},{5,6},{6,5},{7,4},{8,11},{9,10},{10,... | collective-permute-start | bytes 98312 | tf_op jit(solution)/shard_map/ppermute | solution.py:108
  6.7 4.9 %collective-permute-start.1 = (f32[64,128]{1,0:T(8,128)S(1)}, f32[64,128]{1,0:T(8,128)S(1)}, u32[]{:S(2)}, u32[]{:S(2)}) collective-permute-start(f32[64,128]{1,0:T(8,128)S(1)} %get-tuple-element.32.refs_0_), channel_id=1, source_target_pairs={{0,2},{1,3},{2,0},{3,1},{4,6},{5,7},{6,4},{7,5},{8,10},{9,11},{10,... | collective-permute-start | bytes 98312 | tf_op jit(solution)/shard_map/ppermute | solution.py:108
  8.2 3.4 %collective-permute-start.2 = (f32[64,128]{1,0:T(8,128)S(1)}, f32[64,128]{1,0:T(8,128)S(1)}, u32[]{:S(2)}, u32[]{:S(2)}) collective-permute-start(f32[64,128]{1,0:T(8,128)S(1)} %get-tuple-element.32.refs_0_), channel_id=1, source_target_pairs={{0,1},{1,0},{2,3},{3,2},{4,5},{5,4},{6,7},{7,6},{8,9},{9,8},{10,11... | collective-permute-start | bytes 98312 | tf_op jit(solution)/shard_map/ppermute | solution.py:108
  9.0 5.0 %collective-permute-start.6 = (f32[64,128]{1,0:T(8,128)S(1)}, f32[64,128]{1,0:T(8,128)S(1)}, u32[]{:S(2)}, u32[]{:S(2)}) collective-permute-start(f32[64,128]{1,0:T(8,128)S(1)} %shard_map.69.refs_0_), channel_id=1, source_target_pairs={{0,16},{4,20},{8,24},{12,28},{16,0},{20,4},{24,8},{28,12},{1,17},{... | collective-permute-start | bytes 98312 | tf_op jit(solution)/shard_map/ppermute | solution.py:108
  16.6 5.9 %collective-permute-start.7 = (bf16[272,128]{1,0:T(8,128)(2,1)S(1)}, bf16[272,128]{1,0:T(8,128)(2,1)S(1)}, u32[]{:S(2)}, u32[]{:S(2)}) collective-permute-start(bf16[272,128]{1,0:T(8,128)(2,1)S(1)} %shard_map.72.refs_0_), channel_id=1, source_target_pairs={{0,16},{4,20},{8,24},{12,28},{16,0},{20,4},{24,8},{28,12},{1,17},{... | collective-permute-start | bytes 208904 | tf_op jit(solution)/shard_map/ppermute | solution.py:108
  20.6 5.3 %collective-permute-start.11 = (bf16[272,128]{1,0:T(8,128)(2,1)S(1)}, bf16[272,128]{1,0:T(8,128)(2,1)S(1)}, u32[]{:S(2)}, u32[]{:S(2)}) collective-permute-start(bf16[272,128]{1,0:T(8,128)(2,1)S(1)} %shard_map.74.refs_4_), channel_id=1, source_target_pairs={{0,3},{1,2},{2,1},{3,0},{4,7},{5,6},{6,5},{7,4},{8,11},{9,10},{10,... | collective-permute-start | bytes 208904 | tf_op jit(solution)/shard_map/ppermute | solution.py:108
  20.7 6.2 %collective-permute-start.12 = (bf16[272,128]{1,0:T(8,128)(2,1)S(1)}, bf16[272,128]{1,0:T(8,128)(2,1)S(1)}, u32[]{:S(2)}, u32[]{:S(2)}) collective-permute-start(bf16[272,128]{1,0:T(8,128)(2,1)S(1)} %shard_map.74.refs_4_), channel_id=1, source_target_pairs={{0,2},{1,3},{2,0},{3,1},{4,6},{5,7},{6,4},{7,5},{8,10},{9,11},{10,... | collective-permute-start | bytes 208904 | tf_op jit(solution)/shard_map/ppermute | solution.py:108
  22.3 4.6 %collective-permute-start.13 = (bf16[272,128]{1,0:T(8,128)(2,1)S(1)}, bf16[272,128]{1,0:T(8,128)(2,1)S(1)}, u32[]{:S(2)}, u32[]{:S(2)}) collective-permute-start(bf16[272,128]{1,0:T(8,128)(2,1)S(1)} %shard_map.74.refs_4_), channel_id=1, source_target_pairs={{0,1},{1,0},{2,3},{3,2},{4,5},{5,4},{6,7},{7,6},{8,9},{9,8},{10,11... | collective-permute-start | bytes 208904 | tf_op jit(solution)/shard_map/ppermute | solution.py:108
  22.6 5.3 %collective-permute-start.10 = (bf16[272,128]{1,0:T(8,128)(2,1)S(1)}, bf16[272,128]{1,0:T(8,128)(2,1)S(1)}, u32[]{:S(2)}, u32[]{:S(2)}) collective-permute-start(bf16[272,128]{1,0:T(8,128)(2,1)S(1)} %shard_map.73.refs_0_), channel_id=1, source_target_pairs={{0,4},{4,0},{8,12},{12,8},{16,20},{20,16},{24,28},{28,24},{1,5},{5... | collective-permute-start | bytes 208904 | tf_op jit(solution)/shard_map/ppermute | solution.py:108
  24.5 5.6 %collective-permute-start.8 = (bf16[272,128]{1,0:T(8,128)(2,1)S(1)}, bf16[272,128]{1,0:T(8,128)(2,1)S(1)}, u32[]{:S(2)}, u32[]{:S(2)}) collective-permute-start(bf16[272,128]{1,0:T(8,128)(2,1)S(1)} %shard_map.73.refs_0_), channel_id=1, source_target_pairs={{0,12},{4,8},{8,4},{12,0},{16,28},{20,24},{24,20},{28,16},{1,13},{... | collective-permute-start | bytes 208904 | tf_op jit(solution)/shard_map/ppermute | solution.py:108
  25.9 4.3 %collective-permute-start.9 = (bf16[272,128]{1,0:T(8,128)(2,1)S(1)}, bf16[272,128]{1,0:T(8,128)(2,1)S(1)}, u32[]{:S(2)}, u32[]{:S(2)}) collective-permute-start(bf16[272,128]{1,0:T(8,128)(2,1)S(1)} %shard_map.73.refs_0_), channel_id=1, source_target_pairs={{0,8},{4,12},{8,0},{12,4},{16,24},{20,28},{24,16},{28,20},{1,9},{5... | collective-permute-start | bytes 208904 | tf_op jit(solution)/shard_map/ppermute | solution.py:108
  30.3 4.3 %collective-permute-start.14 = (bf16[128,128]{1,0:T(8,128)(2,1)S(1)}, bf16[128,128]{1,0:T(8,128)(2,1)S(1)}, u32[]{:S(2)}, u32[]{:S(2)}) collective-permute-start(bf16[128,128]{1,0:T(8,128)(2,1)S(1)} %get-tuple-element.38.refs_0_), channel_id=1, source_target_pairs={{0,3},{1,2},{2,1},{3,0},{4,7},{5,6},{6,5},{7,4},{8,11},{9,10},{10,... | collective-permute-start | bytes 98312 | tf_op jit(solution)/shard_map/ppermute | solution.py:108
  30.6 4.1 %collective-permute-start.15 = (bf16[128,128]{1,0:T(8,128)(2,1)S(1)}, bf16[128,128]{1,0:T(8,128)(2,1)S(1)}, u32[]{:S(2)}, u32[]{:S(2)}) collective-permute-start(bf16[128,128]{1,0:T(8,128)(2,1)S(1)} %get-tuple-element.38.refs_0_), channel_id=1, source_target_pairs={{0,2},{1,3},{2,0},{3,1},{4,6},{5,7},{6,4},{7,5},{8,10},{9,11},{10,... | collective-permute-start | bytes 98312 | tf_op jit(solution)/shard_map/ppermute | solution.py:108
  34.9 4.7 %collective-permute-start.17 = (bf16[128,128]{1,0:T(8,128)(2,1)S(1)}, bf16[128,128]{1,0:T(8,128)(2,1)S(1)}, u32[]{:S(2)}, u32[]{:S(2)}) collective-permute-start(bf16[128,128]{1,0:T(8,128)(2,1)S(1)} %get-tuple-element.44.refs_0_), channel_id=1, source_target_pairs={{0,3},{1,2},{2,1},{3,0},{4,7},{5,6},{6,5},{7,4},{8,11},{9,10},{10,... | collective-permute-start | bytes 98312 | tf_op jit(solution)/shard_map/ppermute | solution.py:108
  36.0 3.9 %collective-permute-start.18 = (bf16[128,128]{1,0:T(8,128)(2,1)S(1)}, bf16[128,128]{1,0:T(8,128)(2,1)S(1)}, u32[]{:S(2)}, u32[]{:S(2)}) collective-permute-start(bf16[128,128]{1,0:T(8,128)(2,1)S(1)} %get-tuple-element.44.refs_0_), channel_id=1, source_target_pairs={{0,2},{1,3},{2,0},{3,1},{4,6},{5,7},{6,4},{7,5},{8,10},{9,11},{10,... | collective-permute-start | bytes 98312 | tf_op jit(solution)/shard_map/ppermute | solution.py:108
  40.0 6.4 %collective-permute-start.20 = (bf16[176,128]{1,0:T(8,128)(2,1)S(1)}, bf16[176,128]{1,0:T(8,128)(2,1)S(1)}, u32[]{:S(2)}, u32[]{:S(2)}) collective-permute-start(bf16[176,128]{1,0:T(8,128)(2,1)S(1)} %get-tuple-element.48), channel_id=1, source_target_pairs={{0,12},{4,8},{8,4},{12,0},{16,28},{20,24},{24,20},{28,16},{1,13},{... | collective-permute-start | bytes 135176 | tf_op jit(solution)/shard_map/ppermute | solution.py:108
  41.7 5.3 %collective-permute-start.21 = (bf16[176,128]{1,0:T(8,128)(2,1)S(1)}, bf16[176,128]{1,0:T(8,128)(2,1)S(1)}, u32[]{:S(2)}, u32[]{:S(2)}) collective-permute-start(bf16[176,128]{1,0:T(8,128)(2,1)S(1)} %get-tuple-element.49), channel_id=1, source_target_pairs={{0,8},{4,12},{8,0},{12,4},{16,24},{20,28},{24,16},{28,20},{1,9},{5... | collective-permute-start | bytes 135176 | tf_op jit(solution)/shard_map/ppermute | solution.py:108
  42.6 4.4 %collective-permute-start.22 = (bf16[176,128]{1,0:T(8,128)(2,1)S(1)}, bf16[176,128]{1,0:T(8,128)(2,1)S(1)}, u32[]{:S(2)}, u32[]{:S(2)}) collective-permute-start(bf16[176,128]{1,0:T(8,128)(2,1)S(1)} %get-tuple-element.50), channel_id=1, source_target_pairs={{0,4},{4,0},{8,12},{12,8},{16,20},{20,16},{24,28},{28,24},{1,5},{5... | collective-permute-start | bytes 135176 | tf_op jit(solution)/shard_map/ppermute | solution.py:108
  45.1 4.2 %collective-permute-start.24 = (f32[80,128]{1,0:T(8,128)S(1)}, f32[80,128]{1,0:T(8,128)S(1)}, u32[]{:S(2)}, u32[]{:S(2)}) collective-permute-start(f32[80,128]{1,0:T(8,128)S(1)} %get-tuple-element.56), channel_id=1, source_target_pairs={{0,3},{1,2},{2,1},{3,0},{4,7},{5,6},{6,5},{7,4},{8,11},{9,10},{10,... | collective-permute-start | bytes 122888 | tf_op jit(solution)/shard_map/ppermute | solution.py:108
  45.4 4.4 %collective-permute-start.25 = (f32[80,128]{1,0:T(8,128)S(1)}, f32[80,128]{1,0:T(8,128)S(1)}, u32[]{:S(2)}, u32[]{:S(2)}) collective-permute-start(f32[80,128]{1,0:T(8,128)S(1)} %get-tuple-element.57), channel_id=1, source_target_pairs={{0,2},{1,3},{2,0},{3,1},{4,6},{5,7},{6,4},{7,5},{8,10},{9,11},{10,... | collective-permute-start | bytes 122888 | tf_op jit(solution)/shard_map/ppermute | solution.py:108
  47.1 5.0 %collective-permute-start.23 = (bf16[160,128]{1,0:T(8,128)(2,1)S(1)}, bf16[160,128]{1,0:T(8,128)(2,1)S(1)}, u32[]{:S(2)}, u32[]{:S(2)}) collective-permute-start(bf16[160,128]{1,0:T(8,128)(2,1)S(1)} %get-tuple-element.60), channel_id=1, source_target_pairs={{0,16},{4,20},{8,24},{12,28},{16,0},{20,4},{24,8},{28,12},{1,17},{... | collective-permute-start | bytes 122888 | tf_op jit(solution)/shard_map/ppermute | solution.py:108
  (4 other events, 14.6 us)

commit v6 on v5

--- a/solution.py
+++ b/solution.py
@@ -262,27 +262,35 @@
     put_norm(col_ref, rows_i, squares(b16))
 
 
+def new_a_kernel(n_col, *refs):
+    cols, refs = refs[:n_col], refs[n_col:]
+    a_ref, c_ref, new_a, gram_a = refs
+    rows_i = a_ref.shape[0]
+    norm_c = squares(c_ref[...].astype(BF16))
+    step_a = scaling / (sum_norm(cols, rows_i) * norm_c + epsilon)
+    a2 = damping * a_ref[...] + step_a * sum_rows(cols, 0, rows_i)
+    new_a[...] = a2
+    gram_a[...] = gram(a2.astype(BF16))
+
+
 def middle_kernel(n_row, n_col, *refs):
     rows, refs = refs[:n_row], refs[n_row:]
     cols, refs = refs[:n_col], refs[n_col:]
-    a_ref, b_ref, c_ref, new_a, new_b, part_c, step_c = refs
-    rows_i, rows_j, depth = a_ref.shape[0], b_ref.shape[0], c_ref.shape[0]
+    b_ref, c_ref, new_b, part_c, step_c = refs
+    rows_j, depth = b_ref.shape[0], c_ref.shape[0]
     norm_a = sum_norm(rows, rows_j + depth)
-    norm_b = sum_norm(cols, rows_i)
+    norm_b = sum_norm(cols, cols[0].shape[0] - NORM_ROWS)
     norm_c = squares(c_ref[...].astype(BF16))
-    step_a = scaling / (norm_b * norm_c + epsilon)
     step_b = scaling / (norm_a * norm_c + epsilon)
-    new_a[...] = damping * a_ref[...] + step_a * sum_rows(cols, 0, rows_i)
     new_b[...] = damping * b_ref[...] + step_b * sum_rows(rows, 0, rows_j)
     part_c[...] = sum_rows(rows, rows_j, depth).astype(BF16)
     step_c[...] = jnp.broadcast_to(scaling / (norm_a * norm_b + epsilon), step_c.shape)
 
 
-def second_c_kernel(t_ref, a_ref, b_ref, sum_ref, gram_ref):
-    a16 = a_ref[...].astype(BF16)
+def second_c_kernel(t_ref, a_ref, b_ref, gram_a, sum_ref, gram_ref):
     b16 = b_ref[...].astype(BF16)
     sum_c(t_ref, a_ref, b16, sum_ref)
-    gram_ref[...] = gram(a16) * gram(b16)
+    gram_ref[...] = gram_a[...] * gram(b16)
 
 
 def second_model_kernel(n_col, *refs):
@@ -293,11 +301,10 @@
     out_ref[...] = (sum_ref[...] - dot_wide(c2.astype(BF16), gram_ref[...])).astype(BF16)
 
 
-def second_b_kernel(t_ref, a_ref, b_ref, c_ref, grad_b, low, high):
-    a16 = a_ref[...].astype(BF16)
+def second_b_kernel(t_ref, a_ref, b_ref, c_ref, gram_a, grad_b, low, high):
     c16 = c_ref[...].astype(BF16)
     sum_b(t_ref, a_ref, c16, grad_b, low, high)
-    grad_b[...] -= dot_wide(b_ref[...].astype(BF16), gram(a16) * gram(c16))
+    grad_b[...] -= dot_wide(b_ref[...].astype(BF16), gram_a[...] * gram(c16))
 
 
 def second_a_kernel(weight, own_i, low, high, a_ref, b_ref, c_ref, *refs):
@@ -363,21 +370,28 @@
     return parts
 
 
+def last_a_kernel(n_col, *refs):
+    cols, refs = refs[:n_col], refs[n_col:]
+    a_ref, c_ref, out_a = refs
+    own_i = out_a.shape[0]
+    norm_c = squares(c_ref[...].astype(BF16))
+    step_a = scaling / (sum_norm(cols, 0) * norm_c + epsilon)
+    at_i = pl.ds(pl.multiple_of(lax.axis_index("col") * own_i, own_i), own_i)
+    out_a[...] = damping * a_ref[at_i] + step_a * sum_rows(cols, NORM_ROWS, own_i)
+
+
 def last_kernel(n_row, n_col, *refs):
     rows, refs = refs[:n_row], refs[n_row:]
     cols, refs = refs[:n_col], refs[n_col:]
-    a_ref, b_ref, c_ref, out_a, out_b, out_c = refs
+    b_ref, c_ref, out_b, out_c = refs
     depth = c_ref.shape[0]
-    own_i, own_j = out_a.shape[0], out_b.shape[0]
+    own_j = out_b.shape[0]
     norm_a = sum_norm(rows, depth)
     norm_b = sum_norm(cols, 0)
     norm_c = squares(c_ref[...].astype(BF16))
-    step_a = scaling / (norm_b * norm_c + epsilon)
     step_b = scaling / (norm_a * norm_c + epsilon)
     step_c = scaling / (norm_a * norm_b + epsilon)
-    at_i = pl.ds(pl.multiple_of(lax.axis_index("col") * own_i, own_i), own_i)
     at_j = pl.ds(pl.multiple_of(lax.axis_index("row") * own_j, own_j), own_j)
-    out_a[...] = damping * a_ref[at_i] + step_a * sum_rows(cols, NORM_ROWS, own_i)
     out_b[...] = damping * b_ref[at_j] + step_b * sum_rows(rows, depth + NORM_ROWS, own_j)
     out_c[...] = damping * c_ref[...] + step_c * sum_rows(rows, 0, depth)
 
@@ -409,17 +423,22 @@
     )
     rows = sum_parts(to_row, "row", rows_j + depth, high_first=True)
     cols = sum_parts(to_col, "col", rows_i)
-    a, b, part_c, step_c = call(
+    a, gram_a = call(
+        functools.partial(new_a_kernel, len(cols)),
+        [(a.shape, F32), ((rank, rank), F32)],
+        *cols, a, c,
+    )
+    b, part_c, step_c = call(
         functools.partial(middle_kernel, len(rows), len(cols)),
-        [(a.shape, F32), (b.shape, F32), (c.shape, BF16), ((8, rank), F32)],
-        *rows, *cols, a, b, c,
+        [(b.shape, F32), (c.shape, BF16), ((8, rank), F32)],
+        *rows, *cols, b, c,
     )
 
     parts = sum_parts(part_c, "col")
     sum_t, gram_ab = call(
         second_c_kernel,
         [(c.shape, F32), ((rank, rank), F32)],
-        tensor, a, b,
+        tensor, a, b, gram_a,
         flops=2 * tensor.size * rank,
     )
     c, to_col = call(
@@ -429,7 +448,7 @@
     )
     parts = sum_parts(to_col, "col")
     grad_b, low, high = call(
-        second_b_kernel, [(b.shape, F32)] + kept, tensor, a, b, c, flops=2 * tensor.size * rank
+        second_b_kernel, [(b.shape, F32)] + kept, tensor, a, b, c, gram_a, flops=2 * tensor.size * rank
     )
     weight, radix = first_digit("row")
     to_row = call(
@@ -447,12 +466,19 @@
     )
     rows = sum_shares(to_row, "row", factor_b.shape[0], depth, to_col)
     cols = sum_shares(to_col, "col", factor_a.shape[0], 0)
-    return call(
+    (out_a,) = call(
+        functools.partial(last_a_kernel, len(cols)),
+        [(factor_a.shape, F32)],
+        *cols, a, c,
+        hbm_out=True,
+    )
+    out_b, out_c = call(
         functools.partial(last_kernel, len(rows), len(cols)),
-        [(factor_a.shape, F32), (factor_b.shape, F32), (c.shape, F32)],
-        *rows, *cols, a, b, c,
+        [(factor_b.shape, F32), (c.shape, F32)],
+        *rows, *cols, b, c,
         hbm_out=True,
     )
+    return (out_a, out_b, out_c)
 
 
 def solution(mesh):

time: 53 us -> 52.9 us (level)
  starting transfers between devices: 29.5 us -> 28.1 us
  Pallas kernels: 15.2 us -> 16 us
  waiting for transfers between devices: 7.3 us -> 7.83 us
    ppermute x27, starting transfers between devices: 29.5 us -> 28.1 us  [swap(): lax.ppermute(x, axis, [(i, i ^ q * weight) for i in range(lax.axis_size(a...]
    pallas_call x15 -> x17, Pallas kernels: 14.3 us -> 15.2 us  [call(): pl.pallas_call(body, in_specs=[whole] * len(operands), out_specs=[whole]...]
    ppermute x27, waiting for transfers between devices: 7.3 us -> 7.83 us  [swap(): lax.ppermute(x, axis, [(i, i ^ q * weight) for i in range(lax.axis_size(a...]
  transfers between devices with their start and end apart: 27 -> 27, of which waited for: 7 -> 10; matrix products, arithmetic and copies ran while one was open for 0% -> 0% of each run, Pallas kernels for 22% -> 24%
where the time goes in v6:
time: 52.9 us; the launch traced here: 52.7 us
  starting transfers between devices  28.1 us (53%)
  Pallas kernels  16 us (30%)
  waiting for transfers between devices  7.83 us (15%)
  between operations  0.76 us (1%)
    ppermute x27, starting transfers between devices, swap(): lax.ppermute(x, axis, [(i, i ^ q * weight) for i in range(lax.axis_size(a...  28.1 us
    pallas_call x17, Pallas kernels, call(): pl.pallas_call(body, in_specs=[whole] * len(operands), out_specs=[whole]...  15.2 us
    ppermute x27, waiting for transfers between devices, swap(): lax.ppermute(x, axis, [(i, i ^ q * weight) for i in range(lax.axis_size(a...  7.83 us
  transfers between devices with their start and end apart: 27, of which 10 were waited for; matrix products, arithmetic and copies ran while one was open for 0% of the time, Pallas kernels for 24%

profile of v6, /device:TPU:0, one launch (start us, length us, event | category | flops | bytes accessed | tf_op | source)
XLA Modules:
  0.0 52.7 jit_solution(5890545039214763505)
XLA Ops:
  0.6 4.0 %collective-permute-start.3 = (f32[16,128]{1,0:T(8,128)}, f32[16,128]{1,0:T(8,128)S(1)}, u32[]{:S(2)}, u32[]{:S(2)}) collective-permute-start(f32[16,128]{1,0:T(8,128)} %refs_1_.1), channel_id=1, source_target_pairs={{0,12},{4,8},{8,4},{12,0},{16,28},{20,24},{24,20},{28,16},{1,13},{... | collective-permute-start | bytes 24584 | tf_op jit(solution)/shard_map/ppermute | solution.py:108
  5.3 0.9 %shard_map.67 = (f32[64,128]{1,0:T(8,128)S(1)}, f32[16,128]{1,0:T(8,128)S(1)}, f32[128,128]{1,0:T(8,128)S(1)}) custom-call(f32[64,128]{1,0:T(8,128)} %refs_0_.1, f32[16,128]{1,0:T(8,128)} %refs_1_.1, f32[128,128]{1,0:T(8,128)} %refs_2_.1), custom_call_target="tpu_custom_call" | custom-call | flops 5000000000 | tf_op jit(solution)/shard_map/pallas_call | solution.py:155
  6.7 1.5 %collective-permute-start.1 = (f32[64,128]{1,0:T(8,128)S(1)}, f32[64,128]{1,0:T(8,128)S(1)}, u32[]{:S(2)}, u32[]{:S(2)}) collective-permute-start(f32[64,128]{1,0:T(8,128)S(1)} %get-tuple-element.35.refs_0_), channel_id=1, source_target_pairs={{0,2},{1,3},{2,0},{3,1},{4,6},{5,7},{6,4},{7,5},{8,10},{9,11},{10,... | collective-permute-start | bytes 98312 | tf_op jit(solution)/shard_map/ppermute | solution.py:108
  9.0 2.6 %collective-permute-start.6 = (f32[64,128]{1,0:T(8,128)S(1)}, f32[64,128]{1,0:T(8,128)S(1)}, u32[]{:S(2)}, u32[]{:S(2)}) collective-permute-start(f32[64,128]{1,0:T(8,128)S(1)} %shard_map.70.refs_0_), channel_id=1, source_target_pairs={{0,16},{4,20},{8,24},{12,28},{16,0},{20,4},{24,8},{28,12},{1,17},{... | collective-permute-start | bytes 98312 | tf_op jit(solution)/shard_map/ppermute | solution.py:108
  11.6 2.4 %shard_map.69 = (f32[128,128]{1,0:T(8,128)S(1)}, f32[128,128,128]{2,1,0:T(8,128)S(1)}, f32[128,128,128]{2,1,0:T(8,128)S(1)}) custom-call(bf16[256,128,128]{2,1,0:T(8,128)(2,1)S(1)} %copy-done, f32[256,128]{1,0:T(8,128)S(1)} %shard_map.68.a_ref.refs_4_, f32[128,128]{1,0:T(8,128)S(1)} %get-tuple-element.36.c_ref.refs_5_.refs_9_), custom_call_target="tpu_custom_call" | custom-call | flops 1073741824 | tf_op jit(solution)/shard_map/pallas_call | solution.py:30
  14.0 2.6 %shard_map.74.refs_0_ = bf16[272,128]{1,0:T(8,128)(2,1)S(1)} custom-call(bf16[256,128,128]{2,1,0:T(8,128)(2,1)S(1)} %copy-done, f32[256,128]{1,0:T(8,128)S(1)} %shard_map.68.a_ref.refs_4_, f32[128,128]{1,0:T(8,128)S(1)} %shard_map.71.b_ref.refs_8_, f32[128,128]{1,0:T(8,128)S(1)} %get-tuple-element.36.c_ref.refs_5_.refs_9_, ...), custom_call_target="tpu_custom_call" | custom-call | flops 1073741824 | tf_op jit(solution)/shard_map/pallas_call | solution.py:30
  16.6 2.5 %collective-permute-start.10 = (bf16[272,128]{1,0:T(8,128)(2,1)S(1)}, bf16[272,128]{1,0:T(8,128)(2,1)S(1)}, u32[]{:S(2)}, u32[]{:S(2)}) collective-permute-start(bf16[272,128]{1,0:T(8,128)(2,1)S(1)} %shard_map.74.refs_0_), channel_id=1, source_target_pairs={{0,16},{4,20},{8,24},{12,28},{16,0},{20,4},{24,8},{28,12},{1,17},{... | collective-permute-start | bytes 208904 | tf_op jit(solution)/shard_map/ppermute | solution.py:108
  19.1 1.5 %shard_map.72.refs_0_.refs_4_ = bf16[272,128]{1,0:T(8,128)(2,1)S(1)} custom-call(f32[128,128,128]{2,1,0:T(8,128)S(1)} %get-tuple-element.37.low, f32[128,128,128]{2,1,0:T(8,128)S(1)} %get-tuple-element.38.high, f32[256,128]{1,0:T(8,128)S(1)} %shard_map.68.a_ref.refs_4_, f32[128,128]{1,0:T(8,128)S(1)} %shard_map.71.b_ref.refs_8_, ...), custom_call_target="tpu_custom_call" | custom-call | flops 536870912 | tf_op jit(solution)/shard_map/pallas_call | solution.py:30
  20.7 1.6 %collective-permute-start.8 = (bf16[272,128]{1,0:T(8,128)(2,1)S(1)}, bf16[272,128]{1,0:T(8,128)(2,1)S(1)}, u32[]{:S(2)}, u32[]{:S(2)}) collective-permute-start(bf16[272,128]{1,0:T(8,128)(2,1)S(1)} %shard_map.72.refs_0_.refs_4_), channel_id=1, source_target_pairs={{0,2},{1,3},{2,0},{3,1},{4,6},{5,7},{6,4},{7,5},{8,10},{9,11},{10,... | collective-permute-start | bytes 208904 | tf_op jit(solution)/shard_map/ppermute | solution.py:108
  22.6 2.4 %collective-permute-start.11 = (bf16[272,128]{1,0:T(8,128)(2,1)S(1)}, bf16[272,128]{1,0:T(8,128)(2,1)S(1)}, u32[]{:S(2)}, u32[]{:S(2)}) collective-permute-start(bf16[272,128]{1,0:T(8,128)(2,1)S(1)} %shard_map.75.refs_0_), channel_id=1, source_target_pairs={{0,12},{4,8},{8,4},{12,0},{16,28},{20,24},{24,20},{28,16},{1,13},{... | collective-permute-start | bytes 208904 | tf_op jit(solution)/shard_map/ppermute | solution.py:108
  24.9 1.1 %collective-permute-start.12 = (bf16[272,128]{1,0:T(8,128)(2,1)S(1)}, bf16[272,128]{1,0:T(8,128)(2,1)S(1)}, u32[]{:S(2)}, u32[]{:S(2)}) collective-permute-start(bf16[272,128]{1,0:T(8,128)(2,1)S(1)} %shard_map.75.refs_0_), channel_id=1, source_target_pairs={{0,8},{4,12},{8,0},{12,4},{16,24},{20,28},{24,16},{28,20},{1,9},{5... | collective-permute-start | bytes 208904 | tf_op jit(solution)/shard_map/ppermute | solution.py:108
  26.9 1.0 %collective-permute-done.11.refs_1_ = bf16[272,128]{1,0:T(8,128)(2,1)S(1)} collective-permute-done((bf16[272,128]{1,0:T(8,128)(2,1)S(1)}, bf16[272,128]{1,0:T(8,128)(2,1)S(1)}, u32[]{:S(2)}, u32[]{:S(2)}) %collective-permute-start.11) | collective-permute-done | bytes 69664 | tf_op jit(solution)/shard_map/ppermute | solution.py:108
  27.9 1.9 %collective-permute-done.12.refs_2_ = bf16[272,128]{1,0:T(8,128)(2,1)S(1)} collective-permute-done((bf16[272,128]{1,0:T(8,128)(2,1)S(1)}, bf16[272,128]{1,0:T(8,128)(2,1)S(1)}, u32[]{:S(2)}, u32[]{:S(2)}) %collective-permute-start.12) | collective-permute-done | bytes 69664 | tf_op jit(solution)/shard_map/ppermute | solution.py:108
  30.5 1.4 %collective-permute-start.15 = (bf16[128,128]{1,0:T(8,128)(2,1)S(1)}, bf16[128,128]{1,0:T(8,128)(2,1)S(1)}, u32[]{:S(2)}, u32[]{:S(2)}) collective-permute-start(bf16[128,128]{1,0:T(8,128)(2,1)S(1)} %get-tuple-element.43.refs_0_), channel_id=1, source_target_pairs={{0,2},{1,3},{2,0},{3,1},{4,6},{5,7},{6,4},{7,5},{8,10},{9,11},{10,... | collective-permute-start | bytes 98312 | tf_op jit(solution)/shard_map/ppermute | solution.py:108
  32.3 2.4 %shard_map.77 = (f32[128,128]{1,0:T(8,128)S(1)}, f32[128,128]{1,0:T(8,128)S(1)}) custom-call(bf16[256,128,128]{2,1,0:T(8,128)(2,1)S(1)} %copy-done, f32[256,128]{1,0:T(8,128)S(1)} %get-tuple-element.40.a_ref.refs_4_, f32[128,128]{1,0:T(8,128)S(1)} %get-tuple-element.42.b_ref.refs_6_, f32[128,128]{1,0:T(8,128)S(1)} %get-tuple-element.45.gram_a), custom_call_target="tpu_custom_call" | custom-call | flops 1073741824 | tf_op jit(solution)/shard_map/pallas_call | solution.py:30
  34.9 1.0 %collective-permute-start.20 = (bf16[128,128]{1,0:T(8,128)(2,1)S(1)}, bf16[128,128]{1,0:T(8,128)(2,1)S(1)}, u32[]{:S(2)}, u32[]{:S(2)}) collective-permute-start(bf16[128,128]{1,0:T(8,128)(2,1)S(1)} %get-tuple-element.55.refs_0_), channel_id=1, source_target_pairs={{0,3},{1,2},{2,1},{3,0},{4,7},{5,6},{6,5},{7,4},{8,11},{9,10},{10,... | collective-permute-start | bytes 98312 | tf_op jit(solution)/shard_map/ppermute | solution.py:108
  36.9 2.7 %shard_map.79 = (f32[128,128]{1,0:T(8,128)S(1)}, f32[128,128,128]{2,1,0:T(8,128)S(1)}, f32[128,128,128]{2,1,0:T(8,128)S(1)}) custom-call(bf16[256,128,128]{2,1,0:T(8,128)(2,1)S(1)} %copy-done, f32[256,128]{1,0:T(8,128)S(1)} %get-tuple-element.40.a_ref.refs_4_, f32[128,128]{1,0:T(8,128)S(1)} %get-tuple-element.42.b_ref.refs_6_, ...), custom_call_target="tpu_custom_call" | custom-call | flops 1073741824 | tf_op jit(solution)/shard_map/pallas_call | solution.py:30
  39.9 1.6 %collective-permute-start.23 = (bf16[176,128]{1,0:T(8,128)(2,1)S(1)}, bf16[176,128]{1,0:T(8,128)(2,1)S(1)}, u32[]{:S(2)}, u32[]{:S(2)}) collective-permute-start(bf16[176,128]{1,0:T(8,128)(2,1)S(1)} %get-tuple-element.58), channel_id=1, source_target_pairs={{0,12},{4,8},{8,4},{12,0},{16,28},{20,24},{24,20},{28,16},{1,13},{... | collective-permute-start | bytes 135176 | tf_op jit(solution)/shard_map/ppermute | solution.py:108
  42.0 1.4 %collective-permute-start.25 = (bf16[176,128]{1,0:T(8,128)(2,1)S(1)}, bf16[176,128]{1,0:T(8,128)(2,1)S(1)}, u32[]{:S(2)}, u32[]{:S(2)}) collective-permute-start(bf16[176,128]{1,0:T(8,128)(2,1)S(1)} %get-tuple-element.60), channel_id=1, source_target_pairs={{0,4},{4,0},{8,12},{12,8},{16,20},{20,16},{24,28},{28,24},{1,5},{5... | collective-permute-start | bytes 135176 | tf_op jit(solution)/shard_map/ppermute | solution.py:108
  43.4 1.5 %shard_map.80 = (f32[80,128]{1,0:T(8,128)S(1)}, f32[80,128]{1,0:T(8,128)S(1)}, f32[80,128]{1,0:T(8,128)S(1)}, f32[80,128]{1,0:T(8,128)S(1)}) custom-call(f32[128,128,128]{2,1,0:T(8,128)S(1)} %get-tuple-element.49.low, f32[128,128,128]{2,1,0:T(8,128)S(1)} %get-tuple-element.50.high, f32[256,128]{1,0:T(8,128)S(1)} %get-tuple-element.40.a_ref.refs_4_, ...), custom_call_target="tpu_custom_call" | custom-call | flops 536870912 | tf_op jit(solution)/shard_map/pallas_call | solution.py:30
  45.2 1.0 %collective-permute-start.18 = (f32[80,128]{1,0:T(8,128)S(1)}, f32[80,128]{1,0:T(8,128)S(1)}, u32[]{:S(2)}, u32[]{:S(2)}) collective-permute-start(f32[80,128]{1,0:T(8,128)S(1)} %get-tuple-element.53), channel_id=1, source_target_pairs={{0,2},{1,3},{2,0},{3,1},{4,6},{5,7},{6,4},{7,5},{8,10},{9,11},{10,... | collective-permute-start | bytes 122888 | tf_op jit(solution)/shard_map/ppermute | solution.py:108
  47.0 1.5 %collective-permute-start.26 = (bf16[160,128]{1,0:T(8,128)(2,1)S(1)}, bf16[160,128]{1,0:T(8,128)(2,1)S(1)}, u32[]{:S(2)}, u32[]{:S(2)}) collective-permute-start(bf16[160,128]{1,0:T(8,128)(2,1)S(1)} %get-tuple-element.64), channel_id=1, source_target_pairs={{0,16},{4,20},{8,24},{12,28},{16,0},{20,4},{24,8},{28,12},{1,17},{... | collective-permute-start | bytes 122888 | tf_op jit(solution)/shard_map/ppermute | solution.py:108
  48.6 1.0 %collective-permute-done.18.refs_2_.refs_4_ = f32[80,128]{1,0:T(8,128)S(1)} collective-permute-done((f32[80,128]{1,0:T(8,128)S(1)}, f32[80,128]{1,0:T(8,128)S(1)}, u32[]{:S(2)}, u32[]{:S(2)}) %collective-permute-start.18) | collective-permute-done | bytes 40992 | tf_op jit(solution)/shard_map/ppermute | solution.py:108
  50.2 1.8 %collective-permute-done.26.refs_1_ = bf16[160,128]{1,0:T(8,128)(2,1)S(1)} collective-permute-done((bf16[160,128]{1,0:T(8,128)(2,1)S(1)}, bf16[160,128]{1,0:T(8,128)(2,1)S(1)}, u32[]{:S(2)}, u32[]{:S(2)}) %collective-permute-start.26) | collective-permute-done | bytes 40992 | tf_op jit(solution)/shard_map/ppermute | solution.py:108
  (50 shorter events, 8.8 us)
Async XLA Ops:
  0.6 7.6 %collective-permute-start.3 = (f32[16,128]{1,0:T(8,128)}, f32[16,128]{1,0:T(8,128)S(1)}, u32[]{:S(2)}, u32[]{:S(2)}) collective-permute-start(f32[16,128]{1,0:T(8,128)} %refs_1_.1), channel_id=1, source_target_pairs={{0,12},{4,8},{8,4},{12,0},{16,28},{20,24},{24,20},{28,16},{1,13},{... | collective-permute-start | bytes 24584 | tf_op jit(solution)/shard_map/ppermute | solution.py:108
  4.6 3.9 %collective-permute-start.4 = (f32[16,128]{1,0:T(8,128)}, f32[16,128]{1,0:T(8,128)S(1)}, u32[]{:S(2)}, u32[]{:S(2)}) collective-permute-start(f32[16,128]{1,0:T(8,128)} %refs_1_.1), channel_id=1, source_target_pairs={{0,8},{4,12},{8,0},{12,4},{16,24},{20,28},{24,16},{28,20},{1,9},{5... | collective-permute-start | bytes 24584 | tf_op jit(solution)/shard_map/ppermute | solution.py:108
  5.1 3.9 %collective-permute-start.5 = (f32[16,128]{1,0:T(8,128)}, f32[16,128]{1,0:T(8,128)S(1)}, u32[]{:S(2)}, u32[]{:S(2)}) collective-permute-start(f32[16,128]{1,0:T(8,128)} %refs_1_.1), channel_id=1, source_target_pairs={{0,4},{4,0},{8,12},{12,8},{16,20},{20,16},{24,28},{28,24},{1,5},{5... | collective-permute-start | bytes 24584 | tf_op jit(solution)/shard_map/ppermute | solution.py:108
  6.2 5.4 %collective-permute-start = (f32[64,128]{1,0:T(8,128)S(1)}, f32[64,128]{1,0:T(8,128)S(1)}, u32[]{:S(2)}, u32[]{:S(2)}) collective-permute-start(f32[64,128]{1,0:T(8,128)S(1)} %get-tuple-element.35.refs_0_), channel_id=1, source_target_pairs={{0,3},{1,2},{2,1},{3,0},{4,7},{5,6},{6,5},{7,4},{8,11},{9,10},{10,... | collective-permute-start | bytes 98312 | tf_op jit(solution)/shard_map/ppermute | solution.py:108
  6.7 4.9 %collective-permute-start.1 = (f32[64,128]{1,0:T(8,128)S(1)}, f32[64,128]{1,0:T(8,128)S(1)}, u32[]{:S(2)}, u32[]{:S(2)}) collective-permute-start(f32[64,128]{1,0:T(8,128)S(1)} %get-tuple-element.35.refs_0_), channel_id=1, source_target_pairs={{0,2},{1,3},{2,0},{3,1},{4,6},{5,7},{6,4},{7,5},{8,10},{9,11},{10,... | collective-permute-start | bytes 98312 | tf_op jit(solution)/shard_map/ppermute | solution.py:108
  8.2 3.4 %collective-permute-start.2 = (f32[64,128]{1,0:T(8,128)S(1)}, f32[64,128]{1,0:T(8,128)S(1)}, u32[]{:S(2)}, u32[]{:S(2)}) collective-permute-start(f32[64,128]{1,0:T(8,128)S(1)} %get-tuple-element.35.refs_0_), channel_id=1, source_target_pairs={{0,1},{1,0},{2,3},{3,2},{4,5},{5,4},{6,7},{7,6},{8,9},{9,8},{10,11... | collective-permute-start | bytes 98312 | tf_op jit(solution)/shard_map/ppermute | solution.py:108
  9.0 5.0 %collective-permute-start.6 = (f32[64,128]{1,0:T(8,128)S(1)}, f32[64,128]{1,0:T(8,128)S(1)}, u32[]{:S(2)}, u32[]{:S(2)}) collective-permute-start(f32[64,128]{1,0:T(8,128)S(1)} %shard_map.70.refs_0_), channel_id=1, source_target_pairs={{0,16},{4,20},{8,24},{12,28},{16,0},{20,4},{24,8},{28,12},{1,17},{... | collective-permute-start | bytes 98312 | tf_op jit(solution)/shard_map/ppermute | solution.py:108
  16.6 5.9 %collective-permute-start.10 = (bf16[272,128]{1,0:T(8,128)(2,1)S(1)}, bf16[272,128]{1,0:T(8,128)(2,1)S(1)}, u32[]{:S(2)}, u32[]{:S(2)}) collective-permute-start(bf16[272,128]{1,0:T(8,128)(2,1)S(1)} %shard_map.74.refs_0_), channel_id=1, source_target_pairs={{0,16},{4,20},{8,24},{12,28},{16,0},{20,4},{24,8},{28,12},{1,17},{... | collective-permute-start | bytes 208904 | tf_op jit(solution)/shard_map/ppermute | solution.py:108
  20.6 5.4 %collective-permute-start.7 = (bf16[272,128]{1,0:T(8,128)(2,1)S(1)}, bf16[272,128]{1,0:T(8,128)(2,1)S(1)}, u32[]{:S(2)}, u32[]{:S(2)}) collective-permute-start(bf16[272,128]{1,0:T(8,128)(2,1)S(1)} %shard_map.72.refs_0_.refs_4_), channel_id=1, source_target_pairs={{0,3},{1,2},{2,1},{3,0},{4,7},{5,6},{6,5},{7,4},{8,11},{9,10},{10,... | collective-permute-start | bytes 208904 | tf_op jit(solution)/shard_map/ppermute | solution.py:108
  20.7 6.0 %collective-permute-start.8 = (bf16[272,128]{1,0:T(8,128)(2,1)S(1)}, bf16[272,128]{1,0:T(8,128)(2,1)S(1)}, u32[]{:S(2)}, u32[]{:S(2)}) collective-permute-start(bf16[272,128]{1,0:T(8,128)(2,1)S(1)} %shard_map.72.refs_0_.refs_4_), channel_id=1, source_target_pairs={{0,2},{1,3},{2,0},{3,1},{4,6},{5,7},{6,4},{7,5},{8,10},{9,11},{10,... | collective-permute-start | bytes 208904 | tf_op jit(solution)/shard_map/ppermute | solution.py:108
  22.3 4.4 %collective-permute-start.9 = (bf16[272,128]{1,0:T(8,128)(2,1)S(1)}, bf16[272,128]{1,0:T(8,128)(2,1)S(1)}, u32[]{:S(2)}, u32[]{:S(2)}) collective-permute-start(bf16[272,128]{1,0:T(8,128)(2,1)S(1)} %shard_map.72.refs_0_.refs_4_), channel_id=1, source_target_pairs={{0,1},{1,0},{2,3},{3,2},{4,5},{5,4},{6,7},{7,6},{8,9},{9,8},{10,11... | collective-permute-start | bytes 208904 | tf_op jit(solution)/shard_map/ppermute | solution.py:108
  22.6 5.3 %collective-permute-start.11 = (bf16[272,128]{1,0:T(8,128)(2,1)S(1)}, bf16[272,128]{1,0:T(8,128)(2,1)S(1)}, u32[]{:S(2)}, u32[]{:S(2)}) collective-permute-start(bf16[272,128]{1,0:T(8,128)(2,1)S(1)} %shard_map.75.refs_0_), channel_id=1, source_target_pairs={{0,12},{4,8},{8,4},{12,0},{16,28},{20,24},{24,20},{28,16},{1,13},{... | collective-permute-start | bytes 208904 | tf_op jit(solution)/shard_map/ppermute | solution.py:108
  24.9 4.8 %collective-permute-start.12 = (bf16[272,128]{1,0:T(8,128)(2,1)S(1)}, bf16[272,128]{1,0:T(8,128)(2,1)S(1)}, u32[]{:S(2)}, u32[]{:S(2)}) collective-permute-start(bf16[272,128]{1,0:T(8,128)(2,1)S(1)} %shard_map.75.refs_0_), channel_id=1, source_target_pairs={{0,8},{4,12},{8,0},{12,4},{16,24},{20,28},{24,16},{28,20},{1,9},{5... | collective-permute-start | bytes 208904 | tf_op jit(solution)/shard_map/ppermute | solution.py:108
  26.0 4.3 %collective-permute-start.13 = (bf16[272,128]{1,0:T(8,128)(2,1)S(1)}, bf16[272,128]{1,0:T(8,128)(2,1)S(1)}, u32[]{:S(2)}, u32[]{:S(2)}) collective-permute-start(bf16[272,128]{1,0:T(8,128)(2,1)S(1)} %shard_map.75.refs_0_), channel_id=1, source_target_pairs={{0,4},{4,0},{8,12},{12,8},{16,20},{20,16},{24,28},{28,24},{1,5},{5... | collective-permute-start | bytes 208904 | tf_op jit(solution)/shard_map/ppermute | solution.py:108
  30.4 4.3 %collective-permute-start.14 = (bf16[128,128]{1,0:T(8,128)(2,1)S(1)}, bf16[128,128]{1,0:T(8,128)(2,1)S(1)}, u32[]{:S(2)}, u32[]{:S(2)}) collective-permute-start(bf16[128,128]{1,0:T(8,128)(2,1)S(1)} %get-tuple-element.43.refs_0_), channel_id=1, source_target_pairs={{0,3},{1,2},{2,1},{3,0},{4,7},{5,6},{6,5},{7,4},{8,11},{9,10},{10,... | collective-permute-start | bytes 98312 | tf_op jit(solution)/shard_map/ppermute | solution.py:108
  30.5 4.3 %collective-permute-start.15 = (bf16[128,128]{1,0:T(8,128)(2,1)S(1)}, bf16[128,128]{1,0:T(8,128)(2,1)S(1)}, u32[]{:S(2)}, u32[]{:S(2)}) collective-permute-start(bf16[128,128]{1,0:T(8,128)(2,1)S(1)} %get-tuple-element.43.refs_0_), channel_id=1, source_target_pairs={{0,2},{1,3},{2,0},{3,1},{4,6},{5,7},{6,4},{7,5},{8,10},{9,11},{10,... | collective-permute-start | bytes 98312 | tf_op jit(solution)/shard_map/ppermute | solution.py:108
  34.9 4.7 %collective-permute-start.20 = (bf16[128,128]{1,0:T(8,128)(2,1)S(1)}, bf16[128,128]{1,0:T(8,128)(2,1)S(1)}, u32[]{:S(2)}, u32[]{:S(2)}) collective-permute-start(bf16[128,128]{1,0:T(8,128)(2,1)S(1)} %get-tuple-element.55.refs_0_), channel_id=1, source_target_pairs={{0,3},{1,2},{2,1},{3,0},{4,7},{5,6},{6,5},{7,4},{8,11},{9,10},{10,... | collective-permute-start | bytes 98312 | tf_op jit(solution)/shard_map/ppermute | solution.py:108
  35.9 3.9 %collective-permute-start.21 = (bf16[128,128]{1,0:T(8,128)(2,1)S(1)}, bf16[128,128]{1,0:T(8,128)(2,1)S(1)}, u32[]{:S(2)}, u32[]{:S(2)}) collective-permute-start(bf16[128,128]{1,0:T(8,128)(2,1)S(1)} %get-tuple-element.55.refs_0_), channel_id=1, source_target_pairs={{0,2},{1,3},{2,0},{3,1},{4,6},{5,7},{6,4},{7,5},{8,10},{9,11},{10,... | collective-permute-start | bytes 98312 | tf_op jit(solution)/shard_map/ppermute | solution.py:108
  39.9 6.3 %collective-permute-start.23 = (bf16[176,128]{1,0:T(8,128)(2,1)S(1)}, bf16[176,128]{1,0:T(8,128)(2,1)S(1)}, u32[]{:S(2)}, u32[]{:S(2)}) collective-permute-start(bf16[176,128]{1,0:T(8,128)(2,1)S(1)} %get-tuple-element.58), channel_id=1, source_target_pairs={{0,12},{4,8},{8,4},{12,0},{16,28},{20,24},{24,20},{28,16},{1,13},{... | collective-permute-start | bytes 135176 | tf_op jit(solution)/shard_map/ppermute | solution.py:108
  41.5 5.4 %collective-permute-start.24 = (bf16[176,128]{1,0:T(8,128)(2,1)S(1)}, bf16[176,128]{1,0:T(8,128)(2,1)S(1)}, u32[]{:S(2)}, u32[]{:S(2)}) collective-permute-start(bf16[176,128]{1,0:T(8,128)(2,1)S(1)} %get-tuple-element.59), channel_id=1, source_target_pairs={{0,8},{4,12},{8,0},{12,4},{16,24},{20,28},{24,16},{28,20},{1,9},{5... | collective-permute-start | bytes 135176 | tf_op jit(solution)/shard_map/ppermute | solution.py:108
  42.0 4.9 %collective-permute-start.25 = (bf16[176,128]{1,0:T(8,128)(2,1)S(1)}, bf16[176,128]{1,0:T(8,128)(2,1)S(1)}, u32[]{:S(2)}, u32[]{:S(2)}) collective-permute-start(bf16[176,128]{1,0:T(8,128)(2,1)S(1)} %get-tuple-element.60), channel_id=1, source_target_pairs={{0,4},{4,0},{8,12},{12,8},{16,20},{20,16},{24,28},{28,24},{1,5},{5... | collective-permute-start | bytes 135176 | tf_op jit(solution)/shard_map/ppermute | solution.py:108
  45.0 3.6 %collective-permute-start.17 = (f32[80,128]{1,0:T(8,128)S(1)}, f32[80,128]{1,0:T(8,128)S(1)}, u32[]{:S(2)}, u32[]{:S(2)}) collective-permute-start(f32[80,128]{1,0:T(8,128)S(1)} %get-tuple-element.52), channel_id=1, source_target_pairs={{0,3},{1,2},{2,1},{3,0},{4,7},{5,6},{6,5},{7,4},{8,11},{9,10},{10,... | collective-permute-start | bytes 122888 | tf_op jit(solution)/shard_map/ppermute | solution.py:108
  45.2 4.4 %collective-permute-start.18 = (f32[80,128]{1,0:T(8,128)S(1)}, f32[80,128]{1,0:T(8,128)S(1)}, u32[]{:S(2)}, u32[]{:S(2)}) collective-permute-start(f32[80,128]{1,0:T(8,128)S(1)} %get-tuple-element.53), channel_id=1, source_target_pairs={{0,2},{1,3},{2,0},{3,1},{4,6},{5,7},{6,4},{7,5},{8,10},{9,11},{10,... | collective-permute-start | bytes 122888 | tf_op jit(solution)/shard_map/ppermute | solution.py:108
  47.0 5.1 %collective-permute-start.26 = (bf16[160,128]{1,0:T(8,128)(2,1)S(1)}, bf16[160,128]{1,0:T(8,128)(2,1)S(1)}, u32[]{:S(2)}, u32[]{:S(2)}) collective-permute-start(bf16[160,128]{1,0:T(8,128)(2,1)S(1)} %get-tuple-element.64), channel_id=1, source_target_pairs={{0,16},{4,20},{8,24},{12,28},{16,0},{20,4},{24,8},{28,12},{1,17},{... | collective-permute-start | bytes 122888 | tf_op jit(solution)/shard_map/ppermute | solution.py:108
  (4 other events, 14.9 us)

commit v7 on v6

--- a/solution.py
+++ b/solution.py
@@ -329,10 +329,17 @@
         out[depth + NORM_ROWS :] = jnp.concatenate(rows, 0).astype(out.dtype)
 
 
+def core_rows(rows, other=False):
+    core = digit_of("col", 1, 2)
+    return pl.ds(pl.multiple_of(((1 - core) if other else core) * rows, rows), rows)
+
+
 def shares_kernel(n_col, own_j, weight, *refs):
     parts, refs = refs[:n_col], refs[n_col:]
-    a_ref, grad_b, outs = refs[0], refs[1], refs[2:]
-    shared = sum_rows(parts, 0, parts[0].shape[0]).astype(BF16)
+    a_ref, grad_b, outs, total = refs[0], refs[1], refs[2:-1], refs[-1]
+    depth = total.shape[0]
+    total[...] = sum_rows(parts, 0, depth)
+    shared = total[core_rows(depth // 2)].astype(BF16)
     put_shares("row", weight, own_j, shared, squares(a_ref[...].astype(BF16)), grad_b, outs)
 
 
@@ -380,20 +387,28 @@
     out_a[...] = damping * a_ref[at_i] + step_a * sum_rows(cols, NORM_ROWS, own_i)
 
 
-def last_kernel(n_row, n_col, *refs):
+def half_kernel(n_row, n_col, *refs):
     rows, refs = refs[:n_row], refs[n_row:]
-    cols, refs = refs[:n_col], refs[n_col:]
-    b_ref, c_ref, out_b, out_c = refs
-    depth = c_ref.shape[0]
-    own_j = out_b.shape[0]
-    norm_a = sum_norm(rows, depth)
-    norm_b = sum_norm(cols, 0)
+    cols, (half, step_c) = refs[:n_col], refs[n_col:]
+    half[...] = sum_rows(rows, 0, half.shape[0])
+    norm = sum_norm(rows, half.shape[0]) * sum_norm(cols, 0)
+    step_c[...] = jnp.broadcast_to(scaling / (norm + epsilon), step_c.shape)
+
+
+def last_b_kernel(n_row, *refs):
+    rows, (b_ref, c_ref, out_b) = refs[:n_row], refs[n_row:]
+    depth, own_j = c_ref.shape[0] // 2, out_b.shape[0]
     norm_c = squares(c_ref[...].astype(BF16))
-    step_b = scaling / (norm_a * norm_c + epsilon)
-    step_c = scaling / (norm_a * norm_b + epsilon)
+    step_b = scaling / (sum_norm(rows, depth) * norm_c + epsilon)
     at_j = pl.ds(pl.multiple_of(lax.axis_index("row") * own_j, own_j), own_j)
     out_b[...] = damping * b_ref[at_j] + step_b * sum_rows(rows, depth + NORM_ROWS, own_j)
-    out_c[...] = damping * c_ref[...] + step_c * sum_rows(rows, 0, depth)
+
+
+def last_c_kernel(half, got, step_c, c_ref, out_c):
+    rows = half.shape[0]
+    for ref, other in ((half, False), (got, True)):
+        at = core_rows(rows, other)
+        out_c[at] = damping * c_ref[at] + step_c[0:1] * ref[...]
 
 
 def local(tensor, factor_a, factor_b, factor_c):
@@ -453,8 +468,9 @@
     weight, radix = first_digit("row")
     to_row = call(
         functools.partial(shares_kernel, len(parts), factor_b.shape[0], weight),
-        messages(depth, rows_j, rank, radix, BF16),
+        messages(depth // 2, rows_j, rank, radix, BF16),
         *parts, a, grad_b,
+        scratch=[pltpu.VMEM(c.shape, F32)],
     )
     weight, radix = first_digit("col")
     to_col = call(
@@ -464,7 +480,7 @@
         scratch=[pltpu.VMEM((rows_i, rank), F32)],
         flops=tensor.size * rank,
     )
-    rows = sum_shares(to_row, "row", factor_b.shape[0], depth, to_col)
+    rows = sum_shares(to_row, "row", factor_b.shape[0], depth // 2, to_col)
     cols = sum_shares(to_col, "col", factor_a.shape[0], 0)
     (out_a,) = call(
         functools.partial(last_a_kernel, len(cols)),
@@ -472,12 +488,19 @@
         *cols, a, c,
         hbm_out=True,
     )
-    out_b, out_c = call(
-        functools.partial(last_kernel, len(rows), len(cols)),
-        [(factor_b.shape, F32), (c.shape, F32)],
-        *rows, *cols, b, c,
+    half, step_c = call(
+        functools.partial(half_kernel, len(rows), len(cols)),
+        [((depth // 2, rank), F32), ((8, rank), F32)],
+        *rows, *cols,
+    )
+    got = swap(half, "col", 1, 1)
+    (out_b,) = call(
+        functools.partial(last_b_kernel, len(rows)),
+        [(factor_b.shape, F32)],
+        *rows, b, c,
         hbm_out=True,
     )
+    (out_c,) = call(last_c_kernel, [(c.shape, F32)], half, got, step_c, c, hbm_out=True)
     return (out_a, out_b, out_c)
 
 

time: 52.9 us -> 54 us (1.021)
  Pallas kernels: 16 us -> 16.7 us
    pallas_call x17 -> x19, Pallas kernels: 15.2 us -> 15.8 us  [call(): pl.pallas_call(body, in_specs=[whole] * len(operands), out_specs=[whole]...]
    ppermute x27 -> x28, waiting for transfers between devices: 7.83 us -> 8.22 us  [swap(): lax.ppermute(x, axis, [(i, i ^ q * weight) for i in range(lax.axis_size(a...]
    ppermute x27 -> x28, starting transfers between devices: 28.1 us -> 28.1 us  [swap(): lax.ppermute(x, axis, [(i, i ^ q * weight) for i in range(lax.axis_size(a...]
  transfers between devices with their start and end apart: 27 -> 28, of which waited for: 10 -> 10; matrix products, arithmetic and copies ran while one was open for 0% -> 0% of each run, Pallas kernels for 24% -> 24%
where the time goes in v7:
time: 54 us; the launch traced here: 53.8 us
  starting transfers between devices  28.1 us (52%)
  Pallas kernels  16.7 us (31%)
  waiting for transfers between devices  8.22 us (15%)
  between operations  0.77 us (1%)
    ppermute x28, starting transfers between devices, swap(): lax.ppermute(x, axis, [(i, i ^ q * weight) for i in range(lax.axis_size(a...  28.1 us
    pallas_call x19, Pallas kernels, call(): pl.pallas_call(body, in_specs=[whole] * len(operands), out_specs=[whole]...  15.8 us
    ppermute x28, waiting for transfers between devices, swap(): lax.ppermute(x, axis, [(i, i ^ q * weight) for i in range(lax.axis_size(a...  8.22 us
  transfers between devices with their start and end apart: 28, of which 10 were waited for; matrix products, arithmetic and copies ran while one was open for 0% of the time, Pallas kernels for 24%

profile of v7, /device:TPU:0, one launch (start us, length us, event | category | flops | bytes accessed | tf_op | source)
XLA Modules:
  0.0 53.8 jit_solution(1369701036457452120)
XLA Ops:
  0.6 4.0 %collective-permute-start.3 = (f32[16,128]{1,0:T(8,128)}, f32[16,128]{1,0:T(8,128)S(1)}, u32[]{:S(2)}, u32[]{:S(2)}) collective-permute-start(f32[16,128]{1,0:T(8,128)} %refs_1_.1), channel_id=1, source_target_pairs={{0,12},{4,8},{8,4},{12,0},{16,28},{20,24},{24,20},{28,16},{1,13},{... | collective-permute-start | bytes 24584 | tf_op jit(solution)/shard_map/ppermute | solution.py:108
  5.3 0.9 %shard_map.67 = (f32[64,128]{1,0:T(8,128)S(1)}, f32[16,128]{1,0:T(8,128)S(1)}, f32[128,128]{1,0:T(8,128)S(1)}) custom-call(f32[64,128]{1,0:T(8,128)} %refs_0_.1, f32[16,128]{1,0:T(8,128)} %refs_1_.1, f32[128,128]{1,0:T(8,128)} %refs_2_.1), custom_call_target="tpu_custom_call" | custom-call | flops 5000000000 | tf_op jit(solution)/shard_map/pallas_call | solution.py:155
  6.7 1.5 %collective-permute-start.1 = (f32[64,128]{1,0:T(8,128)S(1)}, f32[64,128]{1,0:T(8,128)S(1)}, u32[]{:S(2)}, u32[]{:S(2)}) collective-permute-start(f32[64,128]{1,0:T(8,128)S(1)} %get-tuple-element.35.refs_0_), channel_id=1, source_target_pairs={{0,2},{1,3},{2,0},{3,1},{4,6},{5,7},{6,4},{7,5},{8,10},{9,11},{10,... | collective-permute-start | bytes 98312 | tf_op jit(solution)/shard_map/ppermute | solution.py:108
  9.0 2.6 %collective-permute-start.6 = (f32[64,128]{1,0:T(8,128)S(1)}, f32[64,128]{1,0:T(8,128)S(1)}, u32[]{:S(2)}, u32[]{:S(2)}) collective-permute-start(f32[64,128]{1,0:T(8,128)S(1)} %shard_map.70.refs_0_), channel_id=1, source_target_pairs={{0,16},{4,20},{8,24},{12,28},{16,0},{20,4},{24,8},{28,12},{1,17},{... | collective-permute-start | bytes 98312 | tf_op jit(solution)/shard_map/ppermute | solution.py:108
  11.6 2.4 %shard_map.69 = (f32[128,128]{1,0:T(8,128)S(1)}, f32[128,128,128]{2,1,0:T(8,128)S(1)}, f32[128,128,128]{2,1,0:T(8,128)S(1)}) custom-call(bf16[256,128,128]{2,1,0:T(8,128)(2,1)S(1)} %copy-done, f32[256,128]{1,0:T(8,128)S(1)} %shard_map.68.a_ref.refs_4_, f32[128,128]{1,0:T(8,128)S(1)} %get-tuple-element.36.c_ref.refs_5_.refs_9_), custom_call_target="tpu_custom_call" | custom-call | flops 1073741824 | tf_op jit(solution)/shard_map/pallas_call | solution.py:30
  14.0 2.6 %shard_map.74.refs_0_ = bf16[272,128]{1,0:T(8,128)(2,1)S(1)} custom-call(bf16[256,128,128]{2,1,0:T(8,128)(2,1)S(1)} %copy-done, f32[256,128]{1,0:T(8,128)S(1)} %shard_map.68.a_ref.refs_4_, f32[128,128]{1,0:T(8,128)S(1)} %shard_map.71.b_ref.refs_8_, f32[128,128]{1,0:T(8,128)S(1)} %get-tuple-element.36.c_ref.refs_5_.refs_9_, ...), custom_call_target="tpu_custom_call" | custom-call | flops 1073741824 | tf_op jit(solution)/shard_map/pallas_call | solution.py:30
  16.6 2.5 %collective-permute-start.10 = (bf16[272,128]{1,0:T(8,128)(2,1)S(1)}, bf16[272,128]{1,0:T(8,128)(2,1)S(1)}, u32[]{:S(2)}, u32[]{:S(2)}) collective-permute-start(bf16[272,128]{1,0:T(8,128)(2,1)S(1)} %shard_map.74.refs_0_), channel_id=1, source_target_pairs={{0,16},{4,20},{8,24},{12,28},{16,0},{20,4},{24,8},{28,12},{1,17},{... | collective-permute-start | bytes 208904 | tf_op jit(solution)/shard_map/ppermute | solution.py:108
  19.1 1.5 %shard_map.72.refs_0_.refs_4_ = bf16[272,128]{1,0:T(8,128)(2,1)S(1)} custom-call(f32[128,128,128]{2,1,0:T(8,128)S(1)} %get-tuple-element.37.low, f32[128,128,128]{2,1,0:T(8,128)S(1)} %get-tuple-element.38.high, f32[256,128]{1,0:T(8,128)S(1)} %shard_map.68.a_ref.refs_4_, f32[128,128]{1,0:T(8,128)S(1)} %shard_map.71.b_ref.refs_8_, ...), custom_call_target="tpu_custom_call" | custom-call | flops 536870912 | tf_op jit(solution)/shard_map/pallas_call | solution.py:30
  20.7 1.6 %collective-permute-start.8 = (bf16[272,128]{1,0:T(8,128)(2,1)S(1)}, bf16[272,128]{1,0:T(8,128)(2,1)S(1)}, u32[]{:S(2)}, u32[]{:S(2)}) collective-permute-start(bf16[272,128]{1,0:T(8,128)(2,1)S(1)} %shard_map.72.refs_0_.refs_4_), channel_id=1, source_target_pairs={{0,2},{1,3},{2,0},{3,1},{4,6},{5,7},{6,4},{7,5},{8,10},{9,11},{10,... | collective-permute-start | bytes 208904 | tf_op jit(solution)/shard_map/ppermute | solution.py:108
  22.6 2.4 %collective-permute-start.11 = (bf16[272,128]{1,0:T(8,128)(2,1)S(1)}, bf16[272,128]{1,0:T(8,128)(2,1)S(1)}, u32[]{:S(2)}, u32[]{:S(2)}) collective-permute-start(bf16[272,128]{1,0:T(8,128)(2,1)S(1)} %shard_map.75.refs_0_), channel_id=1, source_target_pairs={{0,12},{4,8},{8,4},{12,0},{16,28},{20,24},{24,20},{28,16},{1,13},{... | collective-permute-start | bytes 208904 | tf_op jit(solution)/shard_map/ppermute | solution.py:108
  24.9 1.1 %collective-permute-start.12 = (bf16[272,128]{1,0:T(8,128)(2,1)S(1)}, bf16[272,128]{1,0:T(8,128)(2,1)S(1)}, u32[]{:S(2)}, u32[]{:S(2)}) collective-permute-start(bf16[272,128]{1,0:T(8,128)(2,1)S(1)} %shard_map.75.refs_0_), channel_id=1, source_target_pairs={{0,8},{4,12},{8,0},{12,4},{16,24},{20,28},{24,16},{28,20},{1,9},{5... | collective-permute-start | bytes 208904 | tf_op jit(solution)/shard_map/ppermute | solution.py:108
  26.9 1.0 %collective-permute-done.11.refs_1_ = bf16[272,128]{1,0:T(8,128)(2,1)S(1)} collective-permute-done((bf16[272,128]{1,0:T(8,128)(2,1)S(1)}, bf16[272,128]{1,0:T(8,128)(2,1)S(1)}, u32[]{:S(2)}, u32[]{:S(2)}) %collective-permute-start.11) | collective-permute-done | bytes 69664 | tf_op jit(solution)/shard_map/ppermute | solution.py:108
  27.9 1.9 %collective-permute-done.12.refs_2_ = bf16[272,128]{1,0:T(8,128)(2,1)S(1)} collective-permute-done((bf16[272,128]{1,0:T(8,128)(2,1)S(1)}, bf16[272,128]{1,0:T(8,128)(2,1)S(1)}, u32[]{:S(2)}, u32[]{:S(2)}) %collective-permute-start.12) | collective-permute-done | bytes 69664 | tf_op jit(solution)/shard_map/ppermute | solution.py:108
  30.5 1.4 %collective-permute-start.15 = (bf16[128,128]{1,0:T(8,128)(2,1)S(1)}, bf16[128,128]{1,0:T(8,128)(2,1)S(1)}, u32[]{:S(2)}, u32[]{:S(2)}) collective-permute-start(bf16[128,128]{1,0:T(8,128)(2,1)S(1)} %get-tuple-element.43.refs_0_), channel_id=1, source_target_pairs={{0,2},{1,3},{2,0},{3,1},{4,6},{5,7},{6,4},{7,5},{8,10},{9,11},{10,... | collective-permute-start | bytes 98312 | tf_op jit(solution)/shard_map/ppermute | solution.py:108
  32.3 2.4 %shard_map.77 = (f32[128,128]{1,0:T(8,128)S(1)}, f32[128,128]{1,0:T(8,128)S(1)}) custom-call(bf16[256,128,128]{2,1,0:T(8,128)(2,1)S(1)} %copy-done, f32[256,128]{1,0:T(8,128)S(1)} %get-tuple-element.40.a_ref.refs_4_, f32[128,128]{1,0:T(8,128)S(1)} %get-tuple-element.42.b_ref.refs_2_, f32[128,128]{1,0:T(8,128)S(1)} %get-tuple-element.45.gram_a), custom_call_target="tpu_custom_call" | custom-call | flops 1073741824 | tf_op jit(solution)/shard_map/pallas_call | solution.py:30
  34.9 1.0 %collective-permute-start.20 = (bf16[128,128]{1,0:T(8,128)(2,1)S(1)}, bf16[128,128]{1,0:T(8,128)(2,1)S(1)}, u32[]{:S(2)}, u32[]{:S(2)}) collective-permute-start(bf16[128,128]{1,0:T(8,128)(2,1)S(1)} %get-tuple-element.55.refs_0_), channel_id=1, source_target_pairs={{0,3},{1,2},{2,1},{3,0},{4,7},{5,6},{6,5},{7,4},{8,11},{9,10},{10,... | collective-permute-start | bytes 98312 | tf_op jit(solution)/shard_map/ppermute | solution.py:108
  36.9 2.7 %shard_map.79 = (f32[128,128]{1,0:T(8,128)S(1)}, f32[128,128,128]{2,1,0:T(8,128)S(1)}, f32[128,128,128]{2,1,0:T(8,128)S(1)}) custom-call(bf16[256,128,128]{2,1,0:T(8,128)(2,1)S(1)} %copy-done, f32[256,128]{1,0:T(8,128)S(1)} %get-tuple-element.40.a_ref.refs_4_, f32[128,128]{1,0:T(8,128)S(1)} %get-tuple-element.42.b_ref.refs_2_, ...), custom_call_target="tpu_custom_call" | custom-call | flops 1073741824 | tf_op jit(solution)/shard_map/pallas_call | solution.py:30
  39.9 1.6 %collective-permute-start.23 = (bf16[112,128]{1,0:T(8,128)(2,1)S(1)}, bf16[112,128]{1,0:T(8,128)(2,1)S(1)}, u32[]{:S(2)}, u32[]{:S(2)}) collective-permute-start(bf16[112,128]{1,0:T(8,128)(2,1)S(1)} %get-tuple-element.58), channel_id=1, source_target_pairs={{0,12},{4,8},{8,4},{12,0},{16,28},{20,24},{24,20},{28,16},{1,13},{... | collective-permute-start | bytes 86024 | tf_op jit(solution)/shard_map/ppermute | solution.py:108
  42.0 1.4 %collective-permute-start.25 = (bf16[112,128]{1,0:T(8,128)(2,1)S(1)}, bf16[112,128]{1,0:T(8,128)(2,1)S(1)}, u32[]{:S(2)}, u32[]{:S(2)}) collective-permute-start(bf16[112,128]{1,0:T(8,128)(2,1)S(1)} %get-tuple-element.60), channel_id=1, source_target_pairs={{0,4},{4,0},{8,12},{12,8},{16,20},{20,16},{24,28},{28,24},{1,5},{5... | collective-permute-start | bytes 86024 | tf_op jit(solution)/shard_map/ppermute | solution.py:108
  43.4 1.5 %shard_map.80 = (f32[80,128]{1,0:T(8,128)S(1)}, f32[80,128]{1,0:T(8,128)S(1)}, f32[80,128]{1,0:T(8,128)S(1)}, f32[80,128]{1,0:T(8,128)S(1)}) custom-call(f32[128,128,128]{2,1,0:T(8,128)S(1)} %get-tuple-element.49.low, f32[128,128,128]{2,1,0:T(8,128)S(1)} %get-tuple-element.50.high, f32[256,128]{1,0:T(8,128)S(1)} %get-tuple-element.40.a_ref.refs_4_, ...), custom_call_target="tpu_custom_call" | custom-call | flops 536870912 | tf_op jit(solution)/shard_map/pallas_call | solution.py:30
  45.2 1.0 %collective-permute-start.18 = (f32[80,128]{1,0:T(8,128)S(1)}, f32[80,128]{1,0:T(8,128)S(1)}, u32[]{:S(2)}, u32[]{:S(2)}) collective-permute-start(f32[80,128]{1,0:T(8,128)S(1)} %get-tuple-element.53), channel_id=1, source_target_pairs={{0,2},{1,3},{2,0},{3,1},{4,6},{5,7},{6,4},{7,5},{8,10},{9,11},{10,... | collective-permute-start | bytes 122888 | tf_op jit(solution)/shard_map/ppermute | solution.py:108
  47.0 1.5 %collective-permute-start.26 = (bf16[96,128]{1,0:T(8,128)(2,1)S(1)}, bf16[96,128]{1,0:T(8,128)(2,1)S(1)}, u32[]{:S(2)}, u32[]{:S(2)}) collective-permute-start(bf16[96,128]{1,0:T(8,128)(2,1)S(1)} %get-tuple-element.64), channel_id=1, source_target_pairs={{0,16},{4,20},{8,24},{12,28},{16,0},{20,4},{24,8},{28,12},{1,17},{... | collective-permute-start | bytes 73736 | tf_op jit(solution)/shard_map/ppermute | solution.py:108
  48.6 1.0 %collective-permute-done.18.refs_2_.refs_4_ = f32[80,128]{1,0:T(8,128)S(1)} collective-permute-done((f32[80,128]{1,0:T(8,128)S(1)}, f32[80,128]{1,0:T(8,128)S(1)}, u32[]{:S(2)}, u32[]{:S(2)}) %collective-permute-start.18) | collective-permute-done | bytes 40992 | tf_op jit(solution)/shard_map/ppermute | solution.py:108
  49.6 2.2 %collective-permute-done.26.refs_1_ = bf16[96,128]{1,0:T(8,128)(2,1)S(1)} collective-permute-done((bf16[96,128]{1,0:T(8,128)(2,1)S(1)}, bf16[96,128]{1,0:T(8,128)(2,1)S(1)}, u32[]{:S(2)}, u32[]{:S(2)}) %collective-permute-start.26) | collective-permute-done | bytes 24608 | tf_op jit(solution)/shard_map/ppermute | solution.py:108
  (54 shorter events, 9.5 us)
Async XLA Ops:
  0.6 7.6 %collective-permute-start.3 = (f32[16,128]{1,0:T(8,128)}, f32[16,128]{1,0:T(8,128)S(1)}, u32[]{:S(2)}, u32[]{:S(2)}) collective-permute-start(f32[16,128]{1,0:T(8,128)} %refs_1_.1), channel_id=1, source_target_pairs={{0,12},{4,8},{8,4},{12,0},{16,28},{20,24},{24,20},{28,16},{1,13},{... | collective-permute-start | bytes 24584 | tf_op jit(solution)/shard_map/ppermute | solution.py:108
  4.6 3.9 %collective-permute-start.4 = (f32[16,128]{1,0:T(8,128)}, f32[16,128]{1,0:T(8,128)S(1)}, u32[]{:S(2)}, u32[]{:S(2)}) collective-permute-start(f32[16,128]{1,0:T(8,128)} %refs_1_.1), channel_id=1, source_target_pairs={{0,8},{4,12},{8,0},{12,4},{16,24},{20,28},{24,16},{28,20},{1,9},{5... | collective-permute-start | bytes 24584 | tf_op jit(solution)/shard_map/ppermute | solution.py:108
  5.1 3.9 %collective-permute-start.5 = (f32[16,128]{1,0:T(8,128)}, f32[16,128]{1,0:T(8,128)S(1)}, u32[]{:S(2)}, u32[]{:S(2)}) collective-permute-start(f32[16,128]{1,0:T(8,128)} %refs_1_.1), channel_id=1, source_target_pairs={{0,4},{4,0},{8,12},{12,8},{16,20},{20,16},{24,28},{28,24},{1,5},{5... | collective-permute-start | bytes 24584 | tf_op jit(solution)/shard_map/ppermute | solution.py:108
  6.2 5.4 %collective-permute-start = (f32[64,128]{1,0:T(8,128)S(1)}, f32[64,128]{1,0:T(8,128)S(1)}, u32[]{:S(2)}, u32[]{:S(2)}) collective-permute-start(f32[64,128]{1,0:T(8,128)S(1)} %get-tuple-element.35.refs_0_), channel_id=1, source_target_pairs={{0,3},{1,2},{2,1},{3,0},{4,7},{5,6},{6,5},{7,4},{8,11},{9,10},{10,... | collective-permute-start | bytes 98312 | tf_op jit(solution)/shard_map/ppermute | solution.py:108
  6.7 4.9 %collective-permute-start.1 = (f32[64,128]{1,0:T(8,128)S(1)}, f32[64,128]{1,0:T(8,128)S(1)}, u32[]{:S(2)}, u32[]{:S(2)}) collective-permute-start(f32[64,128]{1,0:T(8,128)S(1)} %get-tuple-element.35.refs_0_), channel_id=1, source_target_pairs={{0,2},{1,3},{2,0},{3,1},{4,6},{5,7},{6,4},{7,5},{8,10},{9,11},{10,... | collective-permute-start | bytes 98312 | tf_op jit(solution)/shard_map/ppermute | solution.py:108
  8.2 3.4 %collective-permute-start.2 = (f32[64,128]{1,0:T(8,128)S(1)}, f32[64,128]{1,0:T(8,128)S(1)}, u32[]{:S(2)}, u32[]{:S(2)}) collective-permute-start(f32[64,128]{1,0:T(8,128)S(1)} %get-tuple-element.35.refs_0_), channel_id=1, source_target_pairs={{0,1},{1,0},{2,3},{3,2},{4,5},{5,4},{6,7},{7,6},{8,9},{9,8},{10,11... | collective-permute-start | bytes 98312 | tf_op jit(solution)/shard_map/ppermute | solution.py:108
  9.0 5.0 %collective-permute-start.6 = (f32[64,128]{1,0:T(8,128)S(1)}, f32[64,128]{1,0:T(8,128)S(1)}, u32[]{:S(2)}, u32[]{:S(2)}) collective-permute-start(f32[64,128]{1,0:T(8,128)S(1)} %shard_map.70.refs_0_), channel_id=1, source_target_pairs={{0,16},{4,20},{8,24},{12,28},{16,0},{20,4},{24,8},{28,12},{1,17},{... | collective-permute-start | bytes 98312 | tf_op jit(solution)/shard_map/ppermute | solution.py:108
  16.6 5.9 %collective-permute-start.10 = (bf16[272,128]{1,0:T(8,128)(2,1)S(1)}, bf16[272,128]{1,0:T(8,128)(2,1)S(1)}, u32[]{:S(2)}, u32[]{:S(2)}) collective-permute-start(bf16[272,128]{1,0:T(8,128)(2,1)S(1)} %shard_map.74.refs_0_), channel_id=1, source_target_pairs={{0,16},{4,20},{8,24},{12,28},{16,0},{20,4},{24,8},{28,12},{1,17},{... | collective-permute-start | bytes 208904 | tf_op jit(solution)/shard_map/ppermute | solution.py:108
  20.6 5.4 %collective-permute-start.7 = (bf16[272,128]{1,0:T(8,128)(2,1)S(1)}, bf16[272,128]{1,0:T(8,128)(2,1)S(1)}, u32[]{:S(2)}, u32[]{:S(2)}) collective-permute-start(bf16[272,128]{1,0:T(8,128)(2,1)S(1)} %shard_map.72.refs_0_.refs_4_), channel_id=1, source_target_pairs={{0,3},{1,2},{2,1},{3,0},{4,7},{5,6},{6,5},{7,4},{8,11},{9,10},{10,... | collective-permute-start | bytes 208904 | tf_op jit(solution)/shard_map/ppermute | solution.py:108
  20.7 6.0 %collective-permute-start.8 = (bf16[272,128]{1,0:T(8,128)(2,1)S(1)}, bf16[272,128]{1,0:T(8,128)(2,1)S(1)}, u32[]{:S(2)}, u32[]{:S(2)}) collective-permute-start(bf16[272,128]{1,0:T(8,128)(2,1)S(1)} %shard_map.72.refs_0_.refs_4_), channel_id=1, source_target_pairs={{0,2},{1,3},{2,0},{3,1},{4,6},{5,7},{6,4},{7,5},{8,10},{9,11},{10,... | collective-permute-start | bytes 208904 | tf_op jit(solution)/shard_map/ppermute | solution.py:108
  22.3 4.4 %collective-permute-start.9 = (bf16[272,128]{1,0:T(8,128)(2,1)S(1)}, bf16[272,128]{1,0:T(8,128)(2,1)S(1)}, u32[]{:S(2)}, u32[]{:S(2)}) collective-permute-start(bf16[272,128]{1,0:T(8,128)(2,1)S(1)} %shard_map.72.refs_0_.refs_4_), channel_id=1, source_target_pairs={{0,1},{1,0},{2,3},{3,2},{4,5},{5,4},{6,7},{7,6},{8,9},{9,8},{10,11... | collective-permute-start | bytes 208904 | tf_op jit(solution)/shard_map/ppermute | solution.py:108
  22.6 5.3 %collective-permute-start.11 = (bf16[272,128]{1,0:T(8,128)(2,1)S(1)}, bf16[272,128]{1,0:T(8,128)(2,1)S(1)}, u32[]{:S(2)}, u32[]{:S(2)}) collective-permute-start(bf16[272,128]{1,0:T(8,128)(2,1)S(1)} %shard_map.75.refs_0_), channel_id=1, source_target_pairs={{0,12},{4,8},{8,4},{12,0},{16,28},{20,24},{24,20},{28,16},{1,13},{... | collective-permute-start | bytes 208904 | tf_op jit(solution)/shard_map/ppermute | solution.py:108
  24.9 4.8 %collective-permute-start.12 = (bf16[272,128]{1,0:T(8,128)(2,1)S(1)}, bf16[272,128]{1,0:T(8,128)(2,1)S(1)}, u32[]{:S(2)}, u32[]{:S(2)}) collective-permute-start(bf16[272,128]{1,0:T(8,128)(2,1)S(1)} %shard_map.75.refs_0_), channel_id=1, source_target_pairs={{0,8},{4,12},{8,0},{12,4},{16,24},{20,28},{24,16},{28,20},{1,9},{5... | collective-permute-start | bytes 208904 | tf_op jit(solution)/shard_map/ppermute | solution.py:108
  26.0 4.3 %collective-permute-start.13 = (bf16[272,128]{1,0:T(8,128)(2,1)S(1)}, bf16[272,128]{1,0:T(8,128)(2,1)S(1)}, u32[]{:S(2)}, u32[]{:S(2)}) collective-permute-start(bf16[272,128]{1,0:T(8,128)(2,1)S(1)} %shard_map.75.refs_0_), channel_id=1, source_target_pairs={{0,4},{4,0},{8,12},{12,8},{16,20},{20,16},{24,28},{28,24},{1,5},{5... | collective-permute-start | bytes 208904 | tf_op jit(solution)/shard_map/ppermute | solution.py:108
  30.4 4.3 %collective-permute-start.14 = (bf16[128,128]{1,0:T(8,128)(2,1)S(1)}, bf16[128,128]{1,0:T(8,128)(2,1)S(1)}, u32[]{:S(2)}, u32[]{:S(2)}) collective-permute-start(bf16[128,128]{1,0:T(8,128)(2,1)S(1)} %get-tuple-element.43.refs_0_), channel_id=1, source_target_pairs={{0,3},{1,2},{2,1},{3,0},{4,7},{5,6},{6,5},{7,4},{8,11},{9,10},{10,... | collective-permute-start | bytes 98312 | tf_op jit(solution)/shard_map/ppermute | solution.py:108
  30.5 4.3 %collective-permute-start.15 = (bf16[128,128]{1,0:T(8,128)(2,1)S(1)}, bf16[128,128]{1,0:T(8,128)(2,1)S(1)}, u32[]{:S(2)}, u32[]{:S(2)}) collective-permute-start(bf16[128,128]{1,0:T(8,128)(2,1)S(1)} %get-tuple-element.43.refs_0_), channel_id=1, source_target_pairs={{0,2},{1,3},{2,0},{3,1},{4,6},{5,7},{6,4},{7,5},{8,10},{9,11},{10,... | collective-permute-start | bytes 98312 | tf_op jit(solution)/shard_map/ppermute | solution.py:108
  34.9 4.7 %collective-permute-start.20 = (bf16[128,128]{1,0:T(8,128)(2,1)S(1)}, bf16[128,128]{1,0:T(8,128)(2,1)S(1)}, u32[]{:S(2)}, u32[]{:S(2)}) collective-permute-start(bf16[128,128]{1,0:T(8,128)(2,1)S(1)} %get-tuple-element.55.refs_0_), channel_id=1, source_target_pairs={{0,3},{1,2},{2,1},{3,0},{4,7},{5,6},{6,5},{7,4},{8,11},{9,10},{10,... | collective-permute-start | bytes 98312 | tf_op jit(solution)/shard_map/ppermute | solution.py:108
  35.9 3.9 %collective-permute-start.21 = (bf16[128,128]{1,0:T(8,128)(2,1)S(1)}, bf16[128,128]{1,0:T(8,128)(2,1)S(1)}, u32[]{:S(2)}, u32[]{:S(2)}) collective-permute-start(bf16[128,128]{1,0:T(8,128)(2,1)S(1)} %get-tuple-element.55.refs_0_), channel_id=1, source_target_pairs={{0,2},{1,3},{2,0},{3,1},{4,6},{5,7},{6,4},{7,5},{8,10},{9,11},{10,... | collective-permute-start | bytes 98312 | tf_op jit(solution)/shard_map/ppermute | solution.py:108
  39.9 6.4 %collective-permute-start.23 = (bf16[112,128]{1,0:T(8,128)(2,1)S(1)}, bf16[112,128]{1,0:T(8,128)(2,1)S(1)}, u32[]{:S(2)}, u32[]{:S(2)}) collective-permute-start(bf16[112,128]{1,0:T(8,128)(2,1)S(1)} %get-tuple-element.58), channel_id=1, source_target_pairs={{0,12},{4,8},{8,4},{12,0},{16,28},{20,24},{24,20},{28,16},{1,13},{... | collective-permute-start | bytes 86024 | tf_op jit(solution)/shard_map/ppermute | solution.py:108
  41.5 5.4 %collective-permute-start.24 = (bf16[112,128]{1,0:T(8,128)(2,1)S(1)}, bf16[112,128]{1,0:T(8,128)(2,1)S(1)}, u32[]{:S(2)}, u32[]{:S(2)}) collective-permute-start(bf16[112,128]{1,0:T(8,128)(2,1)S(1)} %get-tuple-element.59), channel_id=1, source_target_pairs={{0,8},{4,12},{8,0},{12,4},{16,24},{20,28},{24,16},{28,20},{1,9},{5... | collective-permute-start | bytes 86024 | tf_op jit(solution)/shard_map/ppermute | solution.py:108
  42.0 4.9 %collective-permute-start.25 = (bf16[112,128]{1,0:T(8,128)(2,1)S(1)}, bf16[112,128]{1,0:T(8,128)(2,1)S(1)}, u32[]{:S(2)}, u32[]{:S(2)}) collective-permute-start(bf16[112,128]{1,0:T(8,128)(2,1)S(1)} %get-tuple-element.60), channel_id=1, source_target_pairs={{0,4},{4,0},{8,12},{12,8},{16,20},{20,16},{24,28},{28,24},{1,5},{5... | collective-permute-start | bytes 86024 | tf_op jit(solution)/shard_map/ppermute | solution.py:108
  45.0 3.6 %collective-permute-start.17 = (f32[80,128]{1,0:T(8,128)S(1)}, f32[80,128]{1,0:T(8,128)S(1)}, u32[]{:S(2)}, u32[]{:S(2)}) collective-permute-start(f32[80,128]{1,0:T(8,128)S(1)} %get-tuple-element.52), channel_id=1, source_target_pairs={{0,3},{1,2},{2,1},{3,0},{4,7},{5,6},{6,5},{7,4},{8,11},{9,10},{10,... | collective-permute-start | bytes 122888 | tf_op jit(solution)/shard_map/ppermute | solution.py:108
  45.2 4.3 %collective-permute-start.18 = (f32[80,128]{1,0:T(8,128)S(1)}, f32[80,128]{1,0:T(8,128)S(1)}, u32[]{:S(2)}, u32[]{:S(2)}) collective-permute-start(f32[80,128]{1,0:T(8,128)S(1)} %get-tuple-element.53), channel_id=1, source_target_pairs={{0,2},{1,3},{2,0},{3,1},{4,6},{5,7},{6,4},{7,5},{8,10},{9,11},{10,... | collective-permute-start | bytes 122888 | tf_op jit(solution)/shard_map/ppermute | solution.py:108
  47.0 4.8 %collective-permute-start.26 = (bf16[96,128]{1,0:T(8,128)(2,1)S(1)}, bf16[96,128]{1,0:T(8,128)(2,1)S(1)}, u32[]{:S(2)}, u32[]{:S(2)}) collective-permute-start(bf16[96,128]{1,0:T(8,128)(2,1)S(1)} %get-tuple-element.64), channel_id=1, source_target_pairs={{0,16},{4,20},{8,24},{12,28},{16,0},{20,4},{24,8},{28,12},{1,17},{... | collective-permute-start | bytes 73736 | tf_op jit(solution)/shard_map/ppermute | solution.py:108
  (5 other events, 16.2 us)

commit v8 on v6

--- a/solution.py
+++ b/solution.py
@@ -246,8 +246,8 @@
     a16 = a_ref[...].astype(BF16)
     b16 = b_ref[...].astype(BF16)
     c16 = c_ref[...].astype(BF16)
+    gram_a, gram_b, gram_c = gram(a16), gram(b16), gram(c16)
     sum_c(t_ref, a_ref, b16, acc_c)
-    gram_a, gram_b, gram_c = gram(a16), gram(b16), gram(c16)
     row_ref[:rows_j] = (acc_b[...] - dot_wide(b16, gram_a * gram_c)).astype(BF16)
     row_ref[rows_j : rows_j + depth] = (acc_c[...] - dot_wide(c16, gram_a * gram_b)).astype(BF16)
     put_norm(row_ref, rows_j + depth, squares(a16))
@@ -303,8 +303,9 @@
 
 def second_b_kernel(t_ref, a_ref, b_ref, c_ref, gram_a, grad_b, low, high):
     c16 = c_ref[...].astype(BF16)
+    model = dot_wide(b_ref[...].astype(BF16), gram_a[...] * gram(c16))
     sum_b(t_ref, a_ref, c16, grad_b, low, high)
-    grad_b[...] -= dot_wide(b_ref[...].astype(BF16), gram_a[...] * gram(c16))
+    grad_b[...] -= model
 
 
 def second_a_kernel(weight, own_i, low, high, a_ref, b_ref, c_ref, *refs):

time: 52.9 us -> 52.7 us (level)
  no operation moved by 1% of the time
where the time goes in v8:
time: 52.7 us; the launch traced here: 52.6 us
  starting transfers between devices  28.1 us (53%)
  Pallas kernels  15.9 us (30%)
  waiting for transfers between devices  7.81 us (15%)
  between operations  0.77 us (1%)
    ppermute x27, starting transfers between devices, swap(): lax.ppermute(x, axis, [(i, i ^ q * weight) for i in range(lax.axis_size(a...  28.1 us
    pallas_call x17, Pallas kernels, call(): pl.pallas_call(body, in_specs=[whole] * len(operands), out_specs=[whole]...  15 us
    ppermute x27, waiting for transfers between devices, swap(): lax.ppermute(x, axis, [(i, i ^ q * weight) for i in range(lax.axis_size(a...  7.81 us
  transfers between devices with their start and end apart: 27, of which 10 were waited for; matrix products, arithmetic and copies ran while one was open for 0% of the time, Pallas kernels for 24%

profile of v8, /device:TPU:0, one launch (start us, length us, event | category | flops | bytes accessed | tf_op | source)
XLA Modules:
  0.0 52.6 jit_solution(12562578575965226684)
XLA Ops:
  0.6 4.0 %collective-permute-start.3 = (f32[16,128]{1,0:T(8,128)}, f32[16,128]{1,0:T(8,128)S(1)}, u32[]{:S(2)}, u32[]{:S(2)}) collective-permute-start(f32[16,128]{1,0:T(8,128)} %refs_1_.1), channel_id=1, source_target_pairs={{0,12},{4,8},{8,4},{12,0},{16,28},{20,24},{24,20},{28,16},{1,13},{... | collective-permute-start | bytes 24584 | tf_op jit(solution)/shard_map/ppermute | solution.py:108
  5.3 0.9 %shard_map.67 = (f32[64,128]{1,0:T(8,128)S(1)}, f32[16,128]{1,0:T(8,128)S(1)}, f32[128,128]{1,0:T(8,128)S(1)}) custom-call(f32[64,128]{1,0:T(8,128)} %refs_0_.1, f32[16,128]{1,0:T(8,128)} %refs_1_.1, f32[128,128]{1,0:T(8,128)} %refs_2_.1), custom_call_target="tpu_custom_call" | custom-call | flops 5000000000 | tf_op jit(solution)/shard_map/pallas_call | solution.py:155
  6.7 1.5 %collective-permute-start.1 = (f32[64,128]{1,0:T(8,128)S(1)}, f32[64,128]{1,0:T(8,128)S(1)}, u32[]{:S(2)}, u32[]{:S(2)}) collective-permute-start(f32[64,128]{1,0:T(8,128)S(1)} %get-tuple-element.35.refs_0_), channel_id=1, source_target_pairs={{0,2},{1,3},{2,0},{3,1},{4,6},{5,7},{6,4},{7,5},{8,10},{9,11},{10,... | collective-permute-start | bytes 98312 | tf_op jit(solution)/shard_map/ppermute | solution.py:108
  9.0 2.6 %collective-permute-start.6 = (f32[64,128]{1,0:T(8,128)S(1)}, f32[64,128]{1,0:T(8,128)S(1)}, u32[]{:S(2)}, u32[]{:S(2)}) collective-permute-start(f32[64,128]{1,0:T(8,128)S(1)} %shard_map.70.refs_0_), channel_id=1, source_target_pairs={{0,16},{4,20},{8,24},{12,28},{16,0},{20,4},{24,8},{28,12},{1,17},{... | collective-permute-start | bytes 98312 | tf_op jit(solution)/shard_map/ppermute | solution.py:108
  11.6 2.4 %shard_map.69 = (f32[128,128]{1,0:T(8,128)S(1)}, f32[128,128,128]{2,1,0:T(8,128)S(1)}, f32[128,128,128]{2,1,0:T(8,128)S(1)}) custom-call(bf16[256,128,128]{2,1,0:T(8,128)(2,1)S(1)} %copy-done, f32[256,128]{1,0:T(8,128)S(1)} %shard_map.68.a_ref.refs_4_, f32[128,128]{1,0:T(8,128)S(1)} %get-tuple-element.36.c_ref.refs_5_.refs_9_), custom_call_target="tpu_custom_call" | custom-call | flops 1073741824 | tf_op jit(solution)/shard_map/pallas_call | solution.py:30
  14.0 2.5 %shard_map.74.refs_0_ = bf16[272,128]{1,0:T(8,128)(2,1)S(1)} custom-call(bf16[256,128,128]{2,1,0:T(8,128)(2,1)S(1)} %copy-done, f32[256,128]{1,0:T(8,128)S(1)} %shard_map.68.a_ref.refs_4_, f32[128,128]{1,0:T(8,128)S(1)} %shard_map.71.b_ref.refs_8_, f32[128,128]{1,0:T(8,128)S(1)} %get-tuple-element.36.c_ref.refs_5_.refs_9_, ...), custom_call_target="tpu_custom_call" | custom-call | flops 1073741824 | tf_op jit(solution)/shard_map/pallas_call | solution.py:30
  16.5 2.5 %collective-permute-start.10 = (bf16[272,128]{1,0:T(8,128)(2,1)S(1)}, bf16[272,128]{1,0:T(8,128)(2,1)S(1)}, u32[]{:S(2)}, u32[]{:S(2)}) collective-permute-start(bf16[272,128]{1,0:T(8,128)(2,1)S(1)} %shard_map.74.refs_0_), channel_id=1, source_target_pairs={{0,16},{4,20},{8,24},{12,28},{16,0},{20,4},{24,8},{28,12},{1,17},{... | collective-permute-start | bytes 208904 | tf_op jit(solution)/shard_map/ppermute | solution.py:108
  18.9 1.5 %shard_map.72.refs_0_.refs_4_ = bf16[272,128]{1,0:T(8,128)(2,1)S(1)} custom-call(f32[128,128,128]{2,1,0:T(8,128)S(1)} %get-tuple-element.37.low, f32[128,128,128]{2,1,0:T(8,128)S(1)} %get-tuple-element.38.high, f32[256,128]{1,0:T(8,128)S(1)} %shard_map.68.a_ref.refs_4_, f32[128,128]{1,0:T(8,128)S(1)} %shard_map.71.b_ref.refs_8_, ...), custom_call_target="tpu_custom_call" | custom-call | flops 536870912 | tf_op jit(solution)/shard_map/pallas_call | solution.py:30
  20.6 1.6 %collective-permute-start.8 = (bf16[272,128]{1,0:T(8,128)(2,1)S(1)}, bf16[272,128]{1,0:T(8,128)(2,1)S(1)}, u32[]{:S(2)}, u32[]{:S(2)}) collective-permute-start(bf16[272,128]{1,0:T(8,128)(2,1)S(1)} %shard_map.72.refs_0_.refs_4_), channel_id=1, source_target_pairs={{0,2},{1,3},{2,0},{3,1},{4,6},{5,7},{6,4},{7,5},{8,10},{9,11},{10,... | collective-permute-start | bytes 208904 | tf_op jit(solution)/shard_map/ppermute | solution.py:108
  22.4 2.4 %collective-permute-start.11 = (bf16[272,128]{1,0:T(8,128)(2,1)S(1)}, bf16[272,128]{1,0:T(8,128)(2,1)S(1)}, u32[]{:S(2)}, u32[]{:S(2)}) collective-permute-start(bf16[272,128]{1,0:T(8,128)(2,1)S(1)} %shard_map.75.refs_0_), channel_id=1, source_target_pairs={{0,12},{4,8},{8,4},{12,0},{16,28},{20,24},{24,20},{28,16},{1,13},{... | collective-permute-start | bytes 208904 | tf_op jit(solution)/shard_map/ppermute | solution.py:108
  24.8 1.1 %collective-permute-start.12 = (bf16[272,128]{1,0:T(8,128)(2,1)S(1)}, bf16[272,128]{1,0:T(8,128)(2,1)S(1)}, u32[]{:S(2)}, u32[]{:S(2)}) collective-permute-start(bf16[272,128]{1,0:T(8,128)(2,1)S(1)} %shard_map.75.refs_0_), channel_id=1, source_target_pairs={{0,8},{4,12},{8,0},{12,4},{16,24},{20,28},{24,16},{28,20},{1,9},{5... | collective-permute-start | bytes 208904 | tf_op jit(solution)/shard_map/ppermute | solution.py:108
  26.8 1.0 %collective-permute-done.11.refs_1_ = bf16[272,128]{1,0:T(8,128)(2,1)S(1)} collective-permute-done((bf16[272,128]{1,0:T(8,128)(2,1)S(1)}, bf16[272,128]{1,0:T(8,128)(2,1)S(1)}, u32[]{:S(2)}, u32[]{:S(2)}) %collective-permute-start.11) | collective-permute-done | bytes 69664 | tf_op jit(solution)/shard_map/ppermute | solution.py:108
  27.7 1.9 %collective-permute-done.12.refs_2_ = bf16[272,128]{1,0:T(8,128)(2,1)S(1)} collective-permute-done((bf16[272,128]{1,0:T(8,128)(2,1)S(1)}, bf16[272,128]{1,0:T(8,128)(2,1)S(1)}, u32[]{:S(2)}, u32[]{:S(2)}) %collective-permute-start.12) | collective-permute-done | bytes 69664 | tf_op jit(solution)/shard_map/ppermute | solution.py:108
  30.3 1.4 %collective-permute-start.15 = (bf16[128,128]{1,0:T(8,128)(2,1)S(1)}, bf16[128,128]{1,0:T(8,128)(2,1)S(1)}, u32[]{:S(2)}, u32[]{:S(2)}) collective-permute-start(bf16[128,128]{1,0:T(8,128)(2,1)S(1)} %get-tuple-element.43.refs_0_), channel_id=1, source_target_pairs={{0,2},{1,3},{2,0},{3,1},{4,6},{5,7},{6,4},{7,5},{8,10},{9,11},{10,... | collective-permute-start | bytes 98312 | tf_op jit(solution)/shard_map/ppermute | solution.py:108
  32.2 2.4 %shard_map.77 = (f32[128,128]{1,0:T(8,128)S(1)}, f32[128,128]{1,0:T(8,128)S(1)}) custom-call(bf16[256,128,128]{2,1,0:T(8,128)(2,1)S(1)} %copy-done, f32[256,128]{1,0:T(8,128)S(1)} %get-tuple-element.40.a_ref.refs_4_, f32[128,128]{1,0:T(8,128)S(1)} %get-tuple-element.42.b_ref.refs_6_, f32[128,128]{1,0:T(8,128)S(1)} %get-tuple-element.45.gram_a), custom_call_target="tpu_custom_call" | custom-call | flops 1073741824 | tf_op jit(solution)/shard_map/pallas_call | solution.py:30
  34.8 1.0 %collective-permute-start.20 = (bf16[128,128]{1,0:T(8,128)(2,1)S(1)}, bf16[128,128]{1,0:T(8,128)(2,1)S(1)}, u32[]{:S(2)}, u32[]{:S(2)}) collective-permute-start(bf16[128,128]{1,0:T(8,128)(2,1)S(1)} %get-tuple-element.55.refs_0_), channel_id=1, source_target_pairs={{0,3},{1,2},{2,1},{3,0},{4,7},{5,6},{6,5},{7,4},{8,11},{9,10},{10,... | collective-permute-start | bytes 98312 | tf_op jit(solution)/shard_map/ppermute | solution.py:108
  36.7 2.7 %shard_map.79 = (f32[128,128]{1,0:T(8,128)S(1)}, f32[128,128,128]{2,1,0:T(8,128)S(1)}, f32[128,128,128]{2,1,0:T(8,128)S(1)}) custom-call(bf16[256,128,128]{2,1,0:T(8,128)(2,1)S(1)} %copy-done, f32[256,128]{1,0:T(8,128)S(1)} %get-tuple-element.40.a_ref.refs_4_, f32[128,128]{1,0:T(8,128)S(1)} %get-tuple-element.42.b_ref.refs_6_, ...), custom_call_target="tpu_custom_call" | custom-call | flops 1073741824 | tf_op jit(solution)/shard_map/pallas_call | solution.py:30
  39.8 1.6 %collective-permute-start.23 = (bf16[176,128]{1,0:T(8,128)(2,1)S(1)}, bf16[176,128]{1,0:T(8,128)(2,1)S(1)}, u32[]{:S(2)}, u32[]{:S(2)}) collective-permute-start(bf16[176,128]{1,0:T(8,128)(2,1)S(1)} %get-tuple-element.58), channel_id=1, source_target_pairs={{0,12},{4,8},{8,4},{12,0},{16,28},{20,24},{24,20},{28,16},{1,13},{... | collective-permute-start | bytes 135176 | tf_op jit(solution)/shard_map/ppermute | solution.py:108
  41.9 1.4 %collective-permute-start.25 = (bf16[176,128]{1,0:T(8,128)(2,1)S(1)}, bf16[176,128]{1,0:T(8,128)(2,1)S(1)}, u32[]{:S(2)}, u32[]{:S(2)}) collective-permute-start(bf16[176,128]{1,0:T(8,128)(2,1)S(1)} %get-tuple-element.60), channel_id=1, source_target_pairs={{0,4},{4,0},{8,12},{12,8},{16,20},{20,16},{24,28},{28,24},{1,5},{5... | collective-permute-start | bytes 135176 | tf_op jit(solution)/shard_map/ppermute | solution.py:108
  43.3 1.5 %shard_map.80 = (f32[80,128]{1,0:T(8,128)S(1)}, f32[80,128]{1,0:T(8,128)S(1)}, f32[80,128]{1,0:T(8,128)S(1)}, f32[80,128]{1,0:T(8,128)S(1)}) custom-call(f32[128,128,128]{2,1,0:T(8,128)S(1)} %get-tuple-element.49.low, f32[128,128,128]{2,1,0:T(8,128)S(1)} %get-tuple-element.50.high, f32[256,128]{1,0:T(8,128)S(1)} %get-tuple-element.40.a_ref.refs_4_, ...), custom_call_target="tpu_custom_call" | custom-call | flops 536870912 | tf_op jit(solution)/shard_map/pallas_call | solution.py:30
  45.1 1.0 %collective-permute-start.18 = (f32[80,128]{1,0:T(8,128)S(1)}, f32[80,128]{1,0:T(8,128)S(1)}, u32[]{:S(2)}, u32[]{:S(2)}) collective-permute-start(f32[80,128]{1,0:T(8,128)S(1)} %get-tuple-element.53), channel_id=1, source_target_pairs={{0,2},{1,3},{2,0},{3,1},{4,6},{5,7},{6,4},{7,5},{8,10},{9,11},{10,... | collective-permute-start | bytes 122888 | tf_op jit(solution)/shard_map/ppermute | solution.py:108
  46.8 1.5 %collective-permute-start.26 = (bf16[160,128]{1,0:T(8,128)(2,1)S(1)}, bf16[160,128]{1,0:T(8,128)(2,1)S(1)}, u32[]{:S(2)}, u32[]{:S(2)}) collective-permute-start(bf16[160,128]{1,0:T(8,128)(2,1)S(1)} %get-tuple-element.64), channel_id=1, source_target_pairs={{0,16},{4,20},{8,24},{12,28},{16,0},{20,4},{24,8},{28,12},{1,17},{... | collective-permute-start | bytes 122888 | tf_op jit(solution)/shard_map/ppermute | solution.py:108
  48.5 1.0 %collective-permute-done.18.refs_2_.refs_4_ = f32[80,128]{1,0:T(8,128)S(1)} collective-permute-done((f32[80,128]{1,0:T(8,128)S(1)}, f32[80,128]{1,0:T(8,128)S(1)}, u32[]{:S(2)}, u32[]{:S(2)}) %collective-permute-start.18) | collective-permute-done | bytes 40992 | tf_op jit(solution)/shard_map/ppermute | solution.py:108
  50.1 1.8 %collective-permute-done.26.refs_1_ = bf16[160,128]{1,0:T(8,128)(2,1)S(1)} collective-permute-done((bf16[160,128]{1,0:T(8,128)(2,1)S(1)}, bf16[160,128]{1,0:T(8,128)(2,1)S(1)}, u32[]{:S(2)}, u32[]{:S(2)}) %collective-permute-start.26) | collective-permute-done | bytes 40992 | tf_op jit(solution)/shard_map/ppermute | solution.py:108
  (50 shorter events, 8.8 us)
Async XLA Ops:
  0.6 7.6 %collective-permute-start.3 = (f32[16,128]{1,0:T(8,128)}, f32[16,128]{1,0:T(8,128)S(1)}, u32[]{:S(2)}, u32[]{:S(2)}) collective-permute-start(f32[16,128]{1,0:T(8,128)} %refs_1_.1), channel_id=1, source_target_pairs={{0,12},{4,8},{8,4},{12,0},{16,28},{20,24},{24,20},{28,16},{1,13},{... | collective-permute-start | bytes 24584 | tf_op jit(solution)/shard_map/ppermute | solution.py:108
  4.6 3.9 %collective-permute-start.4 = (f32[16,128]{1,0:T(8,128)}, f32[16,128]{1,0:T(8,128)S(1)}, u32[]{:S(2)}, u32[]{:S(2)}) collective-permute-start(f32[16,128]{1,0:T(8,128)} %refs_1_.1), channel_id=1, source_target_pairs={{0,8},{4,12},{8,0},{12,4},{16,24},{20,28},{24,16},{28,20},{1,9},{5... | collective-permute-start | bytes 24584 | tf_op jit(solution)/shard_map/ppermute | solution.py:108
  5.1 3.9 %collective-permute-start.5 = (f32[16,128]{1,0:T(8,128)}, f32[16,128]{1,0:T(8,128)S(1)}, u32[]{:S(2)}, u32[]{:S(2)}) collective-permute-start(f32[16,128]{1,0:T(8,128)} %refs_1_.1), channel_id=1, source_target_pairs={{0,4},{4,0},{8,12},{12,8},{16,20},{20,16},{24,28},{28,24},{1,5},{5... | collective-permute-start | bytes 24584 | tf_op jit(solution)/shard_map/ppermute | solution.py:108
  6.2 5.4 %collective-permute-start = (f32[64,128]{1,0:T(8,128)S(1)}, f32[64,128]{1,0:T(8,128)S(1)}, u32[]{:S(2)}, u32[]{:S(2)}) collective-permute-start(f32[64,128]{1,0:T(8,128)S(1)} %get-tuple-element.35.refs_0_), channel_id=1, source_target_pairs={{0,3},{1,2},{2,1},{3,0},{4,7},{5,6},{6,5},{7,4},{8,11},{9,10},{10,... | collective-permute-start | bytes 98312 | tf_op jit(solution)/shard_map/ppermute | solution.py:108
  6.7 4.9 %collective-permute-start.1 = (f32[64,128]{1,0:T(8,128)S(1)}, f32[64,128]{1,0:T(8,128)S(1)}, u32[]{:S(2)}, u32[]{:S(2)}) collective-permute-start(f32[64,128]{1,0:T(8,128)S(1)} %get-tuple-element.35.refs_0_), channel_id=1, source_target_pairs={{0,2},{1,3},{2,0},{3,1},{4,6},{5,7},{6,4},{7,5},{8,10},{9,11},{10,... | collective-permute-start | bytes 98312 | tf_op jit(solution)/shard_map/ppermute | solution.py:108
  8.2 3.4 %collective-permute-start.2 = (f32[64,128]{1,0:T(8,128)S(1)}, f32[64,128]{1,0:T(8,128)S(1)}, u32[]{:S(2)}, u32[]{:S(2)}) collective-permute-start(f32[64,128]{1,0:T(8,128)S(1)} %get-tuple-element.35.refs_0_), channel_id=1, source_target_pairs={{0,1},{1,0},{2,3},{3,2},{4,5},{5,4},{6,7},{7,6},{8,9},{9,8},{10,11... | collective-permute-start | bytes 98312 | tf_op jit(solution)/shard_map/ppermute | solution.py:108
  9.0 5.0 %collective-permute-start.6 = (f32[64,128]{1,0:T(8,128)S(1)}, f32[64,128]{1,0:T(8,128)S(1)}, u32[]{:S(2)}, u32[]{:S(2)}) collective-permute-start(f32[64,128]{1,0:T(8,128)S(1)} %shard_map.70.refs_0_), channel_id=1, source_target_pairs={{0,16},{4,20},{8,24},{12,28},{16,0},{20,4},{24,8},{28,12},{1,17},{... | collective-permute-start | bytes 98312 | tf_op jit(solution)/shard_map/ppermute | solution.py:108
  16.5 5.9 %collective-permute-start.10 = (bf16[272,128]{1,0:T(8,128)(2,1)S(1)}, bf16[272,128]{1,0:T(8,128)(2,1)S(1)}, u32[]{:S(2)}, u32[]{:S(2)}) collective-permute-start(bf16[272,128]{1,0:T(8,128)(2,1)S(1)} %shard_map.74.refs_0_), channel_id=1, source_target_pairs={{0,16},{4,20},{8,24},{12,28},{16,0},{20,4},{24,8},{28,12},{1,17},{... | collective-permute-start | bytes 208904 | tf_op jit(solution)/shard_map/ppermute | solution.py:108
  20.5 5.4 %collective-permute-start.7 = (bf16[272,128]{1,0:T(8,128)(2,1)S(1)}, bf16[272,128]{1,0:T(8,128)(2,1)S(1)}, u32[]{:S(2)}, u32[]{:S(2)}) collective-permute-start(bf16[272,128]{1,0:T(8,128)(2,1)S(1)} %shard_map.72.refs_0_.refs_4_), channel_id=1, source_target_pairs={{0,3},{1,2},{2,1},{3,0},{4,7},{5,6},{6,5},{7,4},{8,11},{9,10},{10,... | collective-permute-start | bytes 208904 | tf_op jit(solution)/shard_map/ppermute | solution.py:108
  20.6 6.0 %collective-permute-start.8 = (bf16[272,128]{1,0:T(8,128)(2,1)S(1)}, bf16[272,128]{1,0:T(8,128)(2,1)S(1)}, u32[]{:S(2)}, u32[]{:S(2)}) collective-permute-start(bf16[272,128]{1,0:T(8,128)(2,1)S(1)} %shard_map.72.refs_0_.refs_4_), channel_id=1, source_target_pairs={{0,2},{1,3},{2,0},{3,1},{4,6},{5,7},{6,4},{7,5},{8,10},{9,11},{10,... | collective-permute-start | bytes 208904 | tf_op jit(solution)/shard_map/ppermute | solution.py:108
  22.1 4.4 %collective-permute-start.9 = (bf16[272,128]{1,0:T(8,128)(2,1)S(1)}, bf16[272,128]{1,0:T(8,128)(2,1)S(1)}, u32[]{:S(2)}, u32[]{:S(2)}) collective-permute-start(bf16[272,128]{1,0:T(8,128)(2,1)S(1)} %shard_map.72.refs_0_.refs_4_), channel_id=1, source_target_pairs={{0,1},{1,0},{2,3},{3,2},{4,5},{5,4},{6,7},{7,6},{8,9},{9,8},{10,11... | collective-permute-start | bytes 208904 | tf_op jit(solution)/shard_map/ppermute | solution.py:108
  22.4 5.3 %collective-permute-start.11 = (bf16[272,128]{1,0:T(8,128)(2,1)S(1)}, bf16[272,128]{1,0:T(8,128)(2,1)S(1)}, u32[]{:S(2)}, u32[]{:S(2)}) collective-permute-start(bf16[272,128]{1,0:T(8,128)(2,1)S(1)} %shard_map.75.refs_0_), channel_id=1, source_target_pairs={{0,12},{4,8},{8,4},{12,0},{16,28},{20,24},{24,20},{28,16},{1,13},{... | collective-permute-start | bytes 208904 | tf_op jit(solution)/shard_map/ppermute | solution.py:108
  24.8 4.8 %collective-permute-start.12 = (bf16[272,128]{1,0:T(8,128)(2,1)S(1)}, bf16[272,128]{1,0:T(8,128)(2,1)S(1)}, u32[]{:S(2)}, u32[]{:S(2)}) collective-permute-start(bf16[272,128]{1,0:T(8,128)(2,1)S(1)} %shard_map.75.refs_0_), channel_id=1, source_target_pairs={{0,8},{4,12},{8,0},{12,4},{16,24},{20,28},{24,16},{28,20},{1,9},{5... | collective-permute-start | bytes 208904 | tf_op jit(solution)/shard_map/ppermute | solution.py:108
  25.9 4.3 %collective-permute-start.13 = (bf16[272,128]{1,0:T(8,128)(2,1)S(1)}, bf16[272,128]{1,0:T(8,128)(2,1)S(1)}, u32[]{:S(2)}, u32[]{:S(2)}) collective-permute-start(bf16[272,128]{1,0:T(8,128)(2,1)S(1)} %shard_map.75.refs_0_), channel_id=1, source_target_pairs={{0,4},{4,0},{8,12},{12,8},{16,20},{20,16},{24,28},{28,24},{1,5},{5... | collective-permute-start | bytes 208904 | tf_op jit(solution)/shard_map/ppermute | solution.py:108
  30.3 4.4 %collective-permute-start.14 = (bf16[128,128]{1,0:T(8,128)(2,1)S(1)}, bf16[128,128]{1,0:T(8,128)(2,1)S(1)}, u32[]{:S(2)}, u32[]{:S(2)}) collective-permute-start(bf16[128,128]{1,0:T(8,128)(2,1)S(1)} %get-tuple-element.43.refs_0_), channel_id=1, source_target_pairs={{0,3},{1,2},{2,1},{3,0},{4,7},{5,6},{6,5},{7,4},{8,11},{9,10},{10,... | collective-permute-start | bytes 98312 | tf_op jit(solution)/shard_map/ppermute | solution.py:108
  30.3 4.3 %collective-permute-start.15 = (bf16[128,128]{1,0:T(8,128)(2,1)S(1)}, bf16[128,128]{1,0:T(8,128)(2,1)S(1)}, u32[]{:S(2)}, u32[]{:S(2)}) collective-permute-start(bf16[128,128]{1,0:T(8,128)(2,1)S(1)} %get-tuple-element.43.refs_0_), channel_id=1, source_target_pairs={{0,2},{1,3},{2,0},{3,1},{4,6},{5,7},{6,4},{7,5},{8,10},{9,11},{10,... | collective-permute-start | bytes 98312 | tf_op jit(solution)/shard_map/ppermute | solution.py:108
  34.8 4.7 %collective-permute-start.20 = (bf16[128,128]{1,0:T(8,128)(2,1)S(1)}, bf16[128,128]{1,0:T(8,128)(2,1)S(1)}, u32[]{:S(2)}, u32[]{:S(2)}) collective-permute-start(bf16[128,128]{1,0:T(8,128)(2,1)S(1)} %get-tuple-element.55.refs_0_), channel_id=1, source_target_pairs={{0,3},{1,2},{2,1},{3,0},{4,7},{5,6},{6,5},{7,4},{8,11},{9,10},{10,... | collective-permute-start | bytes 98312 | tf_op jit(solution)/shard_map/ppermute | solution.py:108
  35.8 3.9 %collective-permute-start.21 = (bf16[128,128]{1,0:T(8,128)(2,1)S(1)}, bf16[128,128]{1,0:T(8,128)(2,1)S(1)}, u32[]{:S(2)}, u32[]{:S(2)}) collective-permute-start(bf16[128,128]{1,0:T(8,128)(2,1)S(1)} %get-tuple-element.55.refs_0_), channel_id=1, source_target_pairs={{0,2},{1,3},{2,0},{3,1},{4,6},{5,7},{6,4},{7,5},{8,10},{9,11},{10,... | collective-permute-start | bytes 98312 | tf_op jit(solution)/shard_map/ppermute | solution.py:108
  39.8 6.4 %collective-permute-start.23 = (bf16[176,128]{1,0:T(8,128)(2,1)S(1)}, bf16[176,128]{1,0:T(8,128)(2,1)S(1)}, u32[]{:S(2)}, u32[]{:S(2)}) collective-permute-start(bf16[176,128]{1,0:T(8,128)(2,1)S(1)} %get-tuple-element.58), channel_id=1, source_target_pairs={{0,12},{4,8},{8,4},{12,0},{16,28},{20,24},{24,20},{28,16},{1,13},{... | collective-permute-start | bytes 135176 | tf_op jit(solution)/shard_map/ppermute | solution.py:108
  41.4 5.4 %collective-permute-start.24 = (bf16[176,128]{1,0:T(8,128)(2,1)S(1)}, bf16[176,128]{1,0:T(8,128)(2,1)S(1)}, u32[]{:S(2)}, u32[]{:S(2)}) collective-permute-start(bf16[176,128]{1,0:T(8,128)(2,1)S(1)} %get-tuple-element.59), channel_id=1, source_target_pairs={{0,8},{4,12},{8,0},{12,4},{16,24},{20,28},{24,16},{28,20},{1,9},{5... | collective-permute-start | bytes 135176 | tf_op jit(solution)/shard_map/ppermute | solution.py:108
  41.9 4.9 %collective-permute-start.25 = (bf16[176,128]{1,0:T(8,128)(2,1)S(1)}, bf16[176,128]{1,0:T(8,128)(2,1)S(1)}, u32[]{:S(2)}, u32[]{:S(2)}) collective-permute-start(bf16[176,128]{1,0:T(8,128)(2,1)S(1)} %get-tuple-element.60), channel_id=1, source_target_pairs={{0,4},{4,0},{8,12},{12,8},{16,20},{20,16},{24,28},{28,24},{1,5},{5... | collective-permute-start | bytes 135176 | tf_op jit(solution)/shard_map/ppermute | solution.py:108
  44.9 3.6 %collective-permute-start.17 = (f32[80,128]{1,0:T(8,128)S(1)}, f32[80,128]{1,0:T(8,128)S(1)}, u32[]{:S(2)}, u32[]{:S(2)}) collective-permute-start(f32[80,128]{1,0:T(8,128)S(1)} %get-tuple-element.52), channel_id=1, source_target_pairs={{0,3},{1,2},{2,1},{3,0},{4,7},{5,6},{6,5},{7,4},{8,11},{9,10},{10,... | collective-permute-start | bytes 122888 | tf_op jit(solution)/shard_map/ppermute | solution.py:108
  45.1 4.4 %collective-permute-start.18 = (f32[80,128]{1,0:T(8,128)S(1)}, f32[80,128]{1,0:T(8,128)S(1)}, u32[]{:S(2)}, u32[]{:S(2)}) collective-permute-start(f32[80,128]{1,0:T(8,128)S(1)} %get-tuple-element.53), channel_id=1, source_target_pairs={{0,2},{1,3},{2,0},{3,1},{4,6},{5,7},{6,4},{7,5},{8,10},{9,11},{10,... | collective-permute-start | bytes 122888 | tf_op jit(solution)/shard_map/ppermute | solution.py:108
  46.8 5.1 %collective-permute-start.26 = (bf16[160,128]{1,0:T(8,128)(2,1)S(1)}, bf16[160,128]{1,0:T(8,128)(2,1)S(1)}, u32[]{:S(2)}, u32[]{:S(2)}) collective-permute-start(bf16[160,128]{1,0:T(8,128)(2,1)S(1)} %get-tuple-element.64), channel_id=1, source_target_pairs={{0,16},{4,20},{8,24},{12,28},{16,0},{20,4},{24,8},{28,12},{1,17},{... | collective-permute-start | bytes 122888 | tf_op jit(solution)/shard_map/ppermute | solution.py:108
  (4 other events, 14.9 us)
